TPU v7x, 256 devices: a whole 4x4x8 slice. The times are simulated.
256 devices in a mesh: ctx: 64 (over z, y, core), dp: 4 (over x).
Axes of the slice: x: 4, y: 4, z: 8, core: 2. Of those that a mesh axis runs over, the one named last changes fastest.
Arguments:
- queries: bfloat16 [32768, 1024], P(('dp', 'ctx')), parts along dimension 0, may hold values from -220 to 220
- keys: bfloat16 [32768, 1024], P(('dp', 'ctx')), parts along dimension 0, may hold values from -8 to 8
- values: bfloat16 [32768, 1024], P(('dp', 'ctx')), parts along dimension 0, may hold values from -6 to 6
- cotangent: bfloat16 [32768, 1024], P(('dp', 'ctx')), parts along dimension 0, may hold values from -6 to 6
Outputs:
- output: bfloat16 [32768, 1024], P(('dp', 'ctx')), parts along dimension 0
- grad_queries: bfloat16 [32768, 1024], P(('dp', 'ctx')), parts along dimension 0
- grad_keys: bfloat16 [32768, 1024], P(('dp', 'ctx')), parts along dimension 0
- grad_values: bfloat16 [32768, 1024], P(('dp', 'ctx')), parts along dimension 0
There are 4 independent parts, one for each index of `dp`. A program takes and returns all parts, laid end to end along the dimension named above; each array names one. Nothing has to cross between parts.
All inputs are finite; a program needn't handle non-finite values.
Results may differ from a plain program's by a relative error of at most 0.012.
Values may be sent and summed in bfloat16 or wider, within the bound.
No kernel may reach another device: no remote copies, remote signals or barrier semaphores. Data moves between devices by JAX's collectives and lax.ppermute only.
A program may use at most 128 MiB of HBM per device.

v0:
```python
import jax
import jax.numpy as jnp
from jax import lax
from jax.experimental import pallas as pl
from jax.experimental.pallas import tpu as pltpu
from jax.sharding import PartitionSpec as P

H = 8
DH = 128
D = H * DH
ROWS = 128
Z = 8
HALF_ROOT = 0.7071067811865476
SCALE = DH ** (-0.5)
LOG2E = 1.4426950408889634
F32 = jnp.float32
BF16 = jnp.bfloat16
VMEM_LIMIT = 48 * 1024 * 1024
PARAMS = pltpu.CompilerParams(vmem_limit_bytes=VMEM_LIMIT)


def z_index():
    return lax.axis_index("ctx") // 8


def swap(block, mask):
    count = lax.axis_size("ctx")
    return lax.ppermute(block, "ctx", [(i, i ^ mask) for i in range(count)])


def z_exchange(block):
    groups = [[z * 8 + rest for z in range(Z)] for rest in range(8)]
    return lax.all_to_all(block, "ctx", 0, 0, tiled=True, axis_index_groups=groups)


def place_of(other):
    level = 4 if other == 1 else 5 if other < 4 else 6
    start = 0 if other == 1 else 4 * (other - 2) if other < 4 else 2 * (other - 4)
    return level, start


def coarsen_kernel(k_ref, v_ref, c1_ref, c2_ref, c3_ref, send_ref, tmp, pack):
    z = z_index()
    pack[...] = jnp.zeros(pack.shape, F32)
    for side, source in enumerate((k_ref, v_ref)):
        for number in range(H):
            columns = slice(number * DH, number * DH + DH)
            plane = tmp.at[side * H + number]
            rows = source[:, columns].astype(F32)
            for level in range(1, 7):
                count = ROWS >> level
                plane[: 2 * count, :] = rows
                total = plane[pl.ds(0, count, stride=2), :] + plane[pl.ds(1, count, stride=2), :]
                exact = (total * HALF_ROOT).astype(BF16)
                rows = exact.astype(F32)
                if level < 4:
                    ref = (c1_ref, c2_ref, c3_ref)[level - 1]
                    ref[side * count : side * count + count, columns] = exact
                for other in range(1, Z):
                    at, start = place_of(other)
                    if at == level:
                        start += 16 * other + 8 * side
                        pack[start : start + count, columns] = rows
    for other in range(Z):
        send_ref[z ^ other] = pack[16 * other : 16 * other + 16, :].astype(BF16)


def coarsen(keys, values):
    return pl.pallas_call(
        coarsen_kernel,
        out_shape=(
            jax.ShapeDtypeStruct((128, D), BF16),
            jax.ShapeDtypeStruct((64, D), BF16),
            jax.ShapeDtypeStruct((32, D), BF16),
            jax.ShapeDtypeStruct((Z, 16, D), BF16),
        ),
        scratch_shapes=[pltpu.VMEM((2 * H, ROWS, DH), F32), pltpu.VMEM((16 * Z, D), F32)],
        compiler_params=PARAMS,
        name="coarsen",
    )(keys, values)


def merge_kernel(got_ref, c2_ref, c3_ref, near_ref, far_ref):
    z = z_index()
    tile_a = got_ref[z ^ 1]
    tile_b = got_ref[z ^ 2] + got_ref[z ^ 3]
    tile_c = (got_ref[z ^ 4] + got_ref[z ^ 5]) + (got_ref[z ^ 6] + got_ref[z ^ 7])
    for ref in (near_ref, far_ref):
        ref[0:16, :] = tile_a
        ref[16:32, :] = tile_b
        ref[32:48, :] = tile_c
    near_ref[48:112, :] = c2_ref[...]
    far_ref[48:80, :] = c3_ref[...]


def merge(got, c2, c3):
    return pl.pallas_call(
        merge_kernel,
        out_shape=(
            jax.ShapeDtypeStruct((112, D), BF16),
            jax.ShapeDtypeStruct((80, D), BF16),
        ),
        compiler_params=PARAMS,
        name="merge",
    )(got, c2, c3)


def place(mine, other, c1_ref, key_all, value_all, key_tmp, value_tmp):
    key_all[128:192, :] = c1_ref[0:64, :]
    value_all[128:192, :] = c1_ref[64:128, :]
    for core, refs in enumerate((mine, other)):
        near, far2, far3, own = refs
        start = 192 + 32 * core
        key_all[start : start + 32, :] = near[48:80, :]
        value_all[start : start + 32, :] = near[80:112, :]
        for number, ref in enumerate((far2, far3)):
            start = 256 + 32 * core + 16 * number
            key_all[start : start + 16, :] = ref[48:64, :]
            value_all[start : start + 16, :] = ref[64:80, :]
        for number, ref in enumerate((own, near, far2, far3)):
            for tile in range(3):
                rows = ref[16 * tile : 16 * tile + 16, :].astype(F32)
                start = 96 * core + 24 * number + 8 * tile
                key_tmp[start : start + 8, :] = rows[:8]
                value_tmp[start : start + 8, :] = rows[8:]
    key_all[320:512, :] = key_tmp[...].astype(BF16)
    value_all[320:512, :] = value_tmp[...].astype(BF16)


def collect(key_grad, value_grad, core, out_ref):
    out = 0

    def tiles(number):
        for tile in range(3):
            start = 320 + 96 * core + 24 * number + 8 * tile
            yield key_grad[start : start + 8, :], value_grad[start : start + 8, :]

    def level2():
        start = 192 + 32 * core
        yield key_grad[start : start + 32, :], value_grad[start : start + 32, :]

    def level3(number):
        start = 256 + 32 * core + 16 * number
        yield key_grad[start : start + 16, :], value_grad[start : start + 16, :]

    order = (tiles(1), level2(), tiles(2), level3(0), tiles(3), level3(1), tiles(0))
    for pieces in order:
        for key_piece, value_piece in pieces:
            count = key_piece.shape[0]
            both = jnp.concatenate([key_piece, value_piece], axis=0)
            out_ref[out : out + 2 * count, :] = both.astype(out_ref.dtype)
            out += 2 * count


def attend_kernel(
    q_ref, k_ref, v_ref, g_ref, c1_ref,
    near_ref, far2_ref, far3_ref, own_ref,
    near_o_ref, far2_o_ref, far3_o_ref, own_o_ref,
    out_ref, grad_q_ref, local_k_ref, local_v_ref, one_ref, mine_ref, other_ref,
    key_all, value_all, key_grad, value_grad, key_tmp, value_tmp,
):
    key_all[0:128, :] = k_ref[...]
    value_all[0:128, :] = v_ref[...]
    place(
        (near_ref, far2_ref, far3_ref, own_ref),
        (near_o_ref, far2_o_ref, far3_o_ref, own_o_ref),
        c1_ref, key_all, value_all, key_tmp, value_tmp,
    )

    def dot(a, b, a_dim, b_dim):
        return lax.dot_general(
            a, b, (((a_dim,), (b_dim,)), ((), ())), preferred_element_type=F32
        )

    def head(number, carry):
        columns = pl.ds(pl.multiple_of(number * DH, DH), DH)
        q = q_ref[:, columns]
        g = g_ref[:, columns]
        k = key_all[:, columns]
        v = value_all[:, columns]
        scores = dot(k, q, 1, 1)
        top = jnp.max(scores, axis=0, keepdims=True)
        exponent = jnp.exp2((scores - top) * (SCALE * LOG2E))
        prob = exponent * (1.0 / jnp.sum(exponent, axis=0, keepdims=True))
        weights = prob.astype(BF16)
        dprob = dot(v, g, 1, 1)
        delta = jnp.sum(prob * dprob, axis=0, keepdims=True)
        dscore = (prob * (dprob - delta) * SCALE).astype(BF16)
        out_ref[:, columns] = dot(weights, v, 0, 0).astype(BF16)
        grad_q_ref[:, columns] = dot(dscore, k, 0, 0).astype(BF16)
        key_grad[:, columns] = dot(dscore, q, 1, 0)
        value_grad[:, columns] = dot(weights, g, 1, 0)
        return carry

    lax.fori_loop(0, H, head, 0)
    local_k_ref[...] = key_grad[0:128, :]
    local_v_ref[...] = value_grad[0:128, :]
    one_ref[0:64, :] = key_grad[128:192, :].astype(BF16)
    one_ref[64:128, :] = value_grad[128:192, :].astype(BF16)
    collect(key_grad, value_grad, 0, mine_ref)
    collect(key_grad, value_grad, 1, other_ref)


def attend(*operands):
    shape = jax.ShapeDtypeStruct
    return pl.pallas_call(
        attend_kernel,
        out_shape=(
            shape((ROWS, D), BF16),
            shape((ROWS, D), BF16),
            shape((ROWS, D), F32),
            shape((ROWS, D), F32),
            shape((128, D), BF16),
            shape((320, D), F32),
            shape((320, D), BF16),
        ),
        scratch_shapes=[
            pltpu.VMEM((512, D), BF16),
            pltpu.VMEM((512, D), BF16),
            pltpu.VMEM((512, D), F32),
            pltpu.VMEM((512, D), F32),
            pltpu.VMEM((192, D), F32),
            pltpu.VMEM((192, D), F32),
        ],
        compiler_params=PARAMS,
        name="attend",
    )(*operands)


def chip_kernel(mine_ref, got_ref, near_ref, far2_ref, far3_ref, own_ref):
    start = 0
    for ref in (near_ref, far2_ref, far3_ref, own_ref):
        count = ref.shape[0]
        total = mine_ref[start : start + count, :] + got_ref[start : start + count, :].astype(F32)
        ref[...] = total.astype(ref.dtype)
        start += count


def chip_sum(mine, got):
    shape = jax.ShapeDtypeStruct
    return pl.pallas_call(
        chip_kernel,
        out_shape=(
            shape((112, D), BF16),
            shape((80, D), BF16),
            shape((80, D), BF16),
            shape((48, D), F32),
        ),
        compiler_params=PARAMS,
        name="chip_sum",
    )(mine, got)


def plane_kernel(own_ref, near_ref, far2_ref, far3_ref, send_ref):
    z = z_index()
    send_ref[z] = jnp.zeros((16, D), BF16)
    for tile in range(3):
        rows = slice(16 * tile, 16 * tile + 16)
        total = (own_ref[rows, :] + near_ref[rows, :].astype(F32)) + (
            far2_ref[rows, :].astype(F32) + far3_ref[rows, :].astype(F32)
        )
        total = total.astype(BF16)
        for other in ((1,), (2, 3), (4, 5, 6, 7))[tile]:
            send_ref[z ^ other] = total


def plane_sum(own, near, far2, far3):
    return pl.pallas_call(
        plane_kernel,
        out_shape=jax.ShapeDtypeStruct((Z, 16, D), BF16),
        compiler_params=PARAMS,
        name="plane_sum",
    )(own, near, far2, far3)


def finish_kernel(
    local_k_ref, local_v_ref, one_ref, near_ref, far2_ref, far3_ref, got_ref,
    grad_k_ref, grad_v_ref, tmp, pick,
):
    z = z_index()
    for other in range(1, Z):
        pick[16 * other : 16 * other + 16, :] = got_ref[z ^ other].astype(F32)
    for side, (local_ref, out_ref) in enumerate(
        ((local_k_ref, grad_k_ref), (local_v_ref, grad_v_ref))
    ):
        for number in range(H):
            columns = slice(number * DH, number * DH + DH)
            plane = tmp.at[side * H + number]

            def part(other, side=side, columns=columns):
                level, start = place_of(other)
                start += 16 * other + 8 * side
                return pick[start : start + (ROWS >> level), columns]

            def rows(ref, start, count, side=side, columns=columns):
                start += side * count
                return ref[start : start + count, columns].astype(F32)

            parts = {
                6: (part(4) + part(5)) + (part(6) + part(7)),
                5: part(2) + part(3),
                4: part(1),
                3: rows(far2_ref, 48, 16) + rows(far3_ref, 48, 16),
                2: rows(near_ref, 48, 32),
                1: rows(one_ref, 0, 64),
                0: local_ref[:, columns],
            }
            total = parts[6]
            for level in range(5, -1, -1):
                count = ROWS >> level
                half = total * HALF_ROOT
                plane[pl.ds(0, count // 2, stride=2), :] = half
                plane[pl.ds(1, count // 2, stride=2), :] = half
                total = plane[:count, :] + parts[level]
            out_ref[:, columns] = total.astype(BF16)


def finish(*operands):
    shape = jax.ShapeDtypeStruct
    return pl.pallas_call(
        finish_kernel,
        out_shape=(shape((ROWS, D), BF16), shape((ROWS, D), BF16)),
        scratch_shapes=[pltpu.VMEM((2 * H, ROWS, DH), F32), pltpu.VMEM((16 * Z, D), F32)],
        compiler_params=PARAMS,
        name="finish",
    )(*operands)


def per_device(queries, keys, values, cotangent):
    c1, c2, c3, send = coarsen(keys, values)
    c1 = swap(c1, 1)
    near, far = merge(z_exchange(send), c2, c3)
    own = near[:48]
    own_o = swap(own, 1)
    far2 = swap(far, 4)
    near = swap(near, 2)
    far3 = swap(far, 6)
    near_o = swap(near, 1)
    far2_o = swap(far2, 1)
    far3_o = swap(far3, 1)
    output, grad_queries, local_k, local_v, one, mine, other = attend(
        queries, keys, values, cotangent, c1,
        near, far2, far3, own, near_o, far2_o, far3_o, own_o,
    )
    got = swap(other, 1)
    one = swap(one, 1)
    near, far2, far3, own = chip_sum(mine, got)
    far2 = swap(far2, 4)
    near = swap(near, 2)
    far3 = swap(far3, 6)
    got = z_exchange(plane_sum(own, near, far2, far3))
    grad_keys, grad_values = finish(local_k, local_v, one, near, far2, far3, got)
    return output, grad_queries, grad_keys, grad_values


def solution(mesh):
    spec = P(("dp", "ctx"), None)
    return jax.shard_map(
        per_device,
        mesh=mesh,
        in_specs=(spec,) * 4,
        out_specs=(spec,) * 4,
        check_vma=False,
    )
```

profile of v0, /device:TPU:6, one launch (start us, length us, event | category | flops | bytes accessed | tf_op | source)
XLA Modules:
  0.0 75.1 jit_solution(16956066730710510020)
XLA Ops:
  0.6 0.9 %copy-done = bf16[128,1024]{1,0:T(8,128)(2,1)S(1)} copy-done((bf16[128,1024]{1,0:T(8,128)(2,1)S(1)}, bf16[128,1024]{1,0:T(8,128)(2,1)}, u32[]{:S(2)}) %copy-start) | copy-done | bytes 262168
  1.6 0.9 %copy-done.2 = bf16[128,1024]{1,0:T(8,128)(2,1)S(1)} copy-done((bf16[128,1024]{1,0:T(8,128)(2,1)S(1)}, bf16[128,1024]{1,0:T(8,128)(2,1)}, u32[]{:S(2)}) %copy-start.2) | copy-done | bytes 262168
  2.5 0.4 coarsen.1
  3.0 20.1 %all_to_all.10.got_ref = bf16[8,16,1024]{2,1,0:T(8,128)(2,1)S(1)} all-to-all(bf16[8,16,1024]{2,1,0:T(8,128)(2,1)S(1)} %get-tuple-element.24), channel_id=1, replica_groups={{0,32,64,96,128,160,192,224},{4,36,68,100,132,164,196,228},{8,40,72,104..., dimensions={0} | all-to-all | bytes 524288 | tf_op jit(solution)/shard_map/all_to_all | solution.py:33
  23.1 1.7 %collective-permute-start.1 = (bf16[112,1024]{1,0:T(8,128)(2,1)S(1)}, bf16[112,1024]{1,0:T(8,128)(2,1)S(1)}, u32[]{:S(2)}, u32[]{:S(2)}) collective-permute-start(bf16[112,1024]{1,0:T(8,128)(2,1)S(1)} %get-tuple-element.27), channel_id=1, source_target_pairs={{0,8},{4,12},{8,0},{12,4},{16,24},{20,28},{24,16},{28,20},{32,40},... | collective-permute-start | bytes 688136 | tf_op jit(solution)/shard_map/ppermute | solution.py:28
  24.8 2.2 %collective-permute-start.3 = (bf16[80,1024]{1,0:T(8,128)(2,1)S(1)}, bf16[80,1024]{1,0:T(8,128)(2,1)S(1)}, u32[]{:S(2)}, u32[]{:S(2)}) collective-permute-start(bf16[80,1024]{1,0:T(8,128)(2,1)S(1)} %get-tuple-element.28), channel_id=1, source_target_pairs={{0,24},{4,28},{8,16},{12,20},{16,8},{20,12},{24,0},{28,4},{32,56},... | collective-permute-start | bytes 491528 | tf_op jit(solution)/shard_map/ppermute | solution.py:28
  27.0 0.7 collective-permute-start.2
  27.7 3.3 %collective-permute-done.1.near_ref = bf16[112,1024]{1,0:T(8,128)(2,1)S(1)} collective-permute-done((bf16[112,1024]{1,0:T(8,128)(2,1)S(1)}, bf16[112,1024]{1,0:T(8,128)(2,1)S(1)}, u32[]{:S(2)}, u32[]{:S(2)}) %collective-permute-start.1) | collective-permute-done | bytes 229408 | tf_op jit(solution)/shard_map/ppermute | solution.py:28
  31.0 1.4 %collective-permute-done.3.far3_ref = bf16[80,1024]{1,0:T(8,128)(2,1)S(1)} collective-permute-done((bf16[80,1024]{1,0:T(8,128)(2,1)S(1)}, bf16[80,1024]{1,0:T(8,128)(2,1)S(1)}, u32[]{:S(2)}, u32[]{:S(2)}) %collective-permute-start.3) | collective-permute-done | bytes 163872 | tf_op jit(solution)/shard_map/ppermute | solution.py:28
  32.4 2.3 %collective-permute-done.2.far2_ref = bf16[80,1024]{1,0:T(8,128)(2,1)S(1)} collective-permute-done((bf16[80,1024]{1,0:T(8,128)(2,1)S(1)}, bf16[80,1024]{1,0:T(8,128)(2,1)S(1)}, u32[]{:S(2)}, u32[]{:S(2)}) %collective-permute-start.2) | collective-permute-done | bytes 163872 | tf_op jit(solution)/shard_map/ppermute | solution.py:28
  34.8 0.6 collective-permute-start.7
  35.3 0.9 %collective-permute-done.7.own_o_ref = bf16[48,1024]{1,0:T(8,128)(2,1)S(1)} collective-permute-done((bf16[48,1024]{1,0:T(8,128)(2,1)S(1)}, bf16[48,1024]{1,0:T(8,128)(2,1)S(1)}, u32[]{:S(2)}, u32[]{:S(2)}) %collective-permute-start.7) | collective-permute-done | bytes 98336 | tf_op jit(solution)/shard_map/ppermute | solution.py:28
  36.3 7.2 %attend.1 = (bf16[128,1024]{1,0:T(8,128)(2,1)}, bf16[128,1024]{1,0:T(8,128)(2,1)}, f32[128,1024]{1,0:T(8,128)S(1)}, f32[128,1024]{1,0:T(8,128)S(1)}, bf16[128,10...) custom-call(bf16[128,1024]{1,0:T(8,128)(2,1)S(1)} %copy-done.4, ...), custom_call_target="tpu_custom_call" | custom-call | tf_op jit(solution)/shard_map/attend/pallas_call | solution.py:206
  43.9 1.7 %collective-permute-done.9.got_ref = bf16[320,1024]{1,0:T(8,128)(2,1)S(1)} collective-permute-done((bf16[320,1024]{1,0:T(8,128)(2,1)S(1)}, bf16[320,1024]{1,0:T(8,128)(2,1)S(1)}, u32[]{:S(2)}, u32[]{:S(2)}) %collective-permute-start.9) | collective-permute-done | bytes 655392 | tf_op jit(solution)/shard_map/ppermute | solution.py:28
  45.8 0.6 collective-permute-start.10
  46.4 2.6 %collective-permute-start.11 = (bf16[80,1024]{1,0:T(8,128)(2,1)S(1)}, bf16[80,1024]{1,0:T(8,128)(2,1)S(1)}, u32[]{:S(2)}, u32[]{:S(2)}) collective-permute-start(bf16[80,1024]{1,0:T(8,128)(2,1)S(1)} %get-tuple-element.37), channel_id=1, source_target_pairs={{0,16},{4,20},{8,24},{12,28},{16,0},{20,4},{24,8},{28,12},{32,48},... | collective-permute-start | bytes 491528 | tf_op jit(solution)/shard_map/ppermute | solution.py:28
  48.9 1.7 %collective-permute-start.12 = (bf16[80,1024]{1,0:T(8,128)(2,1)S(1)}, bf16[80,1024]{1,0:T(8,128)(2,1)S(1)}, u32[]{:S(2)}, u32[]{:S(2)}) collective-permute-start(bf16[80,1024]{1,0:T(8,128)(2,1)S(1)} %get-tuple-element.38), channel_id=1, source_target_pairs={{0,24},{4,28},{8,16},{12,20},{16,8},{20,12},{24,0},{28,4},{32,56},... | collective-permute-start | bytes 491528 | tf_op jit(solution)/shard_map/ppermute | solution.py:28
  50.6 7.6 %collective-permute-done.11.far2_ref = bf16[80,1024]{1,0:T(8,128)(2,1)S(1)} collective-permute-done((bf16[80,1024]{1,0:T(8,128)(2,1)S(1)}, bf16[80,1024]{1,0:T(8,128)(2,1)S(1)}, u32[]{:S(2)}, u32[]{:S(2)}) %collective-permute-start.11) | collective-permute-done | bytes 163872 | tf_op jit(solution)/shard_map/ppermute | solution.py:28
  58.2 1.2 %collective-permute-done.12.far3_ref = bf16[80,1024]{1,0:T(8,128)(2,1)S(1)} collective-permute-done((bf16[80,1024]{1,0:T(8,128)(2,1)S(1)}, bf16[80,1024]{1,0:T(8,128)(2,1)S(1)}, u32[]{:S(2)}, u32[]{:S(2)}) %collective-permute-start.12) | collective-permute-done | bytes 163872 | tf_op jit(solution)/shard_map/ppermute | solution.py:28
  59.3 0.8 %plane_sum.1 = bf16[8,16,1024]{2,1,0:T(8,128)(2,1)} custom-call(f32[48,1024]{1,0:T(8,128)S(1)} %get-tuple-element.39.own_ref, bf16[112,1024]{1,0:T(8,128)(2,1)S(1)} %collective-permute-done.10.near_ref, bf16[80,1024]{1,0:T(8,128)(2,1)S(1)} %collective-permute-done.11.far2_ref, bf16[80,1024]{1,0:T(8,128)(2,1)S(1)} %collective-permute-done.12.far3_ref), custom_call_target="tpu_custom_call" | custom-call | tf_op jit(solution)/shard_map/plane_sum/pallas_call | solution.py:268
  60.1 3.4 %all-to-all-start.1 = ((bf16[8,16,1024]{2,1,0:T(8,128)(2,1)}), bf16[8,16,1024]{2,1,0:T(8,128)(2,1)S(1)}, u32[]{:S(2)}, u32[]{:S(2)}) async-start(bf16[8,16,1024]{2,1,0:T(8,128)(2,1)} %plane_sum.1), calls=%async_computation.1 | async-start | bytes 524288 | tf_op jit(solution)/shard_map/all_to_all | solution.py:33
  63.6 1.5 %collective-permute-done.8.one_ref = bf16[128,1024]{1,0:T(8,128)(2,1)S(1)} collective-permute-done((bf16[128,1024]{1,0:T(8,128)(2,1)S(1)}, bf16[128,1024]{1,0:T(8,128)(2,1)S(1)}, u32[]{:S(2)}, u32[]{:S(2)}) %collective-permute-start.8) | collective-permute-done | bytes 262176 | tf_op jit(solution)/shard_map/ppermute | solution.py:28
  65.1 8.8 %all-to-all-done.1.got_ref = bf16[8,16,1024]{2,1,0:T(8,128)(2,1)S(1)} async-done(((bf16[8,16,1024]{2,1,0:T(8,128)(2,1)}), bf16[8,16,1024]{2,1,0:T(8,128)(2,1)S(1)}, u32[]{:S(2)}, u32[]{:S(2)}) %all-to-all-start.1) | async-done | bytes 262176 | tf_op jit(solution)/shard_map/all_to_all | solution.py:33
  73.9 1.2 %finish.1 = (bf16[128,1024]{1,0:T(8,128)(2,1)}, bf16[128,1024]{1,0:T(8,128)(2,1)}) custom-call(f32[128,1024]{1,0:T(8,128)S(1)} %get-tuple-element.31.local_k_ref, f32[128,1024]{1,0:T(8,128)S(1)} %get-tuple-element.32.local_v_ref, bf16[128,1024]{1,0:T(8,128)(2,1)S(1)} %collective-permute-done.8.one_ref, ...), custom_call_target="tpu_custom_call" | custom-call | tf_op jit(solution)/shard_map/finish/pallas_call | solution.py:320
  (24 shorter events, 0.6 us)
Async XLA Ops:
  0.6 1.0 %copy-start = (bf16[128,1024]{1,0:T(8,128)(2,1)S(1)}, bf16[128,1024]{1,0:T(8,128)(2,1)}, u32[]{:S(2)}) copy-start(bf16[128,1024]{1,0:T(8,128)(2,1)} %k_ref.3) | copy-start | bytes 786436
  1.6 0.9 %copy-start.2 = (bf16[128,1024]{1,0:T(8,128)(2,1)S(1)}, bf16[128,1024]{1,0:T(8,128)(2,1)}, u32[]{:S(2)}) copy-start(bf16[128,1024]{1,0:T(8,128)(2,1)} %v_ref.3) | copy-start | bytes 786436
  2.5 33.8 %copy-start.1 = (bf16[128,1024]{1,0:T(8,128)(2,1)S(1)}, bf16[128,1024]{1,0:T(8,128)(2,1)}, u32[]{:S(2)}) copy-start(bf16[128,1024]{1,0:T(8,128)(2,1)} %k_ref.3) | copy-start | bytes 786436
  2.5 33.8 %copy-start.3 = (bf16[128,1024]{1,0:T(8,128)(2,1)S(1)}, bf16[128,1024]{1,0:T(8,128)(2,1)}, u32[]{:S(2)}) copy-start(bf16[128,1024]{1,0:T(8,128)(2,1)} %v_ref.3) | copy-start | bytes 786436
  2.5 33.8 %copy-start.4 = (bf16[128,1024]{1,0:T(8,128)(2,1)S(1)}, bf16[128,1024]{1,0:T(8,128)(2,1)}, u32[]{:S(2)}) copy-start(bf16[128,1024]{1,0:T(8,128)(2,1)} %q_ref.1) | copy-start | bytes 786436
  2.5 33.8 %copy-start.5 = (bf16[128,1024]{1,0:T(8,128)(2,1)S(1)}, bf16[128,1024]{1,0:T(8,128)(2,1)}, u32[]{:S(2)}) copy-start(bf16[128,1024]{1,0:T(8,128)(2,1)} %g_ref.1) | copy-start | bytes 786436
  23.1 7.9 %collective-permute-start.1 = (bf16[112,1024]{1,0:T(8,128)(2,1)S(1)}, bf16[112,1024]{1,0:T(8,128)(2,1)S(1)}, u32[]{:S(2)}, u32[]{:S(2)}) collective-permute-start(bf16[112,1024]{1,0:T(8,128)(2,1)S(1)} %get-tuple-element.27), channel_id=1, source_target_pairs={{0,8},{4,12},{8,0},{12,4},{16,24},{20,28},{24,16},{28,20},{32,40},... | collective-permute-start | bytes 688136 | tf_op jit(solution)/shard_map/ppermute | solution.py:28
  24.8 7.6 %collective-permute-start.3 = (bf16[80,1024]{1,0:T(8,128)(2,1)S(1)}, bf16[80,1024]{1,0:T(8,128)(2,1)S(1)}, u32[]{:S(2)}, u32[]{:S(2)}) collective-permute-start(bf16[80,1024]{1,0:T(8,128)(2,1)S(1)} %get-tuple-element.28), channel_id=1, source_target_pairs={{0,24},{4,28},{8,16},{12,20},{16,8},{20,12},{24,0},{28,4},{32,56},... | collective-permute-start | bytes 491528 | tf_op jit(solution)/shard_map/ppermute | solution.py:28
  27.0 7.8 %collective-permute-start.2 = (bf16[80,1024]{1,0:T(8,128)(2,1)S(1)}, bf16[80,1024]{1,0:T(8,128)(2,1)S(1)}, u32[]{:S(2)}, u32[]{:S(2)}) collective-permute-start(bf16[80,1024]{1,0:T(8,128)(2,1)S(1)} %get-tuple-element.28), channel_id=1, source_target_pairs={{0,16},{4,20},{8,24},{12,28},{16,0},{20,4},{24,8},{28,12},{32,48},... | collective-permute-start | bytes 491528 | tf_op jit(solution)/shard_map/ppermute | solution.py:28
  27.7 7.6 %collective-permute-start = (bf16[128,1024]{1,0:T(8,128)(2,1)S(1)}, bf16[128,1024]{1,0:T(8,128)(2,1)S(1)}, u32[]{:S(2)}, u32[]{:S(2)}) collective-permute-start(bf16[128,1024]{1,0:T(8,128)(2,1)S(1)} %get-tuple-element.23), channel_id=1, source_target_pairs={{0,4},{4,0},{8,12},{12,8},{16,20},{20,16},{24,28},{28,24},{32,36},... | collective-permute-start | bytes 786440 | tf_op jit(solution)/shard_map/ppermute | solution.py:28
  31.0 5.3 %collective-permute-start.4 = (bf16[112,1024]{1,0:T(8,128)(2,1)S(1)}, bf16[112,1024]{1,0:T(8,128)(2,1)S(1)}, u32[]{:S(2)}, u32[]{:S(2)}) collective-permute-start(bf16[112,1024]{1,0:T(8,128)(2,1)S(1)} %collective-permute-done.1.near_ref), channel_id=1, source_target_pairs={{0,4},{4,0},{8,12},{12,8},{16,20},{20,16},{24,28},{28,24},{32,36},... | collective-permute-start | bytes 688136 | tf_op jit(solution)/shard_map/ppermute | solution.py:28
  32.4 3.9 %collective-permute-start.6 = (bf16[80,1024]{1,0:T(8,128)(2,1)S(1)}, bf16[80,1024]{1,0:T(8,128)(2,1)S(1)}, u32[]{:S(2)}, u32[]{:S(2)}) collective-permute-start(bf16[80,1024]{1,0:T(8,128)(2,1)S(1)} %collective-permute-done.3.far3_ref), channel_id=1, source_target_pairs={{0,4},{4,0},{8,12},{12,8},{16,20},{20,16},{24,28},{28,24},{32,36},... | collective-permute-start | bytes 491528 | tf_op jit(solution)/shard_map/ppermute | solution.py:28
  34.7 1.6 %collective-permute-start.5 = (bf16[80,1024]{1,0:T(8,128)(2,1)S(1)}, bf16[80,1024]{1,0:T(8,128)(2,1)S(1)}, u32[]{:S(2)}, u32[]{:S(2)}) collective-permute-start(bf16[80,1024]{1,0:T(8,128)(2,1)S(1)} %collective-permute-done.2.far2_ref), channel_id=1, source_target_pairs={{0,4},{4,0},{8,12},{12,8},{16,20},{20,16},{24,28},{28,24},{32,36},... | collective-permute-start | bytes 491528 | tf_op jit(solution)/shard_map/ppermute | solution.py:28
  34.8 1.5 %collective-permute-start.7 = (bf16[48,1024]{1,0:T(8,128)(2,1)S(1)}, bf16[48,1024]{1,0:T(8,128)(2,1)S(1)}, u32[]{:S(2)}, u32[]{:S(2)}) collective-permute-start(bf16[48,1024]{1,0:T(8,128)(2,1)S(1)} %slice.3.own_ref), channel_id=1, source_target_pairs={{0,4},{4,0},{8,12},{12,8},{16,20},{20,16},{24,28},{28,24},{32,36},... | collective-permute-start | bytes 294920 | tf_op jit(solution)/shard_map/ppermute | solution.py:28
  43.6 2.1 %collective-permute-start.9 = (bf16[320,1024]{1,0:T(8,128)(2,1)S(1)}, bf16[320,1024]{1,0:T(8,128)(2,1)S(1)}, u32[]{:S(2)}, u32[]{:S(2)}) collective-permute-start(bf16[320,1024]{1,0:T(8,128)(2,1)S(1)} %get-tuple-element.35), channel_id=1, source_target_pairs={{0,4},{4,0},{8,12},{12,8},{16,20},{20,16},{24,28},{28,24},{32,36},... | collective-permute-start | bytes 1966088 | tf_op jit(solution)/shard_map/ppermute | solution.py:28
  45.8 13.5 %collective-permute-start.10 = (bf16[112,1024]{1,0:T(8,128)(2,1)S(1)}, bf16[112,1024]{1,0:T(8,128)(2,1)S(1)}, u32[]{:S(2)}, u32[]{:S(2)}) collective-permute-start(bf16[112,1024]{1,0:T(8,128)(2,1)S(1)} %get-tuple-element.36), channel_id=1, source_target_pairs={{0,8},{4,12},{8,0},{12,4},{16,24},{20,28},{24,16},{28,20},{32,40},... | collective-permute-start | bytes 688136 | tf_op jit(solution)/shard_map/ppermute | solution.py:28
  46.4 11.8 %collective-permute-start.11 = (bf16[80,1024]{1,0:T(8,128)(2,1)S(1)}, bf16[80,1024]{1,0:T(8,128)(2,1)S(1)}, u32[]{:S(2)}, u32[]{:S(2)}) collective-permute-start(bf16[80,1024]{1,0:T(8,128)(2,1)S(1)} %get-tuple-element.37), channel_id=1, source_target_pairs={{0,16},{4,20},{8,24},{12,28},{16,0},{20,4},{24,8},{28,12},{32,48},... | collective-permute-start | bytes 491528 | tf_op jit(solution)/shard_map/ppermute | solution.py:28
  48.9 10.4 %collective-permute-start.12 = (bf16[80,1024]{1,0:T(8,128)(2,1)S(1)}, bf16[80,1024]{1,0:T(8,128)(2,1)S(1)}, u32[]{:S(2)}, u32[]{:S(2)}) collective-permute-start(bf16[80,1024]{1,0:T(8,128)(2,1)S(1)} %get-tuple-element.38), channel_id=1, source_target_pairs={{0,24},{4,28},{8,16},{12,20},{16,8},{20,12},{24,0},{28,4},{32,56},... | collective-permute-start | bytes 491528 | tf_op jit(solution)/shard_map/ppermute | solution.py:28
  60.1 13.8 %all-to-all-start.1 = ((bf16[8,16,1024]{2,1,0:T(8,128)(2,1)}), bf16[8,16,1024]{2,1,0:T(8,128)(2,1)S(1)}, u32[]{:S(2)}, u32[]{:S(2)}) async-start(bf16[8,16,1024]{2,1,0:T(8,128)(2,1)} %plane_sum.1), calls=%async_computation.1 | async-start | bytes 524288 | tf_op jit(solution)/shard_map/all_to_all | solution.py:33
  63.5 1.6 %collective-permute-start.8 = (bf16[128,1024]{1,0:T(8,128)(2,1)S(1)}, bf16[128,1024]{1,0:T(8,128)(2,1)S(1)}, u32[]{:S(2)}, u32[]{:S(2)}) collective-permute-start(bf16[128,1024]{1,0:T(8,128)(2,1)S(1)} %get-tuple-element.33), channel_id=1, source_target_pairs={{0,4},{4,0},{8,12},{12,8},{16,20},{20,16},{24,28},{28,24},{32,36},... | collective-permute-start | bytes 786440 | tf_op jit(solution)/shard_map/ppermute | solution.py:28
where the time goes:
time: 75.4 us; the launch traced here: 75.1 us
  waiting for transfers between devices  28.8 us (38%)
  blocking collectives  20.1 us (27%)
  starting transfers between devices  13.8 us (18%)
  Pallas kernels  9.7 us (13%)
  local copies, waits for them, and re-layouts  1.91 us (3%)
    all_to_all x1, blocking collectives, z_exchange(): lax.all_to_all(block, 'ctx', 0, 0, tiled=True, axis_index_groups=groups)  20.1 us
    ppermute x13, waiting for transfers between devices, swap(): return lax.ppermute(block, 'ctx', [(i, i ^ mask) for i in range(count)])  20 us
    ppermute x13, starting transfers between devices, swap(): return lax.ppermute(block, 'ctx', [(i, i ^ mask) for i in range(count)])  10.4 us
    all_to_all x1, waiting for transfers between devices, z_exchange(): lax.all_to_all(block, 'ctx', 0, 0, tiled=True, axis_index_groups=groups)  8.78 us
    pallas_call x1, Pallas kernels, attend(): pl.pallas_call(attend_kernel, out_shape=(shape((ROWS, D), BF16), shape((R...  7.25 us
    all_to_all x1, starting transfers between devices, z_exchange(): lax.all_to_all(block, 'ctx', 0, 0, tiled=True, axis_index_groups=groups)  3.41 us
    unnamed x12, local copies, waits for them, and re-layouts  1.91 us
  transfers between devices with their start and end apart: 14, of which 9 were waited for; matrix products, arithmetic and copies ran while one was open for 0% of the time, Pallas kernels for 0%

commit v1 on v0

v1 whole, which is shorter than its diff:
```python
import jax
import jax.numpy as jnp
from jax import lax
from jax.experimental import pallas as pl
from jax.experimental.pallas import tpu as pltpu
from jax.sharding import PartitionSpec as P

H = 8
DH = 128
D = H * DH
ROWS = 128
HALF_ROOT = 0.7071067811865476
SCALE = DH ** (-0.5)
LOG2E = 1.4426950408889634
F32 = jnp.float32
BF16 = jnp.bfloat16
VMEM_LIMIT = 48 * 1024 * 1024
PARAMS = pltpu.CompilerParams(vmem_limit_bytes=VMEM_LIMIT)


def swap(block, mask):
    count = lax.axis_size("ctx")
    return lax.ppermute(block, "ctx", [(i, i ^ mask) for i in range(count)])


def coarsen_kernel(
    k_hbm, v_hbm, q_hbm, g_hbm,
    c1_ref, c2_ref, c3_ref, c4_ref, c5_ref, c6_ref, k_ref, v_ref, q_ref, g_ref,
    tmp, pack, sems,
):
    copies = [
        pltpu.make_async_copy(source, target, sems.at[number])
        for number, (source, target) in enumerate(
            ((k_hbm, k_ref), (v_hbm, v_ref), (q_hbm, q_ref), (g_hbm, g_ref))
        )
    ]
    for copy in copies:
        copy.start()
    pack[...] = jnp.zeros(pack.shape, F32)
    for side, source in enumerate((k_ref, v_ref)):
        copies[side].wait()
        for number in range(H):
            columns = slice(number * DH, number * DH + DH)
            plane = tmp.at[side * H + number]
            rows = source[:, columns].astype(F32)
            for level in range(1, 7):
                count = ROWS >> level
                plane[: 2 * count, :] = rows
                total = plane[pl.ds(0, count, stride=2), :] + plane[pl.ds(1, count, stride=2), :]
                exact = (total * HALF_ROOT).astype(BF16)
                rows = exact.astype(F32)
                if level < 4:
                    ref = (c1_ref, c2_ref, c3_ref)[level - 1]
                    ref[side * count : side * count + count, columns] = exact
                else:
                    for start in ((0,), (20,), (32, 34))[level - 4]:
                        start += 8 * side
                        pack[start : start + count, columns] = rows
    for number, ref in enumerate((c4_ref, c5_ref, c6_ref)):
        ref[...] = pack[16 * number : 16 * number + 16, :].astype(BF16)
    for copy in copies[2:]:
        copy.wait()


def coarsen(*operands):
    return pl.pallas_call(
        coarsen_kernel,
        out_shape=tuple(
            jax.ShapeDtypeStruct((count, D), BF16) for count in (128, 64, 32, 16, 16, 16) + (ROWS,) * 4
        ),
        in_specs=[pl.BlockSpec(memory_space=pltpu.HBM)] * 4,
        scratch_shapes=[
            pltpu.VMEM((2 * H, ROWS, DH), F32),
            pltpu.VMEM((48, D), F32),
            pltpu.SemaphoreType.DMA((4,)),
        ],
        compiler_params=PARAMS,
        name="coarsen",
    )(*operands)


def rows_at(first, count):
    row = lax.broadcasted_iota(jnp.int32, (16, 1), 0) % 8
    return (row >= first) & (row < first + count)


NEAR = 256
FAR = 256


def dot(a, b, a_dim, b_dim):
    return lax.dot_general(a, b, (((a_dim,), (b_dim,)), ((), ())), preferred_element_type=F32)


def by_head(body):
    def step(number, carry):
        body(pl.ds(pl.multiple_of(number * DH, DH), DH))
        return carry

    lax.fori_loop(0, H, step, 0, unroll=True)


def near_parts(c1, c2, c2_o):
    return (c1, 128, 64), (c2, 192, 32), (c2_o, 224, 32)


def near_kernel(q_ref, k_ref, v_ref, g_ref, *rest):
    parts, (key_ref, value_ref, exp_ref, dprob_ref, stats_ref) = rest[:3], rest[3:]
    key_ref[0:128, :] = k_ref[...]
    value_ref[0:128, :] = v_ref[...]
    for ref, start, count in near_parts(*parts):
        key_ref[start : start + count, :] = ref[:count, :]
        value_ref[start : start + count, :] = ref[count:, :]

    def head(columns):
        scores = dot(key_ref[:, columns], q_ref[:, columns], 1, 1)
        dprob = dot(value_ref[:, columns], g_ref[:, columns], 1, 1)
        top = jnp.max(scores, axis=0, keepdims=True)
        exponent = jnp.exp2((scores - top) * (SCALE * LOG2E))
        exp_ref[:, columns] = exponent
        dprob_ref[:, columns] = dprob
        stats_ref[0:1, columns] = top
        stats_ref[1:2, columns] = jnp.sum(exponent, axis=0, keepdims=True)
        stats_ref[2:3, columns] = jnp.sum(exponent * dprob, axis=0, keepdims=True)

    by_head(head)


def near_scores(*operands):
    shape = jax.ShapeDtypeStruct
    return pl.pallas_call(
        near_kernel,
        out_shape=(
            shape((NEAR, D), BF16),
            shape((NEAR, D), BF16),
            shape((NEAR, D), F32),
            shape((NEAR, D), F32),
            shape((8, D), F32),
        ),
        compiler_params=PARAMS,
        cost_estimate=pl.CostEstimate(
            flops=4 * NEAR * ROWS * D, bytes_accessed=8 * NEAR * D, transcendentals=NEAR * ROWS * H
        ),
        name="near_scores",
    )(*operands)


def far_kernel(q_ref, g_ref, stats_ref, *rest):
    tiles, rest = rest[:8], rest[8:]
    key_ref, value_ref, weight_ref, dscore_ref, joint_ref, mine_ref, other_ref = rest[:7]
    key_tmp, value_tmp = rest[7:]
    for number, ref in enumerate(tiles):
        for tile in range(3):
            rows = ref[16 * tile : 16 * tile + 16, :].astype(F32)
            start = 24 * number + 8 * tile
            key_tmp[start : start + 8, :] = rows[:8]
            value_tmp[start : start + 8, :] = rows[8:]
    key_ref[:192, :] = key_tmp[...].astype(BF16)
    value_ref[:192, :] = value_tmp[...].astype(BF16)
    for number, ref in enumerate((tiles[2], tiles[3], tiles[6], tiles[7])):
        start = 192 + 16 * number
        key_ref[start : start + 16, :] = ref[48:64, :]
        value_ref[start : start + 16, :] = ref[64:80, :]

    def head(columns):
        q = q_ref[:, columns]
        g = g_ref[:, columns]
        scores = dot(key_ref[:, columns], q, 1, 1)
        dprob = dot(value_ref[:, columns], g, 1, 1)
        near_top = stats_ref[0:1, columns]
        top = jnp.maximum(jnp.max(scores, axis=0, keepdims=True), near_top)
        exponent = jnp.exp2((scores - top) * (SCALE * LOG2E))
        near_factor = jnp.exp2((near_top - top) * (SCALE * LOG2E))
        total = near_factor * stats_ref[1:2, columns] + jnp.sum(exponent, axis=0, keepdims=True)
        moment = near_factor * stats_ref[2:3, columns] + jnp.sum(
            exponent * dprob, axis=0, keepdims=True
        )
        inverse = 1.0 / total
        delta = moment * inverse
        prob = exponent * inverse
        weights = prob.astype(BF16)
        dscore = (prob * (dprob - delta) * SCALE).astype(BF16)
        joint_ref[0:1, columns] = near_factor * inverse
        joint_ref[1:2, columns] = delta
        weight_ref[:, columns] = weights
        dscore_ref[:, columns] = dscore
        key_grad = dot(dscore, q, 1, 0)
        value_grad = dot(weights, g, 1, 0)
        for core, ref in enumerate((mine_ref, other_ref)):
            out = 0
            for number in range(4):
                pieces = [(96 * core + 24 * number + 8 * tile, 8) for tile in range(3)]
                if number > 1:
                    pieces.append((192 + 32 * core + 16 * (number - 2), 16))
                for start, count in pieces:
                    both = jnp.concatenate(
                        [key_grad[start : start + count], value_grad[start : start + count]], axis=0
                    )
                    ref[out : out + 2 * count, columns] = both.astype(ref.dtype)
                    out += 2 * count

    by_head(head)


def far_attend(*operands):
    shape = jax.ShapeDtypeStruct
    return pl.pallas_call(
        far_kernel,
        out_shape=(
            shape((FAR, D), BF16),
            shape((FAR, D), BF16),
            shape((FAR, D), BF16),
            shape((FAR, D), BF16),
            shape((8, D), F32),
            shape((FAR, D), F32),
            shape((FAR, D), BF16),
        ),
        scratch_shapes=[pltpu.VMEM((192, D), F32), pltpu.VMEM((192, D), F32)],
        compiler_params=PARAMS,
        cost_estimate=pl.CostEstimate(
            flops=8 * FAR * ROWS * D, bytes_accessed=8 * FAR * D, transcendentals=FAR * ROWS * H
        ),
        name="far_attend",
    )(*operands)


def rest_kernel(
    q_ref, g_ref, near_key, near_value, exp_ref, dprob_ref,
    far_key, far_value, weight_ref, dscore_ref, joint_ref,
    out_ref, grad_q_ref, local_k_ref, local_v_ref, mine_ref, other_ref,
):
    def head(columns):
        prob = exp_ref[:, columns] * joint_ref[0:1, columns]
        weights = prob.astype(BF16)
        delta = joint_ref[1:2, columns]
        dscore = (prob * (dprob_ref[:, columns] - delta) * SCALE).astype(BF16)
        output = dot(weights, near_value[:, columns], 0, 0)
        output += dot(weight_ref[:, columns], far_value[:, columns], 0, 0)
        out_ref[:, columns] = output.astype(BF16)
        grad_q = dot(dscore, near_key[:, columns], 0, 0)
        grad_q += dot(dscore_ref[:, columns], far_key[:, columns], 0, 0)
        grad_q_ref[:, columns] = grad_q.astype(BF16)
        key_grad = dot(dscore, q_ref[:, columns], 1, 0)
        value_grad = dot(weights, g_ref[:, columns], 1, 0)
        local_k_ref[:, columns] = key_grad[0:128]
        local_v_ref[:, columns] = value_grad[0:128]
        targets = ((other_ref, 0), (mine_ref, 0), (other_ref, 128))
        for (ref, out), (_, start, count) in zip(targets, near_parts(*targets)):
            ref[out : out + count, columns] = key_grad[start : start + count].astype(ref.dtype)
            out += count
            ref[out : out + count, columns] = value_grad[start : start + count].astype(ref.dtype)

    by_head(head)


def rest_attend(*operands):
    shape = jax.ShapeDtypeStruct
    return pl.pallas_call(
        rest_kernel,
        out_shape=(
            shape((ROWS, D), BF16),
            shape((ROWS, D), BF16),
            shape((ROWS, D), F32),
            shape((ROWS, D), F32),
            shape((64, D), F32),
            shape((192, D), BF16),
        ),
        compiler_params=PARAMS,
        cost_estimate=pl.CostEstimate(
            flops=4 * (2 * NEAR + FAR) * ROWS * D, bytes_accessed=16 * NEAR * D, transcendentals=0
        ),
        name="rest_attend",
    )(*operands)


def chip_kernel(mine_ref, got_ref, *pieces):
    start = 0
    skip = got_ref.shape[0] - mine_ref.shape[0]
    for ref in pieces:
        count = ref.shape[0]
        got = got_ref[skip + start : skip + start + count, :].astype(F32)
        ref[...] = (mine_ref[start : start + count, :] + got).astype(ref.dtype)
        start += count


def chip_sum(mine, got, pieces):
    return pl.pallas_call(
        chip_kernel,
        out_shape=tuple(jax.ShapeDtypeStruct((count, D), kind) for count, kind in pieces),
        compiler_params=PARAMS,
        name="chip_sum",
    )(mine, got)


def plane_kernel(own_ref, near_ref, far2_ref, far3_ref, keep_ref, send_ref):
    total = (own_ref[...] + near_ref[...].astype(F32)) + (
        far2_ref[:48, :].astype(F32) + far3_ref[:48, :].astype(F32)
    )
    keep_ref[...] = total[:16, :]
    send_ref[...] = total[16:, :].astype(BF16)


def plane_sum(own, near, far2, far3):
    return pl.pallas_call(
        plane_kernel,
        out_shape=(jax.ShapeDtypeStruct((16, D), F32), jax.ShapeDtypeStruct((32, D), BF16)),
        compiler_params=PARAMS,
        name="plane_sum",
    )(own, near, far2, far3)


def finish_kernel(
    local_k_ref, local_v_ref, c1_ref, c2_ref, far2_ref, far3_ref, z1_ref, z2_ref, z7_ref,
    grad_k_ref, grad_v_ref, tmp, pick,
):
    for number, ref in enumerate((z1_ref, z2_ref, z7_ref)):
        pick[16 * number : 16 * number + 16, :] = ref[:16, :].astype(F32)
    for side, (local_ref, out_ref) in enumerate(
        ((local_k_ref, grad_k_ref), (local_v_ref, grad_v_ref))
    ):
        for number in range(H):
            columns = slice(number * DH, number * DH + DH)
            plane = tmp.at[side * H + number]

            def part(start, count, side=side, columns=columns):
                start += 8 * side
                return pick[start : start + count, columns]

            def rows(ref, start, count, side=side, columns=columns):
                start += side * count
                return ref[start : start + count, columns].astype(F32)

            parts = {
                6: part(32, 2) + part(34, 2),
                5: part(20, 4),
                4: part(0, 8),
                3: rows(far2_ref, 48, 16) + rows(far3_ref, 48, 16),
                2: rows(c2_ref, 0, 32),
                1: rows(c1_ref, 0, 64),
                0: local_ref[:, columns],
            }
            total = parts[6]
            for level in range(5, -1, -1):
                count = ROWS >> level
                half = total * HALF_ROOT
                plane[pl.ds(0, count // 2, stride=2), :] = half
                plane[pl.ds(1, count // 2, stride=2), :] = half
                total = plane[:count, :] + parts[level]
            out_ref[:, columns] = total.astype(BF16)


def finish(*operands):
    shape = jax.ShapeDtypeStruct
    return pl.pallas_call(
        finish_kernel,
        out_shape=(shape((ROWS, D), BF16), shape((ROWS, D), BF16)),
        scratch_shapes=[pltpu.VMEM((2 * H, ROWS, DH), F32), pltpu.VMEM((48, D), F32)],
        compiler_params=PARAMS,
        name="finish",
    )(*operands)


def together(*arrays):
    return lax.optimization_barrier(arrays)


def together(*arrays):
    return lax.optimization_barrier(arrays)


def per_device(queries, keys, values, cotangent):
    pinned = [
        pltpu.with_memory_space_constraint(array, pltpu.HBM)
        for array in (keys, values, queries, cotangent)
    ]
    c1, c2, c3, c4, c5, c6, keys, values, queries, cotangent = coarsen(*pinned)
    six = swap(c6, 56)
    c1 = swap(c1, 1)
    c2 = swap(c2, 2)
    two = swap(jnp.where(rows_at(0, 2), six, c5), 16)
    keep = jnp.where(rows_at(2, 2), six, two)
    send, c2 = together(jnp.concatenate([keep, c4]), c2)
    core = swap(c2, 1)
    own = jnp.concatenate([keep, swap(send, 8)])
    own, c1, c2, core = together(own, c1, c2, core)
    far = jnp.concatenate([own, c3])
    near, far3, far2 = swap(own, 2), swap(far, 6), swap(far, 4)
    near_key, near_value, exponent, dprob, stats = near_scores(
        queries, keys, values, cotangent, c1, c2, core
    )
    near, far2, far3, stats = together(near, far2, far3, stats)
    tiles = [own, near, far2, far3]
    tiles += [swap(part, 1) for part in tiles]
    far_key, far_value, weights, dscore, joint, mine, other = far_attend(
        queries, cotangent, stats, *tiles
    )
    got = swap(other, 1)
    own, near, far2, far3 = chip_sum(mine, got, ((48, F32), (48, BF16), (80, BF16), (80, BF16)))
    joint, near, far2, far3 = together(joint, near, far2, far3)
    near, far3, far2 = swap(near, 2), swap(far3, 6), swap(far2, 4)
    output, grad_queries, local_k, local_v, mine, other = rest_attend(
        queries, cotangent, near_key, near_value, exponent, dprob,
        far_key, far_value, weights, dscore, joint,
    )
    near, far2, far3, other = together(near, far2, far3, other)
    keep, send = plane_sum(own, near, far2, far3)
    got = swap(send, 8)
    core = swap(other, 1)
    (c2,) = chip_sum(mine, core, ((64, BF16),))
    c2 = swap(c2, 2)
    keep = (keep + got[:16].astype(F32)).astype(BF16)
    two = swap(keep, 16)
    six = swap(jnp.where(rows_at(2, 2), keep, two), 56)
    grad_keys, grad_values = finish(
        local_k, local_v, core[:128], c2, far2, far3, got[16:], two, six
    )
    return output, grad_queries, grad_keys, grad_values


def solution(mesh):
    spec = P(("dp", "ctx"), None)
    return jax.shard_map(
        per_device,
        mesh=mesh,
        in_specs=(spec,) * 4,
        out_specs=(spec,) * 4,
        check_vma=False,
    )
```

time: 75.4 us -> 65.2 us (0.86)
  the two profiles are of different devices: /device:TPU:6 before, /device:TPU:36 now
where the time goes in v1:
time: 65.2 us; the launch traced here: 65.1 us
  waiting for transfers between devices  27.2 us (42%)
  starting transfers between devices  25.4 us (39%)
  Pallas kernels  9.49 us (15%)
  local copies, waits for them, and re-layouts  1.99 us (3%)
  between operations  0.74 us (1%)
    ppermute x22, waiting for transfers between devices, swap(): return lax.ppermute(block, 'ctx', [(i, i ^ mask) for i in range(count)])  27.2 us
    ppermute x22, starting transfers between devices, swap(): return lax.ppermute(block, 'ctx', [(i, i ^ mask) for i in range(count)])  25.4 us
    pallas_call x1, Pallas kernels, rest_attend(): pl.pallas_call(rest_kernel, out_shape=(shape((ROWS, D), BF16), shape((ROW...  3.6 us
    pallas_call x1, Pallas kernels, far_attend(): pl.pallas_call(far_kernel, out_shape=(shape((FAR, D), BF16), shape((FAR,...  2.49 us
    unnamed x5, local copies, waits for them, and re-layouts  1.96 us
    pallas_call x1, Pallas kernels, coarsen(): pl.pallas_call(coarsen_kernel, out_shape=tuple((jax.ShapeDtypeStruct((cou...  1.42 us
  transfers between devices with their start and end apart: 22, of which 13 were waited for; matrix products, arithmetic and copies ran while one was open for 0% of the time, Pallas kernels for 7%

profile of v1, /device:TPU:36, one launch (start us, length us, event | category | flops | bytes accessed | tf_op | source)
XLA Modules:
  0.0 65.1 jit_solution(13931495795676843805)
XLA Ops:
  0.6 1.4 %coarsen.1 = (bf16[128,1024]{1,0:T(8,128)(2,1)S(1)}, bf16[64,1024]{1,0:T(8,128)(2,1)S(1)}, bf16[32,1024]{1,0:T(8,128)(2,1)S(1)}, bf16[16,1024]{1,0:T(8,128)(2,1)...) custom-call(bf16[128,1024]{1,0:T(8,128)(2,1)} %k_hbm.1, ...), custom_call_target="tpu_custom_call" | custom-call | tf_op jit(solution)/shard_map/coarsen/pallas_call | solution.py:66
  2.1 5.9 %collective-permute-start = (bf16[16,1024]{1,0:T(8,128)(2,1)S(1)}, bf16[16,1024]{1,0:T(8,128)(2,1)S(1)}, u32[]{:S(2)}, u32[]{:S(2)}) collective-permute-start(bf16[16,1024]{1,0:T(8,128)(2,1)S(1)} %get-tuple-element.62), channel_id=1, source_target_pairs={{0,224},{4,228},{8,232},{12,236},{16,240},{20,244},{24,248},{28,25... | collective-permute-start | bytes 98312 | tf_op jit(solution)/shard_map/ppermute | solution.py:23
  8.0 1.6 %collective-permute-start.2 = (bf16[64,1024]{1,0:T(8,128)(2,1)S(1)}, bf16[64,1024]{1,0:T(8,128)(2,1)S(1)}, u32[]{:S(2)}, u32[]{:S(2)}) collective-permute-start(bf16[64,1024]{1,0:T(8,128)(2,1)S(1)} %get-tuple-element.65), channel_id=1, source_target_pairs={{0,8},{4,12},{8,0},{12,4},{16,24},{20,28},{24,16},{28,20},{32,40},... | collective-permute-start | bytes 393224 | tf_op jit(solution)/shard_map/ppermute | solution.py:23
  10.6 4.2 %collective-permute-done.1 = bf16[16,1024]{1,0:T(8,128)(2,1)S(1)} collective-permute-done((bf16[16,1024]{1,0:T(8,128)(2,1)S(1)}, bf16[16,1024]{1,0:T(8,128)(2,1)S(1)}, u32[]{:S(2)}, u32[]{:S(2)}) %collective-permute-start.1) | collective-permute-done | bytes 32800 | tf_op jit(solution)/shard_map/ppermute | solution.py:23
  15.1 4.1 %collective-permute-done.3 = bf16[32,1024]{1,0:T(8,128)(2,1)S(1)} collective-permute-done((bf16[32,1024]{1,0:T(8,128)(2,1)S(1)}, bf16[32,1024]{1,0:T(8,128)(2,1)S(1)}, u32[]{:S(2)}, u32[]{:S(2)}) %collective-permute-start.3) | collective-permute-done | bytes 65568 | tf_op jit(solution)/shard_map/ppermute | solution.py:23
  19.3 3.1 %collective-permute-start.8 = (bf16[80,1024]{1,0:T(8,128)(2,1)S(1)}, bf16[80,1024]{1,0:T(8,128)(2,1)S(1)}, u32[]{:S(2)}, u32[]{:S(2)}) collective-permute-start(bf16[80,1024]{1,0:T(8,128)(2,1)S(1)} %constant_dynamic-update-slice_fusion), channel_id=1, source_target_pairs={{0,24},{4,28},{8,16},{12,20},{16,8},{20,12},{24,0},{28,4},{32,56},... | collective-permute-start | bytes 491528 | tf_op jit(solution)/shard_map/ppermute | solution.py:23
  24.2 1.0 %copy-done = f32[256,1024]{1,0:T(8,128)} copy-done((f32[256,1024]{1,0:T(8,128)}, f32[256,1024]{1,0:T(8,128)S(1)}, u32[]{:S(2)}) %copy-start) | copy-done | bytes 1048600
  25.2 1.0 %copy-done.1 = f32[256,1024]{1,0:T(8,128)} copy-done((f32[256,1024]{1,0:T(8,128)}, f32[256,1024]{1,0:T(8,128)S(1)}, u32[]{:S(2)}) %copy-start.1) | copy-done | bytes 1048600
  26.2 1.7 %collective-permute-done.6.rest_1_ = bf16[48,1024]{1,0:T(8,128)(2,1)S(1)} collective-permute-done((bf16[48,1024]{1,0:T(8,128)(2,1)S(1)}, bf16[48,1024]{1,0:T(8,128)(2,1)S(1)}, u32[]{:S(2)}, u32[]{:S(2)}) %collective-permute-start.6) | collective-permute-done | bytes 98336 | tf_op jit(solution)/shard_map/ppermute | solution.py:23
  27.9 1.3 %collective-permute-done.7.rest_2_ = bf16[80,1024]{1,0:T(8,128)(2,1)S(1)} collective-permute-done((bf16[80,1024]{1,0:T(8,128)(2,1)S(1)}, bf16[80,1024]{1,0:T(8,128)(2,1)S(1)}, u32[]{:S(2)}, u32[]{:S(2)}) %collective-permute-start.7) | collective-permute-done | bytes 163872 | tf_op jit(solution)/shard_map/ppermute | solution.py:23
  31.2 2.5 %far_attend.1 = (bf16[256,1024]{1,0:T(8,128)(2,1)S(1)}, bf16[256,1024]{1,0:T(8,128)(2,1)S(1)}, bf16[256,1024]{1,0:T(8,128)(2,1)S(1)}, bf16[256,1024]{1,0:T(8,128...) custom-call(bf16[128,1024]{1,0:T(8,128)(2,1)S(1)} %get-tuple-element.58.q_ref, ...), custom_call_target="tpu_custom_call" | custom-call | flops 268435456 | bytes 2097152 | tf_op jit(solution)/shard_map/far_attend/pallas_call | solution.py:207
  34.2 1.6 %collective-permute-done.13.got_ref = bf16[256,1024]{1,0:T(8,128)(2,1)S(1)} collective-permute-done((bf16[256,1024]{1,0:T(8,128)(2,1)S(1)}, bf16[256,1024]{1,0:T(8,128)(2,1)S(1)}, u32[]{:S(2)}, u32[]{:S(2)}) %collective-permute-start.13) | collective-permute-done | bytes 524320 | tf_op jit(solution)/shard_map/ppermute | solution.py:23
  35.8 1.9 %collective-permute-start.15 = (bf16[80,1024]{1,0:T(8,128)(2,1)S(1)}, bf16[80,1024]{1,0:T(8,128)(2,1)S(1)}, u32[]{:S(2)}, u32[]{:S(2)}) collective-permute-start(bf16[80,1024]{1,0:T(8,128)(2,1)S(1)} %get-tuple-element.99), channel_id=1, source_target_pairs={{0,16},{4,20},{8,24},{12,28},{16,0},{20,4},{24,8},{28,12},{32,48},... | collective-permute-start | bytes 491528 | tf_op jit(solution)/shard_map/ppermute | solution.py:23
  37.7 1.1 %collective-permute-start.16 = (bf16[80,1024]{1,0:T(8,128)(2,1)S(1)}, bf16[80,1024]{1,0:T(8,128)(2,1)S(1)}, u32[]{:S(2)}, u32[]{:S(2)}) collective-permute-start(bf16[80,1024]{1,0:T(8,128)(2,1)S(1)} %get-tuple-element.100), channel_id=1, source_target_pairs={{0,24},{4,28},{8,16},{12,20},{16,8},{20,12},{24,0},{28,4},{32,56},... | collective-permute-start | bytes 491528 | tf_op jit(solution)/shard_map/ppermute | solution.py:23
  39.4 3.6 %rest_attend.1 = (bf16[128,1024]{1,0:T(8,128)(2,1)}, bf16[128,1024]{1,0:T(8,128)(2,1)}, f32[128,1024]{1,0:T(8,128)S(1)}, f32[128,1024]{1,0:T(8,128)S(1)}, f32[64...) custom-call(bf16[128,1024]{1,0:T(8,128)(2,1)S(1)} %get-tuple-element.58.q_ref, ...), custom_call_target="tpu_custom_call" | custom-call | flops 402653184 | bytes 4194304 | tf_op jit(solution)/shard_map/rest_attend/pallas_call | solution.py:258
  43.0 2.0 %collective-permute-done.14.near_ref = bf16[48,1024]{1,0:T(8,128)(2,1)S(1)} collective-permute-done((bf16[48,1024]{1,0:T(8,128)(2,1)S(1)}, bf16[48,1024]{1,0:T(8,128)(2,1)S(1)}, u32[]{:S(2)}, u32[]{:S(2)}) %collective-permute-start.14) | collective-permute-done | bytes 98336 | tf_op jit(solution)/shard_map/ppermute | solution.py:23
  45.0 2.4 %collective-permute-done.16.far3_ref = bf16[80,1024]{1,0:T(8,128)(2,1)S(1)} collective-permute-done((bf16[80,1024]{1,0:T(8,128)(2,1)S(1)}, bf16[80,1024]{1,0:T(8,128)(2,1)S(1)}, u32[]{:S(2)}, u32[]{:S(2)}) %collective-permute-start.16) | collective-permute-done | bytes 163872 | tf_op jit(solution)/shard_map/ppermute | solution.py:23
  47.4 0.9 %collective-permute-start.19 = (bf16[32,1024]{1,0:T(8,128)(2,1)S(1)}, bf16[32,1024]{1,0:T(8,128)(2,1)S(1)}, u32[]{:S(2)}, u32[]{:S(2)}) collective-permute-start(bf16[32,1024]{1,0:T(8,128)(2,1)S(1)} %get-tuple-element.108), channel_id=1, source_target_pairs={{0,32},{4,36},{8,40},{12,44},{16,48},{20,52},{24,56},{28,60},{32,0... | collective-permute-start | bytes 196616 | tf_op jit(solution)/shard_map/ppermute | solution.py:23
  48.4 3.7 %collective-permute-done.19 = bf16[32,1024]{1,0:T(8,128)(2,1)S(1)} collective-permute-done((bf16[32,1024]{1,0:T(8,128)(2,1)S(1)}, bf16[32,1024]{1,0:T(8,128)(2,1)S(1)}, u32[]{:S(2)}, u32[]{:S(2)}) %collective-permute-start.19) | collective-permute-done | bytes 65568 | tf_op jit(solution)/shard_map/ppermute | solution.py:23
  52.0 1.4 %collective-permute-start.20 = (bf16[16,1024]{1,0:T(8,128)(2,1)S(1)}, bf16[16,1024]{1,0:T(8,128)(2,1)S(1)}, u32[]{:S(2)}, u32[]{:S(2)}) collective-permute-start(bf16[16,1024]{1,0:T(8,128)(2,1)S(1)} %add_convert_fusion), channel_id=1, source_target_pairs={{0,64},{4,68},{8,72},{12,76},{16,80},{20,84},{24,88},{28,92},{32,9... | collective-permute-start | bytes 98312 | tf_op jit(solution)/shard_map/ppermute | solution.py:23
  53.8 3.1 %collective-permute-done.20.z2_ref = bf16[16,1024]{1,0:T(8,128)(2,1)S(1)} collective-permute-done((bf16[16,1024]{1,0:T(8,128)(2,1)S(1)}, bf16[16,1024]{1,0:T(8,128)(2,1)S(1)}, u32[]{:S(2)}, u32[]{:S(2)}) %collective-permute-start.20) | collective-permute-done | bytes 32800 | tf_op jit(solution)/shard_map/ppermute | solution.py:23
  57.0 5.1 %collective-permute-start.21 = (bf16[16,1024]{1,0:T(8,128)(2,1)S(1)}, bf16[16,1024]{1,0:T(8,128)(2,1)S(1)}, u32[]{:S(2)}, u32[]{:S(2)}) collective-permute-start(bf16[16,1024]{1,0:T(8,128)(2,1)S(1)} %broadcast_select_fusion.1), channel_id=1, source_target_pairs={{0,224},{4,228},{8,232},{12,236},{16,240},{20,244},{24,248},{28,25... | collective-permute-start | bytes 98312 | tf_op jit(solution)/shard_map/ppermute | solution.py:23
  62.1 1.9 %collective-permute-done.21.z7_ref = bf16[16,1024]{1,0:T(8,128)(2,1)S(1)} collective-permute-done((bf16[16,1024]{1,0:T(8,128)(2,1)S(1)}, bf16[16,1024]{1,0:T(8,128)(2,1)S(1)}, u32[]{:S(2)}, u32[]{:S(2)}) %collective-permute-start.21) | collective-permute-done | bytes 32800 | tf_op jit(solution)/shard_map/ppermute | solution.py:23
  63.9 1.1 %finish.1 = (bf16[128,1024]{1,0:T(8,128)(2,1)}, bf16[128,1024]{1,0:T(8,128)(2,1)}) custom-call(f32[128,1024]{1,0:T(8,128)S(1)} %get-tuple-element.96.local_k_ref, f32[128,1024]{1,0:T(8,128)S(1)} %get-tuple-element.97.local_v_ref, bf16[128,1024]{1,0:T(8,128)(2,1)S(1)} %slice.12.c1_ref, bf16[64,1024]{1,0:T(8,128)(2,1)S(1)} %collective-permute-done.18.c2_ref, ...), custom_call_target="tpu_custom_call" | custom-call | tf_op jit(solution)/shard_map/finish/pallas_call | solution.py:354
  (44 shorter events, 6.8 us)
Async XLA Ops:
  2.1 7.8 %collective-permute-start = (bf16[16,1024]{1,0:T(8,128)(2,1)S(1)}, bf16[16,1024]{1,0:T(8,128)(2,1)S(1)}, u32[]{:S(2)}, u32[]{:S(2)}) collective-permute-start(bf16[16,1024]{1,0:T(8,128)(2,1)S(1)} %get-tuple-element.62), channel_id=1, source_target_pairs={{0,224},{4,228},{8,232},{12,236},{16,240},{20,244},{24,248},{28,25... | collective-permute-start | bytes 98312 | tf_op jit(solution)/shard_map/ppermute | solution.py:23
  8.0 6.9 %collective-permute-start.2 = (bf16[64,1024]{1,0:T(8,128)(2,1)S(1)}, bf16[64,1024]{1,0:T(8,128)(2,1)S(1)}, u32[]{:S(2)}, u32[]{:S(2)}) collective-permute-start(bf16[64,1024]{1,0:T(8,128)(2,1)S(1)} %get-tuple-element.65), channel_id=1, source_target_pairs={{0,8},{4,12},{8,0},{12,4},{16,24},{20,28},{24,16},{28,20},{32,40},... | collective-permute-start | bytes 393224 | tf_op jit(solution)/shard_map/ppermute | solution.py:23
  9.6 9.7 %collective-permute-start.4 = (bf16[128,1024]{1,0:T(8,128)(2,1)S(1)}, bf16[128,1024]{1,0:T(8,128)(2,1)S(1)}, u32[]{:S(2)}, u32[]{:S(2)}) collective-permute-start(bf16[128,1024]{1,0:T(8,128)(2,1)S(1)} %get-tuple-element.67), channel_id=1, source_target_pairs={{0,4},{4,0},{8,12},{12,8},{16,20},{20,16},{24,28},{28,24},{32,36},... | collective-permute-start | bytes 786440 | tf_op jit(solution)/shard_map/ppermute | solution.py:23
  10.0 4.8 %collective-permute-start.1 = (bf16[16,1024]{1,0:T(8,128)(2,1)S(1)}, bf16[16,1024]{1,0:T(8,128)(2,1)S(1)}, u32[]{:S(2)}, u32[]{:S(2)}) collective-permute-start(bf16[16,1024]{1,0:T(8,128)(2,1)S(1)} %broadcast_select_fusion), channel_id=1, source_target_pairs={{0,64},{4,68},{8,72},{12,76},{16,80},{20,84},{24,88},{28,92},{32,9... | collective-permute-start | bytes 98312 | tf_op jit(solution)/shard_map/ppermute | solution.py:23
  14.9 4.4 %collective-permute-start.3 = (bf16[32,1024]{1,0:T(8,128)(2,1)S(1)}, bf16[32,1024]{1,0:T(8,128)(2,1)S(1)}, u32[]{:S(2)}, u32[]{:S(2)}) collective-permute-start(bf16[32,1024]{1,0:T(8,128)(2,1)S(1)} %pad_maximum_fusion.1), channel_id=1, source_target_pairs={{0,32},{4,36},{8,40},{12,44},{16,48},{20,52},{24,56},{28,60},{32,0... | collective-permute-start | bytes 196616 | tf_op jit(solution)/shard_map/ppermute | solution.py:23
  15.1 4.2 %collective-permute-start.5 = (bf16[64,1024]{1,0:T(8,128)(2,1)S(1)}, bf16[64,1024]{1,0:T(8,128)(2,1)S(1)}, u32[]{:S(2)}, u32[]{:S(2)}) collective-permute-start(bf16[64,1024]{1,0:T(8,128)(2,1)S(1)} %collective-permute-done.2.rest_1_), channel_id=1, source_target_pairs={{0,4},{4,0},{8,12},{12,8},{16,20},{20,16},{24,28},{28,24},{32,36},... | collective-permute-start | bytes 393224 | tf_op jit(solution)/shard_map/ppermute | solution.py:23
  19.3 8.6 %collective-permute-start.8 = (bf16[80,1024]{1,0:T(8,128)(2,1)S(1)}, bf16[80,1024]{1,0:T(8,128)(2,1)S(1)}, u32[]{:S(2)}, u32[]{:S(2)}) collective-permute-start(bf16[80,1024]{1,0:T(8,128)(2,1)S(1)} %constant_dynamic-update-slice_fusion), channel_id=1, source_target_pairs={{0,24},{4,28},{8,16},{12,20},{16,8},{20,12},{24,0},{28,4},{32,56},... | collective-permute-start | bytes 491528 | tf_op jit(solution)/shard_map/ppermute | solution.py:23
  22.4 6.8 %collective-permute-start.7 = (bf16[80,1024]{1,0:T(8,128)(2,1)S(1)}, bf16[80,1024]{1,0:T(8,128)(2,1)S(1)}, u32[]{:S(2)}, u32[]{:S(2)}) collective-permute-start(bf16[80,1024]{1,0:T(8,128)(2,1)S(1)} %constant_dynamic-update-slice_fusion), channel_id=1, source_target_pairs={{0,16},{4,20},{8,24},{12,28},{16,0},{20,4},{24,8},{28,12},{32,48},... | collective-permute-start | bytes 491528 | tf_op jit(solution)/shard_map/ppermute | solution.py:23
  23.0 4.8 %collective-permute-start.6 = (bf16[48,1024]{1,0:T(8,128)(2,1)S(1)}, bf16[48,1024]{1,0:T(8,128)(2,1)S(1)}, u32[]{:S(2)}, u32[]{:S(2)}) collective-permute-start(bf16[48,1024]{1,0:T(8,128)(2,1)S(1)} %pad_maximum_fusion.rest_0_), channel_id=1, source_target_pairs={{0,8},{4,12},{8,0},{12,4},{16,24},{20,28},{24,16},{28,20},{32,40},... | collective-permute-start | bytes 294920 | tf_op jit(solution)/shard_map/ppermute | solution.py:23
  24.2 1.0 %copy-start = (f32[256,1024]{1,0:T(8,128)}, f32[256,1024]{1,0:T(8,128)S(1)}, u32[]{:S(2)}) copy-start(f32[256,1024]{1,0:T(8,128)S(1)} %get-tuple-element.74.exp_ref) | copy-start | bytes 3145732
  25.2 1.0 %copy-start.1 = (f32[256,1024]{1,0:T(8,128)}, f32[256,1024]{1,0:T(8,128)S(1)}, u32[]{:S(2)}) copy-start(f32[256,1024]{1,0:T(8,128)S(1)} %get-tuple-element.75.dprob_ref) | copy-start | bytes 3145732
  29.2 2.0 %collective-permute-start.11 = (bf16[80,1024]{1,0:T(8,128)(2,1)S(1)}, bf16[80,1024]{1,0:T(8,128)(2,1)S(1)}, u32[]{:S(2)}, u32[]{:S(2)}) collective-permute-start(bf16[80,1024]{1,0:T(8,128)(2,1)S(1)} %collective-permute-done.7.rest_2_), channel_id=1, source_target_pairs={{0,4},{4,0},{8,12},{12,8},{16,20},{20,16},{24,28},{28,24},{32,36},... | collective-permute-start | bytes 491528 | tf_op jit(solution)/shard_map/ppermute | solution.py:23
  29.2 2.0 %collective-permute-start.12 = (bf16[80,1024]{1,0:T(8,128)(2,1)S(1)}, bf16[80,1024]{1,0:T(8,128)(2,1)S(1)}, u32[]{:S(2)}, u32[]{:S(2)}) collective-permute-start(bf16[80,1024]{1,0:T(8,128)(2,1)S(1)} %collective-permute-done.8.rest_3_), channel_id=1, source_target_pairs={{0,4},{4,0},{8,12},{12,8},{16,20},{20,16},{24,28},{28,24},{32,36},... | collective-permute-start | bytes 491528 | tf_op jit(solution)/shard_map/ppermute | solution.py:23
  29.7 1.3 %collective-permute-start.9 = (bf16[48,1024]{1,0:T(8,128)(2,1)S(1)}, bf16[48,1024]{1,0:T(8,128)(2,1)S(1)}, u32[]{:S(2)}, u32[]{:S(2)}) collective-permute-start(bf16[48,1024]{1,0:T(8,128)(2,1)S(1)} %pad_maximum_fusion.rest_0_), channel_id=1, source_target_pairs={{0,4},{4,0},{8,12},{12,8},{16,20},{20,16},{24,28},{28,24},{32,36},... | collective-permute-start | bytes 294920 | tf_op jit(solution)/shard_map/ppermute | solution.py:23
  29.8 1.5 %collective-permute-start.10 = (bf16[48,1024]{1,0:T(8,128)(2,1)S(1)}, bf16[48,1024]{1,0:T(8,128)(2,1)S(1)}, u32[]{:S(2)}, u32[]{:S(2)}) collective-permute-start(bf16[48,1024]{1,0:T(8,128)(2,1)S(1)} %collective-permute-done.6.rest_1_), channel_id=1, source_target_pairs={{0,4},{4,0},{8,12},{12,8},{16,20},{20,16},{24,28},{28,24},{32,36},... | collective-permute-start | bytes 294920 | tf_op jit(solution)/shard_map/ppermute | solution.py:23
  33.7 2.0 %collective-permute-start.13 = (bf16[256,1024]{1,0:T(8,128)(2,1)S(1)}, bf16[256,1024]{1,0:T(8,128)(2,1)S(1)}, u32[]{:S(2)}, u32[]{:S(2)}) collective-permute-start(bf16[256,1024]{1,0:T(8,128)(2,1)S(1)} %get-tuple-element.89), channel_id=1, source_target_pairs={{0,4},{4,0},{8,12},{12,8},{16,20},{20,16},{24,28},{28,24},{32,36},... | collective-permute-start | bytes 1572872 | tf_op jit(solution)/shard_map/ppermute | solution.py:23
  35.8 9.2 %collective-permute-start.15 = (bf16[80,1024]{1,0:T(8,128)(2,1)S(1)}, bf16[80,1024]{1,0:T(8,128)(2,1)S(1)}, u32[]{:S(2)}, u32[]{:S(2)}) collective-permute-start(bf16[80,1024]{1,0:T(8,128)(2,1)S(1)} %get-tuple-element.99), channel_id=1, source_target_pairs={{0,16},{4,20},{8,24},{12,28},{16,0},{20,4},{24,8},{28,12},{32,48},... | collective-permute-start | bytes 491528 | tf_op jit(solution)/shard_map/ppermute | solution.py:23
  37.7 9.7 %collective-permute-start.16 = (bf16[80,1024]{1,0:T(8,128)(2,1)S(1)}, bf16[80,1024]{1,0:T(8,128)(2,1)S(1)}, u32[]{:S(2)}, u32[]{:S(2)}) collective-permute-start(bf16[80,1024]{1,0:T(8,128)(2,1)S(1)} %get-tuple-element.100), channel_id=1, source_target_pairs={{0,24},{4,28},{8,16},{12,20},{16,8},{20,12},{24,0},{28,4},{32,56},... | collective-permute-start | bytes 491528 | tf_op jit(solution)/shard_map/ppermute | solution.py:23
  38.8 6.2 %collective-permute-start.14 = (bf16[48,1024]{1,0:T(8,128)(2,1)S(1)}, bf16[48,1024]{1,0:T(8,128)(2,1)S(1)}, u32[]{:S(2)}, u32[]{:S(2)}) collective-permute-start(bf16[48,1024]{1,0:T(8,128)(2,1)S(1)} %get-tuple-element.98), channel_id=1, source_target_pairs={{0,8},{4,12},{8,0},{12,4},{16,24},{20,28},{24,16},{28,20},{32,40},... | collective-permute-start | bytes 294920 | tf_op jit(solution)/shard_map/ppermute | solution.py:23
  47.4 6.1 %collective-permute-start.17 = (bf16[192,1024]{1,0:T(8,128)(2,1)S(1)}, bf16[192,1024]{1,0:T(8,128)(2,1)S(1)}, u32[]{:S(2)}, u32[]{:S(2)}) collective-permute-start(bf16[192,1024]{1,0:T(8,128)(2,1)S(1)} %get-tuple-element.102), channel_id=1, source_target_pairs={{0,4},{4,0},{8,12},{12,8},{16,20},{20,16},{24,28},{28,24},{32,36},... | collective-permute-start | bytes 1179656 | tf_op jit(solution)/shard_map/ppermute | solution.py:23
  47.4 4.6 %collective-permute-start.19 = (bf16[32,1024]{1,0:T(8,128)(2,1)S(1)}, bf16[32,1024]{1,0:T(8,128)(2,1)S(1)}, u32[]{:S(2)}, u32[]{:S(2)}) collective-permute-start(bf16[32,1024]{1,0:T(8,128)(2,1)S(1)} %get-tuple-element.108), channel_id=1, source_target_pairs={{0,32},{4,36},{8,40},{12,44},{16,48},{20,52},{24,56},{28,60},{32,0... | collective-permute-start | bytes 196616 | tf_op jit(solution)/shard_map/ppermute | solution.py:23
  52.0 4.9 %collective-permute-start.20 = (bf16[16,1024]{1,0:T(8,128)(2,1)S(1)}, bf16[16,1024]{1,0:T(8,128)(2,1)S(1)}, u32[]{:S(2)}, u32[]{:S(2)}) collective-permute-start(bf16[16,1024]{1,0:T(8,128)(2,1)S(1)} %add_convert_fusion), channel_id=1, source_target_pairs={{0,64},{4,68},{8,72},{12,76},{16,80},{20,84},{24,88},{28,92},{32,9... | collective-permute-start | bytes 98312 | tf_op jit(solution)/shard_map/ppermute | solution.py:23
  53.5 10.4 %collective-permute-start.18 = (bf16[64,1024]{1,0:T(8,128)(2,1)S(1)}, bf16[64,1024]{1,0:T(8,128)(2,1)S(1)}, u32[]{:S(2)}, u32[]{:S(2)}) collective-permute-start(bf16[64,1024]{1,0:T(8,128)(2,1)S(1)} %chip_sum.3), channel_id=1, source_target_pairs={{0,8},{4,12},{8,0},{12,4},{16,24},{20,28},{24,16},{28,20},{32,40},... | collective-permute-start | bytes 393224 | tf_op jit(solution)/shard_map/ppermute | solution.py:23
  57.0 6.9 %collective-permute-start.21 = (bf16[16,1024]{1,0:T(8,128)(2,1)S(1)}, bf16[16,1024]{1,0:T(8,128)(2,1)S(1)}, u32[]{:S(2)}, u32[]{:S(2)}) collective-permute-start(bf16[16,1024]{1,0:T(8,128)(2,1)S(1)} %broadcast_select_fusion.1), channel_id=1, source_target_pairs={{0,224},{4,228},{8,232},{12,236},{16,240},{20,244},{24,248},{28,25... | collective-permute-start | bytes 98312 | tf_op jit(solution)/shard_map/ppermute | solution.py:23

commit v2 on v1

--- a/solution.py
+++ b/solution.py
@@ -14,7 +14,7 @@
 LOG2E = 1.4426950408889634
 F32 = jnp.float32
 BF16 = jnp.bfloat16
-VMEM_LIMIT = 48 * 1024 * 1024
+VMEM_LIMIT = 16 * 1024 * 1024
 PARAMS = pltpu.CompilerParams(vmem_limit_bytes=VMEM_LIMIT)
 
 
@@ -28,18 +28,28 @@
     c1_ref, c2_ref, c3_ref, c4_ref, c5_ref, c6_ref, k_ref, v_ref, q_ref, g_ref,
     tmp, pack, sems,
 ):
+    def copy(source, target, number, columns):
+        return pltpu.make_async_copy(
+            source.at[:, columns], target.at[:, columns], sems.at[number]
+        )
+
+    half = D // 2
+    sides = ((k_hbm, k_ref), (v_hbm, v_ref))
     copies = [
-        pltpu.make_async_copy(source, target, sems.at[number])
-        for number, (source, target) in enumerate(
-            ((k_hbm, k_ref), (v_hbm, v_ref), (q_hbm, q_ref), (g_hbm, g_ref))
-        )
+        copy(source, target, 2 * part + side, pl.ds(half * part, half))
+        for part in range(2)
+        for side, (source, target) in enumerate(sides)
     ]
-    for copy in copies:
-        copy.start()
+    copies.append(copy(q_hbm, q_ref, 4, pl.ds(0, D)))
+    copies.append(copy(g_hbm, g_ref, 5, pl.ds(0, D)))
+    for each in copies:
+        each.start()
     pack[...] = jnp.zeros(pack.shape, F32)
-    for side, source in enumerate((k_ref, v_ref)):
-        copies[side].wait()
-        for number in range(H):
+    for part in range(4):
+        copies[part].wait()
+        side = part % 2
+        source = sides[side][1]
+        for number in range(part // 2 * (H // 2), (part // 2 + 1) * (H // 2)):
             columns = slice(number * DH, number * DH + DH)
             plane = tmp.at[side * H + number]
             rows = source[:, columns].astype(F32)
@@ -58,8 +68,8 @@
                         pack[start : start + count, columns] = rows
     for number, ref in enumerate((c4_ref, c5_ref, c6_ref)):
         ref[...] = pack[16 * number : 16 * number + 16, :].astype(BF16)
-    for copy in copies[2:]:
-        copy.wait()
+    for each in copies[4:]:
+        each.wait()
 
 
 def coarsen(*operands):
@@ -72,7 +82,7 @@
         scratch_shapes=[
             pltpu.VMEM((2 * H, ROWS, DH), F32),
             pltpu.VMEM((48, D), F32),
-            pltpu.SemaphoreType.DMA((4,)),
+            pltpu.SemaphoreType.DMA((6,)),
         ],
         compiler_params=PARAMS,
         name="coarsen",
@@ -85,7 +95,7 @@
 
 
 NEAR = 256
-FAR = 256
+FAR = 128
 
 
 def dot(a, b, a_dim, b_dim):
@@ -145,101 +155,184 @@
     )(*operands)
 
 
-def far_kernel(q_ref, g_ref, stats_ref, *rest):
-    tiles, rest = rest[:8], rest[8:]
-    key_ref, value_ref, weight_ref, dscore_ref, joint_ref, mine_ref, other_ref = rest[:7]
-    key_tmp, value_tmp = rest[7:]
-    for number, ref in enumerate(tiles):
+def place_far(tiles, key_ref, value_ref, key_tmp, value_tmp):
+    for number, (ref, base) in enumerate(tiles):
         for tile in range(3):
-            rows = ref[16 * tile : 16 * tile + 16, :].astype(F32)
+            rows = ref[base + 16 * tile : base + 16 * tile + 16, :].astype(F32)
             start = 24 * number + 8 * tile
             key_tmp[start : start + 8, :] = rows[:8]
             value_tmp[start : start + 8, :] = rows[8:]
-    key_ref[:192, :] = key_tmp[...].astype(BF16)
-    value_ref[:192, :] = value_tmp[...].astype(BF16)
-    for number, ref in enumerate((tiles[2], tiles[3], tiles[6], tiles[7])):
-        start = 192 + 16 * number
-        key_ref[start : start + 16, :] = ref[48:64, :]
-        value_ref[start : start + 16, :] = ref[64:80, :]
+    key_ref[:96, :] = key_tmp[...].astype(BF16)
+    value_ref[:96, :] = value_tmp[...].astype(BF16)
+    for number, (ref, base) in enumerate(tiles[2:]):
+        start = 96 + 16 * number
+        key_ref[start : start + 16, :] = ref[base + 48 : base + 64, :]
+        value_ref[start : start + 16, :] = ref[base + 64 : base + 80, :]
+
+
+def pack_far(key_grad, value_grad, ref, columns):
+    out = 0
+    for number in range(4):
+        pieces = [(24 * number + 8 * tile, 8) for tile in range(3)]
+        if number > 1:
+            pieces.append((96 + 16 * (number - 2), 16))
+        for start, count in pieces:
+            both = jnp.concatenate(
+                [key_grad[start : start + count], value_grad[start : start + count]], axis=0
+            )
+            ref[out : out + 2 * count, columns] = both.astype(ref.dtype)
+            out += 2 * count
+
+
+def power(difference):
+    return jnp.exp2(difference * (SCALE * LOG2E))
+
+
+def mine_kernel(
+    q_ref, g_ref, stats_ref, own, near, far2, far3,
+    key_ref, value_ref, exp_ref, dprob_ref, joint_ref, key_tmp, value_tmp,
+):
+    tiles = ((own, 0), (near, 0), (far2, 0), (far3, 0))
+    place_far(tiles, key_ref, value_ref, key_tmp, value_tmp)
 
     def head(columns):
-        q = q_ref[:, columns]
-        g = g_ref[:, columns]
-        scores = dot(key_ref[:, columns], q, 1, 1)
-        dprob = dot(value_ref[:, columns], g, 1, 1)
-        near_top = stats_ref[0:1, columns]
-        top = jnp.maximum(jnp.max(scores, axis=0, keepdims=True), near_top)
-        exponent = jnp.exp2((scores - top) * (SCALE * LOG2E))
-        near_factor = jnp.exp2((near_top - top) * (SCALE * LOG2E))
-        total = near_factor * stats_ref[1:2, columns] + jnp.sum(exponent, axis=0, keepdims=True)
-        moment = near_factor * stats_ref[2:3, columns] + jnp.sum(
+        scores = dot(key_ref[:, columns], q_ref[:, columns], 1, 1)
+        dprob = dot(value_ref[:, columns], g_ref[:, columns], 1, 1)
+        old_top = stats_ref[0:1, columns]
+        top = jnp.maximum(jnp.max(scores, axis=0, keepdims=True), old_top)
+        exponent = power(scores - top)
+        factor = power(old_top - top)
+        exp_ref[:, columns] = exponent
+        dprob_ref[:, columns] = dprob
+        joint_ref[0:1, columns] = top
+        joint_ref[1:2, columns] = factor * stats_ref[1:2, columns] + jnp.sum(
+            exponent, axis=0, keepdims=True
+        )
+        joint_ref[2:3, columns] = factor * stats_ref[2:3, columns] + jnp.sum(
             exponent * dprob, axis=0, keepdims=True
         )
-        inverse = 1.0 / total
-        delta = moment * inverse
-        prob = exponent * inverse
-        weights = prob.astype(BF16)
-        dscore = (prob * (dprob - delta) * SCALE).astype(BF16)
-        joint_ref[0:1, columns] = near_factor * inverse
-        joint_ref[1:2, columns] = delta
-        weight_ref[:, columns] = weights
-        dscore_ref[:, columns] = dscore
-        key_grad = dot(dscore, q, 1, 0)
-        value_grad = dot(weights, g, 1, 0)
-        for core, ref in enumerate((mine_ref, other_ref)):
-            out = 0
-            for number in range(4):
-                pieces = [(96 * core + 24 * number + 8 * tile, 8) for tile in range(3)]
-                if number > 1:
-                    pieces.append((192 + 32 * core + 16 * (number - 2), 16))
-                for start, count in pieces:
-                    both = jnp.concatenate(
-                        [key_grad[start : start + count], value_grad[start : start + count]], axis=0
-                    )
-                    ref[out : out + 2 * count, columns] = both.astype(ref.dtype)
-                    out += 2 * count
+        joint_ref[3:4, columns] = factor
 
     by_head(head)
 
 
-def far_attend(*operands):
-    shape = jax.ShapeDtypeStruct
-    return pl.pallas_call(
-        far_kernel,
+FAR_COST = pl.CostEstimate(
+    flops=4 * FAR * ROWS * D, bytes_accessed=16 * FAR * D, transcendentals=FAR * ROWS * H
+)
+FAR_TMP = [pltpu.VMEM((96, D), F32), pltpu.VMEM((96, D), F32)]
+
+
+def mine_scores(*operands):
+    shape = jax.ShapeDtypeStruct
+    return pl.pallas_call(
+        mine_kernel,
+        out_shape=(
+            shape((FAR, D), BF16),
+            shape((FAR, D), BF16),
+            shape((FAR, D), F32),
+            shape((FAR, D), F32),
+            shape((8, D), F32),
+        ),
+        scratch_shapes=FAR_TMP,
+        compiler_params=PARAMS,
+        cost_estimate=FAR_COST,
+        name="mine_scores",
+    )(*operands)
+
+
+def other_kernel(
+    q_ref, g_ref, joint_ref, early, late,
+    key_ref, value_ref, weight_ref, dscore_ref, final_ref, grad_ref,
+    key_tmp, value_tmp, score_tmp, dprob_tmp,
+):
+    tiles = ((early, 0), (early, 48), (late, 0), (late, 80))
+    place_far(tiles, key_ref, value_ref, key_tmp, value_tmp)
+
+    def scores_of(columns):
+        score_tmp[:, columns] = dot(key_ref[:, columns], q_ref[:, columns], 1, 1)
+        dprob_tmp[:, columns] = dot(value_ref[:, columns], g_ref[:, columns], 1, 1)
+
+    by_head(scores_of)
+    old_top = joint_ref[0:1, :]
+    top = jnp.maximum(jnp.max(score_tmp[...], axis=0, keepdims=True), old_top)
+    factor = power(old_top - top)
+    exponent = power(score_tmp[...] - top)
+    dprob = dprob_tmp[...]
+    total = factor * joint_ref[1:2, :] + jnp.sum(exponent, axis=0, keepdims=True)
+    moment = factor * joint_ref[2:3, :] + jnp.sum(exponent * dprob, axis=0, keepdims=True)
+    inverse = 1.0 / total
+    delta = moment * inverse
+    prob = exponent * inverse
+    weight_ref[...] = prob.astype(BF16)
+    dscore_ref[...] = (prob * (dprob - delta) * SCALE).astype(BF16)
+    mine_factor = factor * inverse
+    final_ref[0:1, :] = mine_factor * joint_ref[3:4, :]
+    final_ref[1:2, :] = mine_factor
+    final_ref[2:3, :] = delta
+
+    def grads_of(columns):
+        key_grad = dot(dscore_ref[:, columns], q_ref[:, columns], 1, 0)
+        value_grad = dot(weight_ref[:, columns], g_ref[:, columns], 1, 0)
+        pack_far(key_grad, value_grad, grad_ref, columns)
+
+    by_head(grads_of)
+
+
+def other_attend(*operands):
+    shape = jax.ShapeDtypeStruct
+    return pl.pallas_call(
+        other_kernel,
         out_shape=(
             shape((FAR, D), BF16),
             shape((FAR, D), BF16),
             shape((FAR, D), BF16),
             shape((FAR, D), BF16),
             shape((8, D), F32),
-            shape((FAR, D), F32),
-            shape((FAR, D), BF16),
-        ),
-        scratch_shapes=[pltpu.VMEM((192, D), F32), pltpu.VMEM((192, D), F32)],
-        compiler_params=PARAMS,
-        cost_estimate=pl.CostEstimate(
-            flops=8 * FAR * ROWS * D, bytes_accessed=8 * FAR * D, transcendentals=FAR * ROWS * H
-        ),
-        name="far_attend",
-    )(*operands)
-
-
-def rest_kernel(
-    q_ref, g_ref, near_key, near_value, exp_ref, dprob_ref,
-    far_key, far_value, weight_ref, dscore_ref, joint_ref,
-    out_ref, grad_q_ref, local_k_ref, local_v_ref, mine_ref, other_ref,
+            shape((2 * FAR, D), BF16),
+        ),
+        scratch_shapes=FAR_TMP + [pltpu.VMEM((FAR, D), F32), pltpu.VMEM((FAR, D), F32)],
+        compiler_params=PARAMS,
+        cost_estimate=FAR_COST,
+        name="other_attend",
+    )(*operands)
+
+
+def soften(exp_ref, dprob_ref, final_ref, row, columns):
+    prob = exp_ref[:, columns] * final_ref[row : row + 1, columns]
+    dscore = prob * (dprob_ref[:, columns] - final_ref[2:3, columns]) * SCALE
+    return prob.astype(BF16), dscore.astype(BF16)
+
+
+def mine_grad_kernel(q_ref, g_ref, exp_ref, dprob_ref, final_ref, weight_ref, dscore_ref, grad_ref):
+    def head(columns):
+        weights, dscore = soften(exp_ref, dprob_ref, final_ref, 1, columns)
+        weight_ref[:, columns] = weights
+        dscore_ref[:, columns] = dscore
+        key_grad = dot(dscore, q_ref[:, columns], 1, 0)
+        pack_far(key_grad, dot(weights, g_ref[:, columns], 1, 0), grad_ref, columns)
+
+    by_head(head)
+
+
+def mine_grads(*operands):
+    shape = jax.ShapeDtypeStruct
+    return pl.pallas_call(
+        mine_grad_kernel,
+        out_shape=(shape((FAR, D), BF16), shape((FAR, D), BF16), shape((2 * FAR, D), F32)),
+        compiler_params=PARAMS,
+        cost_estimate=FAR_COST,
+        name="mine_grads",
+    )(*operands)
+
+
+def near_grad_kernel(
+    q_ref, g_ref, exp_ref, dprob_ref, final_ref,
+    weight_ref, dscore_ref, local_k_ref, local_v_ref, mine_ref, other_ref,
 ):
     def head(columns):
-        prob = exp_ref[:, columns] * joint_ref[0:1, columns]
-        weights = prob.astype(BF16)
-        delta = joint_ref[1:2, columns]
-        dscore = (prob * (dprob_ref[:, columns] - delta) * SCALE).astype(BF16)
-        output = dot(weights, near_value[:, columns], 0, 0)
-        output += dot(weight_ref[:, columns], far_value[:, columns], 0, 0)
-        out_ref[:, columns] = output.astype(BF16)
-        grad_q = dot(dscore, near_key[:, columns], 0, 0)
-        grad_q += dot(dscore_ref[:, columns], far_key[:, columns], 0, 0)
-        grad_q_ref[:, columns] = grad_q.astype(BF16)
+        weights, dscore = soften(exp_ref, dprob_ref, final_ref, 0, columns)
+        weight_ref[:, columns] = weights
+        dscore_ref[:, columns] = dscore
         key_grad = dot(dscore, q_ref[:, columns], 1, 0)
         value_grad = dot(weights, g_ref[:, columns], 1, 0)
         local_k_ref[:, columns] = key_grad[0:128]
@@ -253,13 +346,13 @@
     by_head(head)
 
 
-def rest_attend(*operands):
-    shape = jax.ShapeDtypeStruct
-    return pl.pallas_call(
-        rest_kernel,
+def near_grads(*operands):
+    shape = jax.ShapeDtypeStruct
+    return pl.pallas_call(
+        near_grad_kernel,
         out_shape=(
-            shape((ROWS, D), BF16),
-            shape((ROWS, D), BF16),
+            shape((NEAR, D), BF16),
+            shape((NEAR, D), BF16),
             shape((ROWS, D), F32),
             shape((ROWS, D), F32),
             shape((64, D), F32),
@@ -267,9 +360,36 @@
         ),
         compiler_params=PARAMS,
         cost_estimate=pl.CostEstimate(
-            flops=4 * (2 * NEAR + FAR) * ROWS * D, bytes_accessed=16 * NEAR * D, transcendentals=0
-        ),
-        name="rest_attend",
+            flops=4 * NEAR * ROWS * D, bytes_accessed=16 * NEAR * D, transcendentals=0
+        ),
+        name="near_grads",
+    )(*operands)
+
+
+def output_kernel(*refs):
+    sets, (out_ref, grad_q_ref) = (refs[0:4], refs[4:8], refs[8:12]), refs[12:]
+
+    def head(columns):
+        output = grad_q = 0.0
+        for key, value, weights, dscore in sets:
+            output += dot(weights[:, columns], value[:, columns], 0, 0)
+            grad_q += dot(dscore[:, columns], key[:, columns], 0, 0)
+        out_ref[:, columns] = output.astype(BF16)
+        grad_q_ref[:, columns] = grad_q.astype(BF16)
+
+    by_head(head)
+
+
+def outputs(*operands):
+    shape = jax.ShapeDtypeStruct
+    return pl.pallas_call(
+        output_kernel,
+        out_shape=(shape((ROWS, D), BF16), shape((ROWS, D), BF16)),
+        compiler_params=PARAMS,
+        cost_estimate=pl.CostEstimate(
+            flops=8 * NEAR * ROWS * D, bytes_accessed=16 * NEAR * D, transcendentals=0
+        ),
+        name="outputs",
     )(*operands)
 
 
@@ -294,7 +414,7 @@
 
 def plane_kernel(own_ref, near_ref, far2_ref, far3_ref, keep_ref, send_ref):
     total = (own_ref[...] + near_ref[...].astype(F32)) + (
-        far2_ref[:48, :].astype(F32) + far3_ref[:48, :].astype(F32)
+        far2_ref[...].astype(F32) + far3_ref[:48, :].astype(F32)
     )
     keep_ref[...] = total[:16, :]
     send_ref[...] = total[16:, :].astype(BF16)
@@ -310,7 +430,7 @@
 
 
 def finish_kernel(
-    local_k_ref, local_v_ref, c1_ref, c2_ref, far2_ref, far3_ref, z1_ref, z2_ref, z7_ref,
+    local_k_ref, local_v_ref, c1_ref, c2_ref, c3_ref, far3_ref, z1_ref, z2_ref, z7_ref,
     grad_k_ref, grad_v_ref, tmp, pick,
 ):
     for number, ref in enumerate((z1_ref, z2_ref, z7_ref)):
@@ -334,7 +454,7 @@
                 6: part(32, 2) + part(34, 2),
                 5: part(20, 4),
                 4: part(0, 8),
-                3: rows(far2_ref, 48, 16) + rows(far3_ref, 48, 16),
+                3: rows(c3_ref, 0, 16) + rows(far3_ref, 48, 16),
                 2: rows(c2_ref, 0, 32),
                 1: rows(c1_ref, 0, 64),
                 0: local_ref[:, columns],
@@ -388,31 +508,48 @@
     near_key, near_value, exponent, dprob, stats = near_scores(
         queries, keys, values, cotangent, c1, c2, core
     )
-    near, far2, far3, stats = together(near, far2, far3, stats)
-    tiles = [own, near, far2, far3]
-    tiles += [swap(part, 1) for part in tiles]
-    far_key, far_value, weights, dscore, joint, mine, other = far_attend(
-        queries, cotangent, stats, *tiles
+    early = swap(jnp.concatenate([own, near]), 1)
+    far3, stats = together(far3, stats)
+    late = swap(jnp.concatenate([far2, far3]), 1)
+    mine_key, mine_value, mine_exponent, mine_dprob, joint = mine_scores(
+        queries, cotangent, stats, own, near, far2, far3
+    )
+    joint, *core = together(joint, early, late)
+    other_key, other_value, other_weights, other_dscore, final, other = other_attend(
+        queries, cotangent, joint, *core
     )
     got = swap(other, 1)
-    own, near, far2, far3 = chip_sum(mine, got, ((48, F32), (48, BF16), (80, BF16), (80, BF16)))
-    joint, near, far2, far3 = together(joint, near, far2, far3)
+    mine_weights, mine_dscore, mine = mine_grads(
+        queries, cotangent, mine_exponent, mine_dprob, final
+    )
+    got, mine = together(got, mine)
+    own, near, far2, c3a, far3 = chip_sum(
+        mine, got, ((48, F32), (48, BF16), (48, BF16), (32, BF16), (80, BF16))
+    )
+    final, near, far2, far3 = together(final, near, far2, far3)
     near, far3, far2 = swap(near, 2), swap(far3, 6), swap(far2, 4)
-    output, grad_queries, local_k, local_v, mine, other = rest_attend(
-        queries, cotangent, near_key, near_value, exponent, dprob,
-        far_key, far_value, weights, dscore, joint,
-    )
-    near, far2, far3, other = together(near, far2, far3, other)
+    near_weights, near_dscore, local_k, local_v, mine, other = near_grads(
+        queries, cotangent, exponent, dprob, final
+    )
+    near, far3, far2, other = together(near, far3, far2, other)
     keep, send = plane_sum(own, near, far2, far3)
+    send, near_weights, c3a = together(send, near_weights, c3a)
     got = swap(send, 8)
+    output, grad_queries = outputs(
+        near_key, near_value, near_weights, near_dscore,
+        mine_key, mine_value, mine_weights, mine_dscore,
+        other_key, other_value, other_weights, other_dscore,
+    )
+    got, output = together(got, output)
     core = swap(other, 1)
     (c2,) = chip_sum(mine, core, ((64, BF16),))
     c2 = swap(c2, 2)
+    c3a = swap(c3a, 4)
     keep = (keep + got[:16].astype(F32)).astype(BF16)
     two = swap(keep, 16)
     six = swap(jnp.where(rows_at(2, 2), keep, two), 56)
     grad_keys, grad_values = finish(
-        local_k, local_v, core[:128], c2, far2, far3, got[16:], two, six
+        local_k, local_v, core[:128], c2, c3a, far3, got[16:], two, six
     )
     return output, grad_queries, grad_keys, grad_values
 

time: 65.2 us -> 61.8 us (0.948)
  starting transfers between devices: 25.4 us -> 29 us
  waiting for transfers between devices: 27.2 us -> 24.1 us
  Pallas kernels: 9.49 us -> 7.43 us
  local copies, waits for them, and re-layouts: 1.99 us -> 0.04 us
    ppermute x22 -> x21, starting transfers between devices: 25.4 us -> 29 us  [swap(): return lax.ppermute(block, 'ctx', [(i, i ^ mask) for i in range(count)])]
    ppermute x22 -> x21, waiting for transfers between devices: 27.2 us -> 24.1 us  [swap(): return lax.ppermute(block, 'ctx', [(i, i ^ mask) for i in range(count)])]
    pallas_call x2 -> x5, Pallas kernels: 6.1 us -> 3.98 us  [the longest x1 1.68 us: outputs(): pl.pallas_call(output_kernel, out_shape=(shape((ROWS, D), BF16), shape((R...]
    unnamed x5 -> x1, local copies, waits for them, and re-layouts: 1.96 us -> 0.01 us
  transfers between devices with their start and end apart: 22 -> 21, of which waited for: 13 -> 13; matrix products, arithmetic and copies ran while one was open for 0% -> 1% of each run, Pallas kernels for 7% -> 6%
where the time goes in v2:
time: 61.8 us; the launch traced here: 61.7 us
  starting transfers between devices  29 us (47%)
  waiting for transfers between devices  24.1 us (39%)
  Pallas kernels  7.43 us (12%)
  between operations  0.79 us (1%)
    ppermute x21, starting transfers between devices, swap(): return lax.ppermute(block, 'ctx', [(i, i ^ mask) for i in range(count)])  29 us
    ppermute x21, waiting for transfers between devices, swap(): return lax.ppermute(block, 'ctx', [(i, i ^ mask) for i in range(count)])  24.1 us
    pallas_call x1, Pallas kernels, outputs(): pl.pallas_call(output_kernel, out_shape=(shape((ROWS, D), BF16), shape((R...  1.68 us
    pallas_call x1, Pallas kernels, coarsen(): pl.pallas_call(coarsen_kernel, out_shape=tuple((jax.ShapeDtypeStruct((cou...  1.47 us
  transfers between devices with their start and end apart: 21, of which 13 were waited for; matrix products, arithmetic and copies ran while one was open for 1% of the time, Pallas kernels for 6%

profile of v2, /device:TPU:36, one launch (start us, length us, event | category | flops | bytes accessed | tf_op | source)
XLA Modules:
  0.0 61.7 jit_solution(8250851496994656951)
XLA Ops:
  0.6 1.5 %coarsen.1 = (bf16[128,1024]{1,0:T(8,128)(2,1)S(1)}, bf16[64,1024]{1,0:T(8,128)(2,1)S(1)}, bf16[32,1024]{1,0:T(8,128)(2,1)S(1)}, bf16[16,1024]{1,0:T(8,128)(2,1)...) custom-call(bf16[128,1024]{1,0:T(8,128)(2,1)} %k_hbm.1, ...), custom_call_target="tpu_custom_call" | custom-call | tf_op jit(solution)/shard_map/coarsen/pallas_call | solution.py:76
  2.1 5.9 %collective-permute-start = (bf16[16,1024]{1,0:T(8,128)(2,1)S(1)}, bf16[16,1024]{1,0:T(8,128)(2,1)S(1)}, u32[]{:S(2)}, u32[]{:S(2)}) collective-permute-start(bf16[16,1024]{1,0:T(8,128)(2,1)S(1)} %get-tuple-element.78), channel_id=1, source_target_pairs={{0,224},{4,228},{8,232},{12,236},{16,240},{20,244},{24,248},{28,25... | collective-permute-start | bytes 98312 | tf_op jit(solution)/shard_map/ppermute | solution.py:23
  8.0 1.6 %collective-permute-start.2 = (bf16[64,1024]{1,0:T(8,128)(2,1)S(1)}, bf16[64,1024]{1,0:T(8,128)(2,1)S(1)}, u32[]{:S(2)}, u32[]{:S(2)}) collective-permute-start(bf16[64,1024]{1,0:T(8,128)(2,1)S(1)} %get-tuple-element.81), channel_id=1, source_target_pairs={{0,8},{4,12},{8,0},{12,4},{16,24},{20,28},{24,16},{28,20},{32,40},... | collective-permute-start | bytes 393224 | tf_op jit(solution)/shard_map/ppermute | solution.py:23
  10.7 4.2 %collective-permute-done.1 = bf16[16,1024]{1,0:T(8,128)(2,1)S(1)} collective-permute-done((bf16[16,1024]{1,0:T(8,128)(2,1)S(1)}, bf16[16,1024]{1,0:T(8,128)(2,1)S(1)}, u32[]{:S(2)}, u32[]{:S(2)}) %collective-permute-start.1) | collective-permute-done | bytes 32800 | tf_op jit(solution)/shard_map/ppermute | solution.py:23
  15.2 4.1 %collective-permute-done.3 = bf16[32,1024]{1,0:T(8,128)(2,1)S(1)} collective-permute-done((bf16[32,1024]{1,0:T(8,128)(2,1)S(1)}, bf16[32,1024]{1,0:T(8,128)(2,1)S(1)}, u32[]{:S(2)}, u32[]{:S(2)}) %collective-permute-start.3) | collective-permute-done | bytes 65568 | tf_op jit(solution)/shard_map/ppermute | solution.py:23
  19.4 3.1 %collective-permute-start.6 = (bf16[80,1024]{1,0:T(8,128)(2,1)S(1)}, bf16[80,1024]{1,0:T(8,128)(2,1)S(1)}, u32[]{:S(2)}, u32[]{:S(2)}) collective-permute-start(bf16[80,1024]{1,0:T(8,128)(2,1)S(1)} %constant_dynamic-update-slice_fusion), channel_id=1, source_target_pairs={{0,24},{4,28},{8,16},{12,20},{16,8},{20,12},{24,0},{28,4},{32,56},... | collective-permute-start | bytes 491528 | tf_op jit(solution)/shard_map/ppermute | solution.py:23
  24.2 3.0 %collective-permute-done.6.far3 = bf16[80,1024]{1,0:T(8,128)(2,1)S(1)} collective-permute-done((bf16[80,1024]{1,0:T(8,128)(2,1)S(1)}, bf16[80,1024]{1,0:T(8,128)(2,1)S(1)}, u32[]{:S(2)}, u32[]{:S(2)}) %collective-permute-start.6) | collective-permute-done | bytes 163872 | tf_op jit(solution)/shard_map/ppermute | solution.py:23
  27.2 2.1 %collective-permute-done.8.far2 = bf16[80,1024]{1,0:T(8,128)(2,1)S(1)} collective-permute-done((bf16[80,1024]{1,0:T(8,128)(2,1)S(1)}, bf16[80,1024]{1,0:T(8,128)(2,1)S(1)}, u32[]{:S(2)}, u32[]{:S(2)}) %collective-permute-start.8) | collective-permute-done | bytes 163872 | tf_op jit(solution)/shard_map/ppermute | solution.py:23
  30.6 0.8 %collective-permute-done.9.early = bf16[96,1024]{1,0:T(8,128)(2,1)S(1)} collective-permute-done((bf16[96,1024]{1,0:T(8,128)(2,1)S(1)}, bf16[96,1024]{1,0:T(8,128)(2,1)S(1)}, u32[]{:S(2)}, u32[]{:S(2)}) %collective-permute-start.9) | collective-permute-done | bytes 196640 | tf_op jit(solution)/shard_map/ppermute | solution.py:23
  31.3 0.9 %other_attend.1 = (bf16[128,1024]{1,0:T(8,128)(2,1)S(1)}, bf16[128,1024]{1,0:T(8,128)(2,1)S(1)}, bf16[128,1024]{1,0:T(8,128)(2,1)S(1)}, bf16[128,1024]{1,0:T(8,1...) custom-call(bf16[128,1024]{1,0:T(8,128)(2,1)S(1)} %get-tuple-element.76.q_ref, ...), custom_call_target="tpu_custom_call" | custom-call | flops 67108864 | bytes 2097152 | tf_op jit(solution)/shard_map/other_attend/pallas_call | solution.py:283
  32.8 1.4 %collective-permute-done.11.got_ref = bf16[256,1024]{1,0:T(8,128)(2,1)S(1)} collective-permute-done((bf16[256,1024]{1,0:T(8,128)(2,1)S(1)}, bf16[256,1024]{1,0:T(8,128)(2,1)S(1)}, u32[]{:S(2)}, u32[]{:S(2)}) %collective-permute-start.11) | collective-permute-done | bytes 524320 | tf_op jit(solution)/shard_map/ppermute | solution.py:23
  34.3 1.6 %collective-permute-start.13 = (bf16[80,1024]{1,0:T(8,128)(2,1)S(1)}, bf16[80,1024]{1,0:T(8,128)(2,1)S(1)}, u32[]{:S(2)}, u32[]{:S(2)}) collective-permute-start(bf16[80,1024]{1,0:T(8,128)(2,1)S(1)} %get-tuple-element.111), channel_id=1, source_target_pairs={{0,24},{4,28},{8,16},{12,20},{16,8},{20,12},{24,0},{28,4},{32,56},... | collective-permute-start | bytes 491528 | tf_op jit(solution)/shard_map/ppermute | solution.py:23
  35.8 3.2 %collective-permute-start.14 = (bf16[48,1024]{1,0:T(8,128)(2,1)S(1)}, bf16[48,1024]{1,0:T(8,128)(2,1)S(1)}, u32[]{:S(2)}, u32[]{:S(2)}) collective-permute-start(bf16[48,1024]{1,0:T(8,128)(2,1)S(1)} %get-tuple-element.112), channel_id=1, source_target_pairs={{0,16},{4,20},{8,24},{12,28},{16,0},{20,4},{24,8},{28,12},{32,48},... | collective-permute-start | bytes 294920 | tf_op jit(solution)/shard_map/ppermute | solution.py:23
  39.6 1.8 %collective-permute-done.12.near_ref = bf16[48,1024]{1,0:T(8,128)(2,1)S(1)} collective-permute-done((bf16[48,1024]{1,0:T(8,128)(2,1)S(1)}, bf16[48,1024]{1,0:T(8,128)(2,1)S(1)}, u32[]{:S(2)}, u32[]{:S(2)}) %collective-permute-start.12) | collective-permute-done | bytes 98336 | tf_op jit(solution)/shard_map/ppermute | solution.py:23
  41.5 2.3 %collective-permute-done.14.far2_ref = bf16[48,1024]{1,0:T(8,128)(2,1)S(1)} collective-permute-done((bf16[48,1024]{1,0:T(8,128)(2,1)S(1)}, bf16[48,1024]{1,0:T(8,128)(2,1)S(1)}, u32[]{:S(2)}, u32[]{:S(2)}) %collective-permute-start.14) | collective-permute-done | bytes 98336 | tf_op jit(solution)/shard_map/ppermute | solution.py:23
  44.0 0.9 %collective-permute-start.15 = (bf16[32,1024]{1,0:T(8,128)(2,1)S(1)}, bf16[32,1024]{1,0:T(8,128)(2,1)S(1)}, u32[]{:S(2)}, u32[]{:S(2)}) collective-permute-start(bf16[32,1024]{1,0:T(8,128)(2,1)S(1)} %get-tuple-element.123), channel_id=1, source_target_pairs={{0,32},{4,36},{8,40},{12,44},{16,48},{20,52},{24,56},{28,60},{32,0... | collective-permute-start | bytes 196616 | tf_op jit(solution)/shard_map/ppermute | solution.py:23
  44.9 1.7 %outputs.1 = (bf16[128,1024]{1,0:T(8,128)(2,1)}, bf16[128,1024]{1,0:T(8,128)(2,1)}) custom-call(bf16[256,1024]{1,0:T(8,128)(2,1)S(1)} %get-tuple-element.124.refs_0_, bf16[256,1024]{1,0:T(8,128)(2,1)S(1)} %get-tuple-element.125.refs_1_, bf16[256,1024]{1,0:T(8,128)(2,1)S(1)} %get-tuple-element.126.refs_2_, bf16[256,1024]{1,0:T(8,128)(2,1)S(1)} %get-tuple-element.127.refs_3_, ...), custom_call_target="tpu_custom_call" | custom-call | flops 268435456 | bytes 4194304 | tf_op jit(solution)/shard_map/outputs/pallas_call | solution.py:385
  46.6 2.0 %collective-permute-done.15 = bf16[32,1024]{1,0:T(8,128)(2,1)S(1)} collective-permute-done((bf16[32,1024]{1,0:T(8,128)(2,1)S(1)}, bf16[32,1024]{1,0:T(8,128)(2,1)S(1)}, u32[]{:S(2)}, u32[]{:S(2)}) %collective-permute-start.15) | collective-permute-done | bytes 65568 | tf_op jit(solution)/shard_map/ppermute | solution.py:23
  48.6 1.4 %collective-permute-start.19 = (bf16[16,1024]{1,0:T(8,128)(2,1)S(1)}, bf16[16,1024]{1,0:T(8,128)(2,1)S(1)}, u32[]{:S(2)}, u32[]{:S(2)}) collective-permute-start(bf16[16,1024]{1,0:T(8,128)(2,1)S(1)} %add_convert_fusion), channel_id=1, source_target_pairs={{0,64},{4,68},{8,72},{12,76},{16,80},{20,84},{24,88},{28,92},{32,9... | collective-permute-start | bytes 98312 | tf_op jit(solution)/shard_map/ppermute | solution.py:23
  50.1 1.3 %collective-permute-start.18 = (bf16[32,1024]{1,0:T(8,128)(2,1)S(1)}, bf16[32,1024]{1,0:T(8,128)(2,1)S(1)}, u32[]{:S(2)}, u32[]{:S(2)}) collective-permute-start(bf16[32,1024]{1,0:T(8,128)(2,1)S(1)} %get-tuple-element.143), channel_id=1, source_target_pairs={{0,16},{4,20},{8,24},{12,28},{16,0},{20,4},{24,8},{28,12},{32,48},... | collective-permute-start | bytes 196616 | tf_op jit(solution)/shard_map/ppermute | solution.py:23
  51.4 2.0 %collective-permute-start.17 = (bf16[64,1024]{1,0:T(8,128)(2,1)S(1)}, bf16[64,1024]{1,0:T(8,128)(2,1)S(1)}, u32[]{:S(2)}, u32[]{:S(2)}) collective-permute-start(bf16[64,1024]{1,0:T(8,128)(2,1)S(1)} %chip_sum.3), channel_id=1, source_target_pairs={{0,8},{4,12},{8,0},{12,4},{16,24},{20,28},{24,16},{28,20},{32,40},... | collective-permute-start | bytes 393224 | tf_op jit(solution)/shard_map/ppermute | solution.py:23
  53.6 5.1 %collective-permute-start.20 = (bf16[16,1024]{1,0:T(8,128)(2,1)S(1)}, bf16[16,1024]{1,0:T(8,128)(2,1)S(1)}, u32[]{:S(2)}, u32[]{:S(2)}) collective-permute-start(bf16[16,1024]{1,0:T(8,128)(2,1)S(1)} %broadcast_select_fusion.1), channel_id=1, source_target_pairs={{0,224},{4,228},{8,232},{12,236},{16,240},{20,244},{24,248},{28,25... | collective-permute-start | bytes 98312 | tf_op jit(solution)/shard_map/ppermute | solution.py:23
  58.7 1.9 %collective-permute-done.20.z7_ref = bf16[16,1024]{1,0:T(8,128)(2,1)S(1)} collective-permute-done((bf16[16,1024]{1,0:T(8,128)(2,1)S(1)}, bf16[16,1024]{1,0:T(8,128)(2,1)S(1)}, u32[]{:S(2)}, u32[]{:S(2)}) %collective-permute-start.20) | collective-permute-done | bytes 32800 | tf_op jit(solution)/shard_map/ppermute | solution.py:23
  60.5 1.1 %finish.1 = (bf16[128,1024]{1,0:T(8,128)(2,1)}, bf16[128,1024]{1,0:T(8,128)(2,1)}) custom-call(f32[128,1024]{1,0:T(8,128)S(1)} %get-tuple-element.139.local_k_ref, f32[128,1024]{1,0:T(8,128)S(1)} %get-tuple-element.140.local_v_ref, bf16[128,1024]{1,0:T(8,128)(2,1)S(1)} %slice.12.c1_ref, bf16[64,1024]{1,0:T(8,128)(2,1)S(1)} %collective-permute-done.17.c2_ref, ...), custom_call_target="tpu_custom_call" | custom-call | tf_op jit(solution)/shard_map/finish/pallas_call | solution.py:474
  (43 shorter events, 6.1 us)
Async XLA Ops:
  2.1 7.8 %collective-permute-start = (bf16[16,1024]{1,0:T(8,128)(2,1)S(1)}, bf16[16,1024]{1,0:T(8,128)(2,1)S(1)}, u32[]{:S(2)}, u32[]{:S(2)}) collective-permute-start(bf16[16,1024]{1,0:T(8,128)(2,1)S(1)} %get-tuple-element.78), channel_id=1, source_target_pairs={{0,224},{4,228},{8,232},{12,236},{16,240},{20,244},{24,248},{28,25... | collective-permute-start | bytes 98312 | tf_op jit(solution)/shard_map/ppermute | solution.py:23
  8.0 6.9 %collective-permute-start.2 = (bf16[64,1024]{1,0:T(8,128)(2,1)S(1)}, bf16[64,1024]{1,0:T(8,128)(2,1)S(1)}, u32[]{:S(2)}, u32[]{:S(2)}) collective-permute-start(bf16[64,1024]{1,0:T(8,128)(2,1)S(1)} %get-tuple-element.81), channel_id=1, source_target_pairs={{0,8},{4,12},{8,0},{12,4},{16,24},{20,28},{24,16},{28,20},{32,40},... | collective-permute-start | bytes 393224 | tf_op jit(solution)/shard_map/ppermute | solution.py:23
  9.6 9.7 %collective-permute-start.4 = (bf16[128,1024]{1,0:T(8,128)(2,1)S(1)}, bf16[128,1024]{1,0:T(8,128)(2,1)S(1)}, u32[]{:S(2)}, u32[]{:S(2)}) collective-permute-start(bf16[128,1024]{1,0:T(8,128)(2,1)S(1)} %get-tuple-element.83), channel_id=1, source_target_pairs={{0,4},{4,0},{8,12},{12,8},{16,20},{20,16},{24,28},{28,24},{32,36},... | collective-permute-start | bytes 786440 | tf_op jit(solution)/shard_map/ppermute | solution.py:23
  10.0 4.8 %collective-permute-start.1 = (bf16[16,1024]{1,0:T(8,128)(2,1)S(1)}, bf16[16,1024]{1,0:T(8,128)(2,1)S(1)}, u32[]{:S(2)}, u32[]{:S(2)}) collective-permute-start(bf16[16,1024]{1,0:T(8,128)(2,1)S(1)} %broadcast_select_fusion), channel_id=1, source_target_pairs={{0,64},{4,68},{8,72},{12,76},{16,80},{20,84},{24,88},{28,92},{32,9... | collective-permute-start | bytes 98312 | tf_op jit(solution)/shard_map/ppermute | solution.py:23
  14.9 4.4 %collective-permute-start.3 = (bf16[32,1024]{1,0:T(8,128)(2,1)S(1)}, bf16[32,1024]{1,0:T(8,128)(2,1)S(1)}, u32[]{:S(2)}, u32[]{:S(2)}) collective-permute-start(bf16[32,1024]{1,0:T(8,128)(2,1)S(1)} %pad_maximum_fusion.3), channel_id=1, source_target_pairs={{0,32},{4,36},{8,40},{12,44},{16,48},{20,52},{24,56},{28,60},{32,0... | collective-permute-start | bytes 196616 | tf_op jit(solution)/shard_map/ppermute | solution.py:23
  15.2 4.2 %collective-permute-start.5 = (bf16[64,1024]{1,0:T(8,128)(2,1)S(1)}, bf16[64,1024]{1,0:T(8,128)(2,1)S(1)}, u32[]{:S(2)}, u32[]{:S(2)}) collective-permute-start(bf16[64,1024]{1,0:T(8,128)(2,1)S(1)} %collective-permute-done.2.rest_1_), channel_id=1, source_target_pairs={{0,4},{4,0},{8,12},{12,8},{16,20},{20,16},{24,28},{28,24},{32,36},... | collective-permute-start | bytes 393224 | tf_op jit(solution)/shard_map/ppermute | solution.py:23
  19.4 7.8 %collective-permute-start.6 = (bf16[80,1024]{1,0:T(8,128)(2,1)S(1)}, bf16[80,1024]{1,0:T(8,128)(2,1)S(1)}, u32[]{:S(2)}, u32[]{:S(2)}) collective-permute-start(bf16[80,1024]{1,0:T(8,128)(2,1)S(1)} %constant_dynamic-update-slice_fusion), channel_id=1, source_target_pairs={{0,24},{4,28},{8,16},{12,20},{16,8},{20,12},{24,0},{28,4},{32,56},... | collective-permute-start | bytes 491528 | tf_op jit(solution)/shard_map/ppermute | solution.py:23
  22.5 6.8 %collective-permute-start.8 = (bf16[80,1024]{1,0:T(8,128)(2,1)S(1)}, bf16[80,1024]{1,0:T(8,128)(2,1)S(1)}, u32[]{:S(2)}, u32[]{:S(2)}) collective-permute-start(bf16[80,1024]{1,0:T(8,128)(2,1)S(1)} %constant_dynamic-update-slice_fusion), channel_id=1, source_target_pairs={{0,16},{4,20},{8,24},{12,28},{16,0},{20,4},{24,8},{28,12},{32,48},... | collective-permute-start | bytes 491528 | tf_op jit(solution)/shard_map/ppermute | solution.py:23
  23.1 6.3 %collective-permute-start.7 = (bf16[48,1024]{1,0:T(8,128)(2,1)S(1)}, bf16[48,1024]{1,0:T(8,128)(2,1)S(1)}, u32[]{:S(2)}, u32[]{:S(2)}) collective-permute-start(bf16[48,1024]{1,0:T(8,128)(2,1)S(1)} %pad_maximum_fusion.2.own), channel_id=1, source_target_pairs={{0,8},{4,12},{8,0},{12,4},{16,24},{20,28},{24,16},{28,20},{32,40},... | collective-permute-start | bytes 294920 | tf_op jit(solution)/shard_map/ppermute | solution.py:23
  29.3 2.0 %collective-permute-start.10 = (bf16[160,1024]{1,0:T(8,128)(2,1)S(1)}, bf16[160,1024]{1,0:T(8,128)(2,1)S(1)}, u32[]{:S(2)}, u32[]{:S(2)}) collective-permute-start(bf16[160,1024]{1,0:T(8,128)(2,1)S(1)} %pad_maximum_fusion), channel_id=1, source_target_pairs={{0,4},{4,0},{8,12},{12,8},{16,20},{20,16},{24,28},{28,24},{32,36},... | collective-permute-start | bytes 983048 | tf_op jit(solution)/shard_map/ppermute | solution.py:23
  29.4 1.9 %collective-permute-start.9 = (bf16[96,1024]{1,0:T(8,128)(2,1)S(1)}, bf16[96,1024]{1,0:T(8,128)(2,1)S(1)}, u32[]{:S(2)}, u32[]{:S(2)}) collective-permute-start(bf16[96,1024]{1,0:T(8,128)(2,1)S(1)} %pad_maximum_fusion.1), channel_id=1, source_target_pairs={{0,4},{4,0},{8,12},{12,8},{16,20},{20,16},{24,28},{28,24},{32,36},... | collective-permute-start | bytes 589832 | tf_op jit(solution)/shard_map/ppermute | solution.py:23
  32.2 2.0 %collective-permute-start.11 = (bf16[256,1024]{1,0:T(8,128)(2,1)S(1)}, bf16[256,1024]{1,0:T(8,128)(2,1)S(1)}, u32[]{:S(2)}, u32[]{:S(2)}) collective-permute-start(bf16[256,1024]{1,0:T(8,128)(2,1)S(1)} %get-tuple-element.99), channel_id=1, source_target_pairs={{0,4},{4,0},{8,12},{12,8},{16,20},{20,16},{24,28},{28,24},{32,36},... | collective-permute-start | bytes 1572872 | tf_op jit(solution)/shard_map/ppermute | solution.py:23
  34.3 9.7 %collective-permute-start.13 = (bf16[80,1024]{1,0:T(8,128)(2,1)S(1)}, bf16[80,1024]{1,0:T(8,128)(2,1)S(1)}, u32[]{:S(2)}, u32[]{:S(2)}) collective-permute-start(bf16[80,1024]{1,0:T(8,128)(2,1)S(1)} %get-tuple-element.111), channel_id=1, source_target_pairs={{0,24},{4,28},{8,16},{12,20},{16,8},{20,12},{24,0},{28,4},{32,56},... | collective-permute-start | bytes 491528 | tf_op jit(solution)/shard_map/ppermute | solution.py:23
  35.8 5.6 %collective-permute-start.12 = (bf16[48,1024]{1,0:T(8,128)(2,1)S(1)}, bf16[48,1024]{1,0:T(8,128)(2,1)S(1)}, u32[]{:S(2)}, u32[]{:S(2)}) collective-permute-start(bf16[48,1024]{1,0:T(8,128)(2,1)S(1)} %get-tuple-element.110), channel_id=1, source_target_pairs={{0,8},{4,12},{8,0},{12,4},{16,24},{20,28},{24,16},{28,20},{32,40},... | collective-permute-start | bytes 294920 | tf_op jit(solution)/shard_map/ppermute | solution.py:23
  35.8 7.9 %collective-permute-start.14 = (bf16[48,1024]{1,0:T(8,128)(2,1)S(1)}, bf16[48,1024]{1,0:T(8,128)(2,1)S(1)}, u32[]{:S(2)}, u32[]{:S(2)}) collective-permute-start(bf16[48,1024]{1,0:T(8,128)(2,1)S(1)} %get-tuple-element.112), channel_id=1, source_target_pairs={{0,16},{4,20},{8,24},{12,28},{16,0},{20,4},{24,8},{28,12},{32,48},... | collective-permute-start | bytes 294920 | tf_op jit(solution)/shard_map/ppermute | solution.py:23
  43.9 7.4 %collective-permute-start.16 = (bf16[192,1024]{1,0:T(8,128)(2,1)S(1)}, bf16[192,1024]{1,0:T(8,128)(2,1)S(1)}, u32[]{:S(2)}, u32[]{:S(2)}) collective-permute-start(bf16[192,1024]{1,0:T(8,128)(2,1)S(1)} %get-tuple-element.141), channel_id=1, source_target_pairs={{0,4},{4,0},{8,12},{12,8},{16,20},{20,16},{24,28},{28,24},{32,36},... | collective-permute-start | bytes 1179656 | tf_op jit(solution)/shard_map/ppermute | solution.py:23
  44.0 4.6 %collective-permute-start.15 = (bf16[32,1024]{1,0:T(8,128)(2,1)S(1)}, bf16[32,1024]{1,0:T(8,128)(2,1)S(1)}, u32[]{:S(2)}, u32[]{:S(2)}) collective-permute-start(bf16[32,1024]{1,0:T(8,128)(2,1)S(1)} %get-tuple-element.123), channel_id=1, source_target_pairs={{0,32},{4,36},{8,40},{12,44},{16,48},{20,52},{24,56},{28,60},{32,0... | collective-permute-start | bytes 196616 | tf_op jit(solution)/shard_map/ppermute | solution.py:23
  48.6 4.9 %collective-permute-start.19 = (bf16[16,1024]{1,0:T(8,128)(2,1)S(1)}, bf16[16,1024]{1,0:T(8,128)(2,1)S(1)}, u32[]{:S(2)}, u32[]{:S(2)}) collective-permute-start(bf16[16,1024]{1,0:T(8,128)(2,1)S(1)} %add_convert_fusion), channel_id=1, source_target_pairs={{0,64},{4,68},{8,72},{12,76},{16,80},{20,84},{24,88},{28,92},{32,9... | collective-permute-start | bytes 98312 | tf_op jit(solution)/shard_map/ppermute | solution.py:23
  50.1 8.6 %collective-permute-start.18 = (bf16[32,1024]{1,0:T(8,128)(2,1)S(1)}, bf16[32,1024]{1,0:T(8,128)(2,1)S(1)}, u32[]{:S(2)}, u32[]{:S(2)}) collective-permute-start(bf16[32,1024]{1,0:T(8,128)(2,1)S(1)} %get-tuple-element.143), channel_id=1, source_target_pairs={{0,16},{4,20},{8,24},{12,28},{16,0},{20,4},{24,8},{28,12},{32,48},... | collective-permute-start | bytes 196616 | tf_op jit(solution)/shard_map/ppermute | solution.py:23
  51.4 9.1 %collective-permute-start.17 = (bf16[64,1024]{1,0:T(8,128)(2,1)S(1)}, bf16[64,1024]{1,0:T(8,128)(2,1)S(1)}, u32[]{:S(2)}, u32[]{:S(2)}) collective-permute-start(bf16[64,1024]{1,0:T(8,128)(2,1)S(1)} %chip_sum.3), channel_id=1, source_target_pairs={{0,8},{4,12},{8,0},{12,4},{16,24},{20,28},{24,16},{28,20},{32,40},... | collective-permute-start | bytes 393224 | tf_op jit(solution)/shard_map/ppermute | solution.py:23
  53.6 6.9 %collective-permute-start.20 = (bf16[16,1024]{1,0:T(8,128)(2,1)S(1)}, bf16[16,1024]{1,0:T(8,128)(2,1)S(1)}, u32[]{:S(2)}, u32[]{:S(2)}) collective-permute-start(bf16[16,1024]{1,0:T(8,128)(2,1)S(1)} %broadcast_select_fusion.1), channel_id=1, source_target_pairs={{0,224},{4,228},{8,232},{12,236},{16,240},{20,244},{24,248},{28,25... | collective-permute-start | bytes 98312 | tf_op jit(solution)/shard_map/ppermute | solution.py:23

commit v3 on v2

--- a/solution.py
+++ b/solution.py
@@ -429,12 +429,12 @@
     )(own, near, far2, far3)
 
 
-def finish_kernel(
-    local_k_ref, local_v_ref, c1_ref, c2_ref, c3_ref, far3_ref, z1_ref, z2_ref, z7_ref,
+def gather_kernel(
+    local_k_ref, local_v_ref, c1_ref, c2_ref, c3_ref, far3_ref, z1_ref, z2_ref,
     grad_k_ref, grad_v_ref, tmp, pick,
 ):
-    for number, ref in enumerate((z1_ref, z2_ref, z7_ref)):
-        pick[16 * number : 16 * number + 16, :] = ref[:16, :].astype(F32)
+    for number, ref in enumerate((z1_ref, z2_ref)):
+        pick[16 * number : 16 * number + 16, :] = ref[...].astype(F32)
     for side, (local_ref, out_ref) in enumerate(
         ((local_k_ref, grad_k_ref), (local_v_ref, grad_v_ref))
     ):
@@ -442,31 +442,50 @@
             columns = slice(number * DH, number * DH + DH)
             plane = tmp.at[side * H + number]
 
-            def part(start, count, side=side, columns=columns):
-                start += 8 * side
-                return pick[start : start + count, columns]
-
             def rows(ref, start, count, side=side, columns=columns):
                 start += side * count
                 return ref[start : start + count, columns].astype(F32)
 
             parts = {
-                6: part(32, 2) + part(34, 2),
-                5: part(20, 4),
-                4: part(0, 8),
+                5: pick[20 + 8 * side : 24 + 8 * side, columns],
+                4: rows(pick, 0, 8),
                 3: rows(c3_ref, 0, 16) + rows(far3_ref, 48, 16),
                 2: rows(c2_ref, 0, 32),
                 1: rows(c1_ref, 0, 64),
                 0: local_ref[:, columns],
             }
-            total = parts[6]
-            for level in range(5, -1, -1):
+            total = parts[5]
+            for level in range(4, -1, -1):
                 count = ROWS >> level
                 half = total * HALF_ROOT
                 plane[pl.ds(0, count // 2, stride=2), :] = half
                 plane[pl.ds(1, count // 2, stride=2), :] = half
                 total = plane[:count, :] + parts[level]
-            out_ref[:, columns] = total.astype(BF16)
+            out_ref[:, columns] = total
+
+
+def gather(*operands):
+    shape = jax.ShapeDtypeStruct
+    return pl.pallas_call(
+        gather_kernel,
+        out_shape=(shape((ROWS, D), F32), shape((ROWS, D), F32)),
+        scratch_shapes=[pltpu.VMEM((2 * H, ROWS, DH), F32), pltpu.VMEM((32, D), F32)],
+        compiler_params=PARAMS,
+        cost_estimate=FAR_COST,
+        name="gather",
+    )(*operands)
+
+
+def finish_kernel(part_k_ref, part_v_ref, z7_ref, grad_k_ref, grad_v_ref):
+    top = z7_ref[...].astype(F32)
+    for side, (part_ref, out_ref) in enumerate(
+        ((part_k_ref, grad_k_ref), (part_v_ref, grad_v_ref))
+    ):
+        for row in range(2):
+            first = 8 * side + row
+            both = top[first : first + 1] + top[first + 2 : first + 3]
+            rows = slice(64 * row, 64 * row + 64)
+            out_ref[rows, :] = (part_ref[rows, :] + both * 0.125).astype(BF16)
 
 
 def finish(*operands):
@@ -474,7 +493,6 @@
     return pl.pallas_call(
         finish_kernel,
         out_shape=(shape((ROWS, D), BF16), shape((ROWS, D), BF16)),
-        scratch_shapes=[pltpu.VMEM((2 * H, ROWS, DH), F32), pltpu.VMEM((48, D), F32)],
         compiler_params=PARAMS,
         name="finish",
     )(*operands)
@@ -548,9 +566,9 @@
     keep = (keep + got[:16].astype(F32)).astype(BF16)
     two = swap(keep, 16)
     six = swap(jnp.where(rows_at(2, 2), keep, two), 56)
-    grad_keys, grad_values = finish(
-        local_k, local_v, core[:128], c2, c3a, far3, got[16:], two, six
-    )
+    parts = gather(local_k, local_v, core[:128], c2, c3a, far3, got[16:], two)
+    six, *parts = together(six, *parts)
+    grad_keys, grad_values = finish(*parts, six)
     return output, grad_queries, grad_keys, grad_values
 
 

time: 61.8 us -> 61.5 us (level)
  transfers between devices with their start and end apart: 21 -> 21, of which waited for: 13 -> 13; matrix products, arithmetic and copies ran while one was open for 1% -> 1% of each run, Pallas kernels for 6% -> 7%
where the time goes in v3:
time: 61.5 us; the launch traced here: 61.4 us
  starting transfers between devices  29 us (47%)
  waiting for transfers between devices  23.7 us (39%)
  Pallas kernels  7.54 us (12%)
  between operations  0.8 us (1%)
    ppermute x21, starting transfers between devices, swap(): return lax.ppermute(block, 'ctx', [(i, i ^ mask) for i in range(count)])  29 us
    ppermute x21, waiting for transfers between devices, swap(): return lax.ppermute(block, 'ctx', [(i, i ^ mask) for i in range(count)])  23.7 us
    pallas_call x1, Pallas kernels, outputs(): pl.pallas_call(output_kernel, out_shape=(shape((ROWS, D), BF16), shape((R...  1.68 us
    pallas_call x1, Pallas kernels, coarsen(): pl.pallas_call(coarsen_kernel, out_shape=tuple((jax.ShapeDtypeStruct((cou...  1.47 us
  transfers between devices with their start and end apart: 21, of which 13 were waited for; matrix products, arithmetic and copies ran while one was open for 1% of the time, Pallas kernels for 7%

profile of v3, /device:TPU:36, one launch (start us, length us, event | category | flops | bytes accessed | tf_op | source)
XLA Modules:
  0.0 61.4 jit_solution(678504239132257735)
XLA Ops:
  0.6 1.5 %coarsen.1 = (bf16[128,1024]{1,0:T(8,128)(2,1)S(1)}, bf16[64,1024]{1,0:T(8,128)(2,1)S(1)}, bf16[32,1024]{1,0:T(8,128)(2,1)S(1)}, bf16[16,1024]{1,0:T(8,128)(2,1)...) custom-call(bf16[128,1024]{1,0:T(8,128)(2,1)} %k_hbm.1, ...), custom_call_target="tpu_custom_call" | custom-call | tf_op jit(solution)/shard_map/coarsen/pallas_call | solution.py:76
  2.1 5.9 %collective-permute-start = (bf16[16,1024]{1,0:T(8,128)(2,1)S(1)}, bf16[16,1024]{1,0:T(8,128)(2,1)S(1)}, u32[]{:S(2)}, u32[]{:S(2)}) collective-permute-start(bf16[16,1024]{1,0:T(8,128)(2,1)S(1)} %get-tuple-element.83), channel_id=1, source_target_pairs={{0,224},{4,228},{8,232},{12,236},{16,240},{20,244},{24,248},{28,25... | collective-permute-start | bytes 98312 | tf_op jit(solution)/shard_map/ppermute | solution.py:23
  8.0 1.6 %collective-permute-start.2 = (bf16[64,1024]{1,0:T(8,128)(2,1)S(1)}, bf16[64,1024]{1,0:T(8,128)(2,1)S(1)}, u32[]{:S(2)}, u32[]{:S(2)}) collective-permute-start(bf16[64,1024]{1,0:T(8,128)(2,1)S(1)} %get-tuple-element.86), channel_id=1, source_target_pairs={{0,8},{4,12},{8,0},{12,4},{16,24},{20,28},{24,16},{28,20},{32,40},... | collective-permute-start | bytes 393224 | tf_op jit(solution)/shard_map/ppermute | solution.py:23
  10.7 4.2 %collective-permute-done.1 = bf16[16,1024]{1,0:T(8,128)(2,1)S(1)} collective-permute-done((bf16[16,1024]{1,0:T(8,128)(2,1)S(1)}, bf16[16,1024]{1,0:T(8,128)(2,1)S(1)}, u32[]{:S(2)}, u32[]{:S(2)}) %collective-permute-start.1) | collective-permute-done | bytes 32800 | tf_op jit(solution)/shard_map/ppermute | solution.py:23
  15.2 4.1 %collective-permute-done.3 = bf16[32,1024]{1,0:T(8,128)(2,1)S(1)} collective-permute-done((bf16[32,1024]{1,0:T(8,128)(2,1)S(1)}, bf16[32,1024]{1,0:T(8,128)(2,1)S(1)}, u32[]{:S(2)}, u32[]{:S(2)}) %collective-permute-start.3) | collective-permute-done | bytes 65568 | tf_op jit(solution)/shard_map/ppermute | solution.py:23
  19.4 3.1 %collective-permute-start.6 = (bf16[80,1024]{1,0:T(8,128)(2,1)S(1)}, bf16[80,1024]{1,0:T(8,128)(2,1)S(1)}, u32[]{:S(2)}, u32[]{:S(2)}) collective-permute-start(bf16[80,1024]{1,0:T(8,128)(2,1)S(1)} %constant_dynamic-update-slice_fusion), channel_id=1, source_target_pairs={{0,24},{4,28},{8,16},{12,20},{16,8},{20,12},{24,0},{28,4},{32,56},... | collective-permute-start | bytes 491528 | tf_op jit(solution)/shard_map/ppermute | solution.py:23
  24.2 3.0 %collective-permute-done.6.far3 = bf16[80,1024]{1,0:T(8,128)(2,1)S(1)} collective-permute-done((bf16[80,1024]{1,0:T(8,128)(2,1)S(1)}, bf16[80,1024]{1,0:T(8,128)(2,1)S(1)}, u32[]{:S(2)}, u32[]{:S(2)}) %collective-permute-start.6) | collective-permute-done | bytes 163872 | tf_op jit(solution)/shard_map/ppermute | solution.py:23
  27.2 2.1 %collective-permute-done.8.far2 = bf16[80,1024]{1,0:T(8,128)(2,1)S(1)} collective-permute-done((bf16[80,1024]{1,0:T(8,128)(2,1)S(1)}, bf16[80,1024]{1,0:T(8,128)(2,1)S(1)}, u32[]{:S(2)}, u32[]{:S(2)}) %collective-permute-start.8) | collective-permute-done | bytes 163872 | tf_op jit(solution)/shard_map/ppermute | solution.py:23
  30.6 0.8 %collective-permute-done.9.early = bf16[96,1024]{1,0:T(8,128)(2,1)S(1)} collective-permute-done((bf16[96,1024]{1,0:T(8,128)(2,1)S(1)}, bf16[96,1024]{1,0:T(8,128)(2,1)S(1)}, u32[]{:S(2)}, u32[]{:S(2)}) %collective-permute-start.9) | collective-permute-done | bytes 196640 | tf_op jit(solution)/shard_map/ppermute | solution.py:23
  31.3 0.9 %other_attend.1 = (bf16[128,1024]{1,0:T(8,128)(2,1)S(1)}, bf16[128,1024]{1,0:T(8,128)(2,1)S(1)}, bf16[128,1024]{1,0:T(8,128)(2,1)S(1)}, bf16[128,1024]{1,0:T(8,1...) custom-call(bf16[128,1024]{1,0:T(8,128)(2,1)S(1)} %get-tuple-element.81.q_ref, ...), custom_call_target="tpu_custom_call" | custom-call | flops 67108864 | bytes 2097152 | tf_op jit(solution)/shard_map/other_attend/pallas_call | solution.py:283
  32.8 1.4 %collective-permute-done.11.got_ref = bf16[256,1024]{1,0:T(8,128)(2,1)S(1)} collective-permute-done((bf16[256,1024]{1,0:T(8,128)(2,1)S(1)}, bf16[256,1024]{1,0:T(8,128)(2,1)S(1)}, u32[]{:S(2)}, u32[]{:S(2)}) %collective-permute-start.11) | collective-permute-done | bytes 524320 | tf_op jit(solution)/shard_map/ppermute | solution.py:23
  34.3 1.6 %collective-permute-start.13 = (bf16[80,1024]{1,0:T(8,128)(2,1)S(1)}, bf16[80,1024]{1,0:T(8,128)(2,1)S(1)}, u32[]{:S(2)}, u32[]{:S(2)}) collective-permute-start(bf16[80,1024]{1,0:T(8,128)(2,1)S(1)} %get-tuple-element.116), channel_id=1, source_target_pairs={{0,24},{4,28},{8,16},{12,20},{16,8},{20,12},{24,0},{28,4},{32,56},... | collective-permute-start | bytes 491528 | tf_op jit(solution)/shard_map/ppermute | solution.py:23
  35.8 3.2 %collective-permute-start.14 = (bf16[48,1024]{1,0:T(8,128)(2,1)S(1)}, bf16[48,1024]{1,0:T(8,128)(2,1)S(1)}, u32[]{:S(2)}, u32[]{:S(2)}) collective-permute-start(bf16[48,1024]{1,0:T(8,128)(2,1)S(1)} %get-tuple-element.117), channel_id=1, source_target_pairs={{0,16},{4,20},{8,24},{12,28},{16,0},{20,4},{24,8},{28,12},{32,48},... | collective-permute-start | bytes 294920 | tf_op jit(solution)/shard_map/ppermute | solution.py:23
  39.6 1.8 %collective-permute-done.12.near_ref = bf16[48,1024]{1,0:T(8,128)(2,1)S(1)} collective-permute-done((bf16[48,1024]{1,0:T(8,128)(2,1)S(1)}, bf16[48,1024]{1,0:T(8,128)(2,1)S(1)}, u32[]{:S(2)}, u32[]{:S(2)}) %collective-permute-start.12) | collective-permute-done | bytes 98336 | tf_op jit(solution)/shard_map/ppermute | solution.py:23
  41.5 2.3 %collective-permute-done.14.far2_ref = bf16[48,1024]{1,0:T(8,128)(2,1)S(1)} collective-permute-done((bf16[48,1024]{1,0:T(8,128)(2,1)S(1)}, bf16[48,1024]{1,0:T(8,128)(2,1)S(1)}, u32[]{:S(2)}, u32[]{:S(2)}) %collective-permute-start.14) | collective-permute-done | bytes 98336 | tf_op jit(solution)/shard_map/ppermute | solution.py:23
  44.0 0.9 %collective-permute-start.15 = (bf16[32,1024]{1,0:T(8,128)(2,1)S(1)}, bf16[32,1024]{1,0:T(8,128)(2,1)S(1)}, u32[]{:S(2)}, u32[]{:S(2)}) collective-permute-start(bf16[32,1024]{1,0:T(8,128)(2,1)S(1)} %get-tuple-element.128), channel_id=1, source_target_pairs={{0,32},{4,36},{8,40},{12,44},{16,48},{20,52},{24,56},{28,60},{32,0... | collective-permute-start | bytes 196616 | tf_op jit(solution)/shard_map/ppermute | solution.py:23
  44.9 1.7 %outputs.1 = (bf16[128,1024]{1,0:T(8,128)(2,1)}, bf16[128,1024]{1,0:T(8,128)(2,1)}) custom-call(bf16[256,1024]{1,0:T(8,128)(2,1)S(1)} %get-tuple-element.129.refs_0_, bf16[256,1024]{1,0:T(8,128)(2,1)S(1)} %get-tuple-element.130.refs_1_, bf16[256,1024]{1,0:T(8,128)(2,1)S(1)} %get-tuple-element.131.refs_2_, bf16[256,1024]{1,0:T(8,128)(2,1)S(1)} %get-tuple-element.132.refs_3_, ...), custom_call_target="tpu_custom_call" | custom-call | flops 268435456 | bytes 4194304 | tf_op jit(solution)/shard_map/outputs/pallas_call | solution.py:385
  46.6 2.0 %collective-permute-done.15 = bf16[32,1024]{1,0:T(8,128)(2,1)S(1)} collective-permute-done((bf16[32,1024]{1,0:T(8,128)(2,1)S(1)}, bf16[32,1024]{1,0:T(8,128)(2,1)S(1)}, u32[]{:S(2)}, u32[]{:S(2)}) %collective-permute-start.15) | collective-permute-done | bytes 65568 | tf_op jit(solution)/shard_map/ppermute | solution.py:23
  48.6 1.4 %collective-permute-start.16 = (bf16[16,1024]{1,0:T(8,128)(2,1)S(1)}, bf16[16,1024]{1,0:T(8,128)(2,1)S(1)}, u32[]{:S(2)}, u32[]{:S(2)}) collective-permute-start(bf16[16,1024]{1,0:T(8,128)(2,1)S(1)} %add_convert_fusion), channel_id=1, source_target_pairs={{0,64},{4,68},{8,72},{12,76},{16,80},{20,84},{24,88},{28,92},{32,9... | collective-permute-start | bytes 98312 | tf_op jit(solution)/shard_map/ppermute | solution.py:23
  50.1 1.3 %collective-permute-start.20 = (bf16[32,1024]{1,0:T(8,128)(2,1)S(1)}, bf16[32,1024]{1,0:T(8,128)(2,1)S(1)}, u32[]{:S(2)}, u32[]{:S(2)}) collective-permute-start(bf16[32,1024]{1,0:T(8,128)(2,1)S(1)} %get-tuple-element.150), channel_id=1, source_target_pairs={{0,16},{4,20},{8,24},{12,28},{16,0},{20,4},{24,8},{28,12},{32,48},... | collective-permute-start | bytes 196616 | tf_op jit(solution)/shard_map/ppermute | solution.py:23
  51.4 2.0 %collective-permute-start.19 = (bf16[64,1024]{1,0:T(8,128)(2,1)S(1)}, bf16[64,1024]{1,0:T(8,128)(2,1)S(1)}, u32[]{:S(2)}, u32[]{:S(2)}) collective-permute-start(bf16[64,1024]{1,0:T(8,128)(2,1)S(1)} %chip_sum.3), channel_id=1, source_target_pairs={{0,8},{4,12},{8,0},{12,4},{16,24},{20,28},{24,16},{28,20},{32,40},... | collective-permute-start | bytes 393224 | tf_op jit(solution)/shard_map/ppermute | solution.py:23
  53.6 5.1 %collective-permute-start.17 = (bf16[16,1024]{1,0:T(8,128)(2,1)S(1)}, bf16[16,1024]{1,0:T(8,128)(2,1)S(1)}, u32[]{:S(2)}, u32[]{:S(2)}) collective-permute-start(bf16[16,1024]{1,0:T(8,128)(2,1)S(1)} %broadcast_select_fusion.1), channel_id=1, source_target_pairs={{0,224},{4,228},{8,232},{12,236},{16,240},{20,244},{24,248},{28,25... | collective-permute-start | bytes 98312 | tf_op jit(solution)/shard_map/ppermute | solution.py:23
  59.1 1.5 %collective-permute-done.17.z7_ref = bf16[16,1024]{1,0:T(8,128)(2,1)S(1)} collective-permute-done((bf16[16,1024]{1,0:T(8,128)(2,1)S(1)}, bf16[16,1024]{1,0:T(8,128)(2,1)S(1)}, u32[]{:S(2)}, u32[]{:S(2)}) %collective-permute-start.17) | collective-permute-done | bytes 32800 | tf_op jit(solution)/shard_map/ppermute | solution.py:23
  60.5 0.8 %finish.1 = (bf16[128,1024]{1,0:T(8,128)(2,1)}, bf16[128,1024]{1,0:T(8,128)(2,1)}) custom-call(f32[128,1024]{1,0:T(8,128)S(1)} %get-tuple-element.153.part_k_ref, f32[128,1024]{1,0:T(8,128)S(1)} %get-tuple-element.154.part_v_ref, bf16[16,1024]{1,0:T(8,128)(2,1)S(1)} %collective-permute-done.17.z7_ref), custom_call_target="tpu_custom_call" | custom-call | tf_op jit(solution)/shard_map/finish/pallas_call | solution.py:493
  (44 shorter events, 6.4 us)
Async XLA Ops:
  2.1 7.8 %collective-permute-start = (bf16[16,1024]{1,0:T(8,128)(2,1)S(1)}, bf16[16,1024]{1,0:T(8,128)(2,1)S(1)}, u32[]{:S(2)}, u32[]{:S(2)}) collective-permute-start(bf16[16,1024]{1,0:T(8,128)(2,1)S(1)} %get-tuple-element.83), channel_id=1, source_target_pairs={{0,224},{4,228},{8,232},{12,236},{16,240},{20,244},{24,248},{28,25... | collective-permute-start | bytes 98312 | tf_op jit(solution)/shard_map/ppermute | solution.py:23
  8.0 6.9 %collective-permute-start.2 = (bf16[64,1024]{1,0:T(8,128)(2,1)S(1)}, bf16[64,1024]{1,0:T(8,128)(2,1)S(1)}, u32[]{:S(2)}, u32[]{:S(2)}) collective-permute-start(bf16[64,1024]{1,0:T(8,128)(2,1)S(1)} %get-tuple-element.86), channel_id=1, source_target_pairs={{0,8},{4,12},{8,0},{12,4},{16,24},{20,28},{24,16},{28,20},{32,40},... | collective-permute-start | bytes 393224 | tf_op jit(solution)/shard_map/ppermute | solution.py:23
  9.6 9.7 %collective-permute-start.4 = (bf16[128,1024]{1,0:T(8,128)(2,1)S(1)}, bf16[128,1024]{1,0:T(8,128)(2,1)S(1)}, u32[]{:S(2)}, u32[]{:S(2)}) collective-permute-start(bf16[128,1024]{1,0:T(8,128)(2,1)S(1)} %get-tuple-element.88), channel_id=1, source_target_pairs={{0,4},{4,0},{8,12},{12,8},{16,20},{20,16},{24,28},{28,24},{32,36},... | collective-permute-start | bytes 786440 | tf_op jit(solution)/shard_map/ppermute | solution.py:23
  10.0 4.8 %collective-permute-start.1 = (bf16[16,1024]{1,0:T(8,128)(2,1)S(1)}, bf16[16,1024]{1,0:T(8,128)(2,1)S(1)}, u32[]{:S(2)}, u32[]{:S(2)}) collective-permute-start(bf16[16,1024]{1,0:T(8,128)(2,1)S(1)} %broadcast_select_fusion), channel_id=1, source_target_pairs={{0,64},{4,68},{8,72},{12,76},{16,80},{20,84},{24,88},{28,92},{32,9... | collective-permute-start | bytes 98312 | tf_op jit(solution)/shard_map/ppermute | solution.py:23
  14.9 4.4 %collective-permute-start.3 = (bf16[32,1024]{1,0:T(8,128)(2,1)S(1)}, bf16[32,1024]{1,0:T(8,128)(2,1)S(1)}, u32[]{:S(2)}, u32[]{:S(2)}) collective-permute-start(bf16[32,1024]{1,0:T(8,128)(2,1)S(1)} %pad_maximum_fusion.3), channel_id=1, source_target_pairs={{0,32},{4,36},{8,40},{12,44},{16,48},{20,52},{24,56},{28,60},{32,0... | collective-permute-start | bytes 196616 | tf_op jit(solution)/shard_map/ppermute | solution.py:23
  15.2 4.2 %collective-permute-start.5 = (bf16[64,1024]{1,0:T(8,128)(2,1)S(1)}, bf16[64,1024]{1,0:T(8,128)(2,1)S(1)}, u32[]{:S(2)}, u32[]{:S(2)}) collective-permute-start(bf16[64,1024]{1,0:T(8,128)(2,1)S(1)} %collective-permute-done.2.rest_1_), channel_id=1, source_target_pairs={{0,4},{4,0},{8,12},{12,8},{16,20},{20,16},{24,28},{28,24},{32,36},... | collective-permute-start | bytes 393224 | tf_op jit(solution)/shard_map/ppermute | solution.py:23
  19.4 7.8 %collective-permute-start.6 = (bf16[80,1024]{1,0:T(8,128)(2,1)S(1)}, bf16[80,1024]{1,0:T(8,128)(2,1)S(1)}, u32[]{:S(2)}, u32[]{:S(2)}) collective-permute-start(bf16[80,1024]{1,0:T(8,128)(2,1)S(1)} %constant_dynamic-update-slice_fusion), channel_id=1, source_target_pairs={{0,24},{4,28},{8,16},{12,20},{16,8},{20,12},{24,0},{28,4},{32,56},... | collective-permute-start | bytes 491528 | tf_op jit(solution)/shard_map/ppermute | solution.py:23
  22.5 6.8 %collective-permute-start.8 = (bf16[80,1024]{1,0:T(8,128)(2,1)S(1)}, bf16[80,1024]{1,0:T(8,128)(2,1)S(1)}, u32[]{:S(2)}, u32[]{:S(2)}) collective-permute-start(bf16[80,1024]{1,0:T(8,128)(2,1)S(1)} %constant_dynamic-update-slice_fusion), channel_id=1, source_target_pairs={{0,16},{4,20},{8,24},{12,28},{16,0},{20,4},{24,8},{28,12},{32,48},... | collective-permute-start | bytes 491528 | tf_op jit(solution)/shard_map/ppermute | solution.py:23
  23.1 6.3 %collective-permute-start.7 = (bf16[48,1024]{1,0:T(8,128)(2,1)S(1)}, bf16[48,1024]{1,0:T(8,128)(2,1)S(1)}, u32[]{:S(2)}, u32[]{:S(2)}) collective-permute-start(bf16[48,1024]{1,0:T(8,128)(2,1)S(1)} %pad_maximum_fusion.2.own), channel_id=1, source_target_pairs={{0,8},{4,12},{8,0},{12,4},{16,24},{20,28},{24,16},{28,20},{32,40},... | collective-permute-start | bytes 294920 | tf_op jit(solution)/shard_map/ppermute | solution.py:23
  29.3 2.0 %collective-permute-start.10 = (bf16[160,1024]{1,0:T(8,128)(2,1)S(1)}, bf16[160,1024]{1,0:T(8,128)(2,1)S(1)}, u32[]{:S(2)}, u32[]{:S(2)}) collective-permute-start(bf16[160,1024]{1,0:T(8,128)(2,1)S(1)} %pad_maximum_fusion), channel_id=1, source_target_pairs={{0,4},{4,0},{8,12},{12,8},{16,20},{20,16},{24,28},{28,24},{32,36},... | collective-permute-start | bytes 983048 | tf_op jit(solution)/shard_map/ppermute | solution.py:23
  29.4 1.9 %collective-permute-start.9 = (bf16[96,1024]{1,0:T(8,128)(2,1)S(1)}, bf16[96,1024]{1,0:T(8,128)(2,1)S(1)}, u32[]{:S(2)}, u32[]{:S(2)}) collective-permute-start(bf16[96,1024]{1,0:T(8,128)(2,1)S(1)} %pad_maximum_fusion.1), channel_id=1, source_target_pairs={{0,4},{4,0},{8,12},{12,8},{16,20},{20,16},{24,28},{28,24},{32,36},... | collective-permute-start | bytes 589832 | tf_op jit(solution)/shard_map/ppermute | solution.py:23
  32.2 2.0 %collective-permute-start.11 = (bf16[256,1024]{1,0:T(8,128)(2,1)S(1)}, bf16[256,1024]{1,0:T(8,128)(2,1)S(1)}, u32[]{:S(2)}, u32[]{:S(2)}) collective-permute-start(bf16[256,1024]{1,0:T(8,128)(2,1)S(1)} %get-tuple-element.104), channel_id=1, source_target_pairs={{0,4},{4,0},{8,12},{12,8},{16,20},{20,16},{24,28},{28,24},{32,36},... | collective-permute-start | bytes 1572872 | tf_op jit(solution)/shard_map/ppermute | solution.py:23
  34.3 9.7 %collective-permute-start.13 = (bf16[80,1024]{1,0:T(8,128)(2,1)S(1)}, bf16[80,1024]{1,0:T(8,128)(2,1)S(1)}, u32[]{:S(2)}, u32[]{:S(2)}) collective-permute-start(bf16[80,1024]{1,0:T(8,128)(2,1)S(1)} %get-tuple-element.116), channel_id=1, source_target_pairs={{0,24},{4,28},{8,16},{12,20},{16,8},{20,12},{24,0},{28,4},{32,56},... | collective-permute-start | bytes 491528 | tf_op jit(solution)/shard_map/ppermute | solution.py:23
  35.8 5.6 %collective-permute-start.12 = (bf16[48,1024]{1,0:T(8,128)(2,1)S(1)}, bf16[48,1024]{1,0:T(8,128)(2,1)S(1)}, u32[]{:S(2)}, u32[]{:S(2)}) collective-permute-start(bf16[48,1024]{1,0:T(8,128)(2,1)S(1)} %get-tuple-element.115), channel_id=1, source_target_pairs={{0,8},{4,12},{8,0},{12,4},{16,24},{20,28},{24,16},{28,20},{32,40},... | collective-permute-start | bytes 294920 | tf_op jit(solution)/shard_map/ppermute | solution.py:23
  35.8 7.9 %collective-permute-start.14 = (bf16[48,1024]{1,0:T(8,128)(2,1)S(1)}, bf16[48,1024]{1,0:T(8,128)(2,1)S(1)}, u32[]{:S(2)}, u32[]{:S(2)}) collective-permute-start(bf16[48,1024]{1,0:T(8,128)(2,1)S(1)} %get-tuple-element.117), channel_id=1, source_target_pairs={{0,16},{4,20},{8,24},{12,28},{16,0},{20,4},{24,8},{28,12},{32,48},... | collective-permute-start | bytes 294920 | tf_op jit(solution)/shard_map/ppermute | solution.py:23
  43.9 7.4 %collective-permute-start.18 = (bf16[192,1024]{1,0:T(8,128)(2,1)S(1)}, bf16[192,1024]{1,0:T(8,128)(2,1)S(1)}, u32[]{:S(2)}, u32[]{:S(2)}) collective-permute-start(bf16[192,1024]{1,0:T(8,128)(2,1)S(1)} %get-tuple-element.148), channel_id=1, source_target_pairs={{0,4},{4,0},{8,12},{12,8},{16,20},{20,16},{24,28},{28,24},{32,36},... | collective-permute-start | bytes 1179656 | tf_op jit(solution)/shard_map/ppermute | solution.py:23
  44.0 4.6 %collective-permute-start.15 = (bf16[32,1024]{1,0:T(8,128)(2,1)S(1)}, bf16[32,1024]{1,0:T(8,128)(2,1)S(1)}, u32[]{:S(2)}, u32[]{:S(2)}) collective-permute-start(bf16[32,1024]{1,0:T(8,128)(2,1)S(1)} %get-tuple-element.128), channel_id=1, source_target_pairs={{0,32},{4,36},{8,40},{12,44},{16,48},{20,52},{24,56},{28,60},{32,0... | collective-permute-start | bytes 196616 | tf_op jit(solution)/shard_map/ppermute | solution.py:23
  48.6 4.9 %collective-permute-start.16 = (bf16[16,1024]{1,0:T(8,128)(2,1)S(1)}, bf16[16,1024]{1,0:T(8,128)(2,1)S(1)}, u32[]{:S(2)}, u32[]{:S(2)}) collective-permute-start(bf16[16,1024]{1,0:T(8,128)(2,1)S(1)} %add_convert_fusion), channel_id=1, source_target_pairs={{0,64},{4,68},{8,72},{12,76},{16,80},{20,84},{24,88},{28,92},{32,9... | collective-permute-start | bytes 98312 | tf_op jit(solution)/shard_map/ppermute | solution.py:23
  50.1 8.6 %collective-permute-start.20 = (bf16[32,1024]{1,0:T(8,128)(2,1)S(1)}, bf16[32,1024]{1,0:T(8,128)(2,1)S(1)}, u32[]{:S(2)}, u32[]{:S(2)}) collective-permute-start(bf16[32,1024]{1,0:T(8,128)(2,1)S(1)} %get-tuple-element.150), channel_id=1, source_target_pairs={{0,16},{4,20},{8,24},{12,28},{16,0},{20,4},{24,8},{28,12},{32,48},... | collective-permute-start | bytes 196616 | tf_op jit(solution)/shard_map/ppermute | solution.py:23
  51.4 7.3 %collective-permute-start.19 = (bf16[64,1024]{1,0:T(8,128)(2,1)S(1)}, bf16[64,1024]{1,0:T(8,128)(2,1)S(1)}, u32[]{:S(2)}, u32[]{:S(2)}) collective-permute-start(bf16[64,1024]{1,0:T(8,128)(2,1)S(1)} %chip_sum.3), channel_id=1, source_target_pairs={{0,8},{4,12},{8,0},{12,4},{16,24},{20,28},{24,16},{28,20},{32,40},... | collective-permute-start | bytes 393224 | tf_op jit(solution)/shard_map/ppermute | solution.py:23
  53.6 6.9 %collective-permute-start.17 = (bf16[16,1024]{1,0:T(8,128)(2,1)S(1)}, bf16[16,1024]{1,0:T(8,128)(2,1)S(1)}, u32[]{:S(2)}, u32[]{:S(2)}) collective-permute-start(bf16[16,1024]{1,0:T(8,128)(2,1)S(1)} %broadcast_select_fusion.1), channel_id=1, source_target_pairs={{0,224},{4,228},{8,232},{12,236},{16,240},{20,244},{24,248},{28,25... | collective-permute-start | bytes 98312 | tf_op jit(solution)/shard_map/ppermute | solution.py:23

commit v4 on v3

--- a/solution.py
+++ b/solution.py
@@ -515,17 +515,19 @@
     six = swap(c6, 56)
     c1 = swap(c1, 1)
     c2 = swap(c2, 2)
+    c3a = swap(c3, 4)
     two = swap(jnp.where(rows_at(0, 2), six, c5), 16)
     keep = jnp.where(rows_at(2, 2), six, two)
-    send, c2 = together(jnp.concatenate([keep, c4]), c2)
+    send, c2, c3a = together(jnp.concatenate([keep, c4]), c2, c3a)
     core = swap(c2, 1)
     own = jnp.concatenate([keep, swap(send, 8)])
     own, c1, c2, core = together(own, c1, c2, core)
     far = jnp.concatenate([own, c3])
-    near, far3, far2 = swap(own, 2), swap(far, 6), swap(far, 4)
+    near, far3, far2 = swap(own, 2), swap(far, 6), swap(own, 4)
     near_key, near_value, exponent, dprob, stats = near_scores(
         queries, keys, values, cotangent, c1, c2, core
     )
+    far2 = jnp.concatenate([far2, c3a])
     early = swap(jnp.concatenate([own, near]), 1)
     far3, stats = together(far3, stats)
     late = swap(jnp.concatenate([far2, far3]), 1)

time: 61.5 us -> 61.3 us (level)
  waiting for transfers between devices: 23.7 us -> 22.6 us
  starting transfers between devices: 29 us -> 29.9 us
    ppermute x21 -> x22, waiting for transfers between devices: 23.7 us -> 22.6 us  [swap(): return lax.ppermute(block, 'ctx', [(i, i ^ mask) for i in range(count)])]
    ppermute x21 -> x22, starting transfers between devices: 29 us -> 29.9 us  [swap(): return lax.ppermute(block, 'ctx', [(i, i ^ mask) for i in range(count)])]
  transfers between devices with their start and end apart: 21 -> 22, of which waited for: 13 -> 12; matrix products, arithmetic and copies ran while one was open for 1% -> 1% of each run, Pallas kernels for 7% -> 7%
where the time goes in v4:
time: 61.3 us; the launch traced here: 61.2 us
  starting transfers between devices  29.9 us (49%)
  waiting for transfers between devices  22.6 us (37%)
  Pallas kernels  7.53 us (12%)
  between operations  0.8 us (1%)
    ppermute x22, starting transfers between devices, swap(): return lax.ppermute(block, 'ctx', [(i, i ^ mask) for i in range(count)])  29.9 us
    ppermute x22, waiting for transfers between devices, swap(): return lax.ppermute(block, 'ctx', [(i, i ^ mask) for i in range(count)])  22.6 us
    pallas_call x1, Pallas kernels, outputs(): pl.pallas_call(output_kernel, out_shape=(shape((ROWS, D), BF16), shape((R...  1.68 us
    pallas_call x1, Pallas kernels, coarsen(): pl.pallas_call(coarsen_kernel, out_shape=tuple((jax.ShapeDtypeStruct((cou...  1.47 us
  transfers between devices with their start and end apart: 22, of which 12 were waited for; matrix products, arithmetic and copies ran while one was open for 1% of the time, Pallas kernels for 7%

profile of v4, /device:TPU:36, one launch (start us, length us, event | category | flops | bytes accessed | tf_op | source)
XLA Modules:
  0.0 61.2 jit_solution(16542535255788371101)
XLA Ops:
  0.6 1.5 %coarsen.1 = (bf16[128,1024]{1,0:T(8,128)(2,1)S(1)}, bf16[64,1024]{1,0:T(8,128)(2,1)S(1)}, bf16[32,1024]{1,0:T(8,128)(2,1)S(1)}, bf16[16,1024]{1,0:T(8,128)(2,1)...) custom-call(bf16[128,1024]{1,0:T(8,128)(2,1)} %k_hbm.1, ...), custom_call_target="tpu_custom_call" | custom-call | tf_op jit(solution)/shard_map/coarsen/pallas_call | solution.py:76
  2.1 5.9 %collective-permute-start = (bf16[16,1024]{1,0:T(8,128)(2,1)S(1)}, bf16[16,1024]{1,0:T(8,128)(2,1)S(1)}, u32[]{:S(2)}, u32[]{:S(2)}) collective-permute-start(bf16[16,1024]{1,0:T(8,128)(2,1)S(1)} %get-tuple-element.84), channel_id=1, source_target_pairs={{0,224},{4,228},{8,232},{12,236},{16,240},{20,244},{24,248},{28,25... | collective-permute-start | bytes 98312 | tf_op jit(solution)/shard_map/ppermute | solution.py:23
  8.0 3.2 %collective-permute-start.3 = (bf16[32,1024]{1,0:T(8,128)(2,1)S(1)}, bf16[32,1024]{1,0:T(8,128)(2,1)S(1)}, u32[]{:S(2)}, u32[]{:S(2)}) collective-permute-start(bf16[32,1024]{1,0:T(8,128)(2,1)S(1)} %get-tuple-element.88), channel_id=1, source_target_pairs={{0,16},{4,20},{8,24},{12,28},{16,0},{20,4},{24,8},{28,12},{32,48},... | collective-permute-start | bytes 196616 | tf_op jit(solution)/shard_map/ppermute | solution.py:23
  12.6 4.3 %collective-permute-done.1 = bf16[16,1024]{1,0:T(8,128)(2,1)S(1)} collective-permute-done((bf16[16,1024]{1,0:T(8,128)(2,1)S(1)}, bf16[16,1024]{1,0:T(8,128)(2,1)S(1)}, u32[]{:S(2)}, u32[]{:S(2)}) %collective-permute-start.1) | collective-permute-done | bytes 32800 | tf_op jit(solution)/shard_map/ppermute | solution.py:23
  17.2 4.1 %collective-permute-done.4 = bf16[32,1024]{1,0:T(8,128)(2,1)S(1)} collective-permute-done((bf16[32,1024]{1,0:T(8,128)(2,1)S(1)}, bf16[32,1024]{1,0:T(8,128)(2,1)S(1)}, u32[]{:S(2)}, u32[]{:S(2)}) %collective-permute-start.4) | collective-permute-done | bytes 65568 | tf_op jit(solution)/shard_map/ppermute | solution.py:23
  21.4 1.1 %collective-permute-start.7 = (bf16[80,1024]{1,0:T(8,128)(2,1)S(1)}, bf16[80,1024]{1,0:T(8,128)(2,1)S(1)}, u32[]{:S(2)}, u32[]{:S(2)}) collective-permute-start(bf16[80,1024]{1,0:T(8,128)(2,1)S(1)} %pad_maximum_fusion.2), channel_id=1, source_target_pairs={{0,24},{4,28},{8,16},{12,20},{16,8},{20,12},{24,0},{28,4},{32,56},... | collective-permute-start | bytes 491528 | tf_op jit(solution)/shard_map/ppermute | solution.py:23
  22.5 2.4 %collective-permute-start.9 = (bf16[48,1024]{1,0:T(8,128)(2,1)S(1)}, bf16[48,1024]{1,0:T(8,128)(2,1)S(1)}, u32[]{:S(2)}, u32[]{:S(2)}) collective-permute-start(bf16[48,1024]{1,0:T(8,128)(2,1)S(1)} %pad_maximum_fusion.4.own), channel_id=1, source_target_pairs={{0,16},{4,20},{8,24},{12,28},{16,0},{20,4},{24,8},{28,12},{32,48},... | collective-permute-start | bytes 294920 | tf_op jit(solution)/shard_map/ppermute | solution.py:23
  26.2 2.8 %collective-permute-done.7.far3 = bf16[80,1024]{1,0:T(8,128)(2,1)S(1)} collective-permute-done((bf16[80,1024]{1,0:T(8,128)(2,1)S(1)}, bf16[80,1024]{1,0:T(8,128)(2,1)S(1)}, u32[]{:S(2)}, u32[]{:S(2)}) %collective-permute-start.7) | collective-permute-done | bytes 163872 | tf_op jit(solution)/shard_map/ppermute | solution.py:23
  31.1 0.9 %other_attend.1 = (bf16[128,1024]{1,0:T(8,128)(2,1)S(1)}, bf16[128,1024]{1,0:T(8,128)(2,1)S(1)}, bf16[128,1024]{1,0:T(8,128)(2,1)S(1)}, bf16[128,1024]{1,0:T(8,1...) custom-call(bf16[128,1024]{1,0:T(8,128)(2,1)S(1)} %get-tuple-element.82.q_ref, ...), custom_call_target="tpu_custom_call" | custom-call | flops 67108864 | bytes 2097152 | tf_op jit(solution)/shard_map/other_attend/pallas_call | solution.py:283
  32.6 1.4 %collective-permute-done.12.got_ref = bf16[256,1024]{1,0:T(8,128)(2,1)S(1)} collective-permute-done((bf16[256,1024]{1,0:T(8,128)(2,1)S(1)}, bf16[256,1024]{1,0:T(8,128)(2,1)S(1)}, u32[]{:S(2)}, u32[]{:S(2)}) %collective-permute-start.12) | collective-permute-done | bytes 524320 | tf_op jit(solution)/shard_map/ppermute | solution.py:23
  34.1 1.8 %collective-permute-start.14 = (bf16[80,1024]{1,0:T(8,128)(2,1)S(1)}, bf16[80,1024]{1,0:T(8,128)(2,1)S(1)}, u32[]{:S(2)}, u32[]{:S(2)}) collective-permute-start(bf16[80,1024]{1,0:T(8,128)(2,1)S(1)} %get-tuple-element.118), channel_id=1, source_target_pairs={{0,24},{4,28},{8,16},{12,20},{16,8},{20,12},{24,0},{28,4},{32,56},... | collective-permute-start | bytes 491528 | tf_op jit(solution)/shard_map/ppermute | solution.py:23
  36.0 2.8 %collective-permute-start.15 = (bf16[48,1024]{1,0:T(8,128)(2,1)S(1)}, bf16[48,1024]{1,0:T(8,128)(2,1)S(1)}, u32[]{:S(2)}, u32[]{:S(2)}) collective-permute-start(bf16[48,1024]{1,0:T(8,128)(2,1)S(1)} %get-tuple-element.119), channel_id=1, source_target_pairs={{0,16},{4,20},{8,24},{12,28},{16,0},{20,4},{24,8},{28,12},{32,48},... | collective-permute-start | bytes 294920 | tf_op jit(solution)/shard_map/ppermute | solution.py:23
  39.4 2.1 %collective-permute-done.13.near_ref = bf16[48,1024]{1,0:T(8,128)(2,1)S(1)} collective-permute-done((bf16[48,1024]{1,0:T(8,128)(2,1)S(1)}, bf16[48,1024]{1,0:T(8,128)(2,1)S(1)}, u32[]{:S(2)}, u32[]{:S(2)}) %collective-permute-start.13) | collective-permute-done | bytes 98336 | tf_op jit(solution)/shard_map/ppermute | solution.py:23
  41.5 2.1 %collective-permute-done.15.far2_ref = bf16[48,1024]{1,0:T(8,128)(2,1)S(1)} collective-permute-done((bf16[48,1024]{1,0:T(8,128)(2,1)S(1)}, bf16[48,1024]{1,0:T(8,128)(2,1)S(1)}, u32[]{:S(2)}, u32[]{:S(2)}) %collective-permute-start.15) | collective-permute-done | bytes 98336 | tf_op jit(solution)/shard_map/ppermute | solution.py:23
  43.8 1.1 %collective-permute-start.16 = (bf16[32,1024]{1,0:T(8,128)(2,1)S(1)}, bf16[32,1024]{1,0:T(8,128)(2,1)S(1)}, u32[]{:S(2)}, u32[]{:S(2)}) collective-permute-start(bf16[32,1024]{1,0:T(8,128)(2,1)S(1)} %get-tuple-element.130), channel_id=1, source_target_pairs={{0,32},{4,36},{8,40},{12,44},{16,48},{20,52},{24,56},{28,60},{32,0... | collective-permute-start | bytes 196616 | tf_op jit(solution)/shard_map/ppermute | solution.py:23
  44.9 1.7 %outputs.1 = (bf16[128,1024]{1,0:T(8,128)(2,1)}, bf16[128,1024]{1,0:T(8,128)(2,1)}) custom-call(bf16[256,1024]{1,0:T(8,128)(2,1)S(1)} %get-tuple-element.131.refs_0_, bf16[256,1024]{1,0:T(8,128)(2,1)S(1)} %get-tuple-element.132.refs_1_, bf16[256,1024]{1,0:T(8,128)(2,1)S(1)} %get-tuple-element.133.refs_2_, bf16[256,1024]{1,0:T(8,128)(2,1)S(1)} %get-tuple-element.134.refs_3_, ...), custom_call_target="tpu_custom_call" | custom-call | flops 268435456 | bytes 4194304 | tf_op jit(solution)/shard_map/outputs/pallas_call | solution.py:385
  46.6 1.8 %collective-permute-done.16 = bf16[32,1024]{1,0:T(8,128)(2,1)S(1)} collective-permute-done((bf16[32,1024]{1,0:T(8,128)(2,1)S(1)}, bf16[32,1024]{1,0:T(8,128)(2,1)S(1)}, u32[]{:S(2)}, u32[]{:S(2)}) %collective-permute-start.16) | collective-permute-done | bytes 65568 | tf_op jit(solution)/shard_map/ppermute | solution.py:23
  48.4 1.5 %collective-permute-start.17 = (bf16[16,1024]{1,0:T(8,128)(2,1)S(1)}, bf16[16,1024]{1,0:T(8,128)(2,1)S(1)}, u32[]{:S(2)}, u32[]{:S(2)}) collective-permute-start(bf16[16,1024]{1,0:T(8,128)(2,1)S(1)} %add_convert_fusion), channel_id=1, source_target_pairs={{0,64},{4,68},{8,72},{12,76},{16,80},{20,84},{24,88},{28,92},{32,9... | collective-permute-start | bytes 98312 | tf_op jit(solution)/shard_map/ppermute | solution.py:23
  49.9 1.3 %collective-permute-start.21 = (bf16[32,1024]{1,0:T(8,128)(2,1)S(1)}, bf16[32,1024]{1,0:T(8,128)(2,1)S(1)}, u32[]{:S(2)}, u32[]{:S(2)}) collective-permute-start(bf16[32,1024]{1,0:T(8,128)(2,1)S(1)} %get-tuple-element.152), channel_id=1, source_target_pairs={{0,16},{4,20},{8,24},{12,28},{16,0},{20,4},{24,8},{28,12},{32,48},... | collective-permute-start | bytes 196616 | tf_op jit(solution)/shard_map/ppermute | solution.py:23
  51.2 1.2 %collective-permute-start.20 = (bf16[64,1024]{1,0:T(8,128)(2,1)S(1)}, bf16[64,1024]{1,0:T(8,128)(2,1)S(1)}, u32[]{:S(2)}, u32[]{:S(2)}) collective-permute-start(bf16[64,1024]{1,0:T(8,128)(2,1)S(1)} %chip_sum.3), channel_id=1, source_target_pairs={{0,8},{4,12},{8,0},{12,4},{16,24},{20,28},{24,16},{28,20},{32,40},... | collective-permute-start | bytes 393224 | tf_op jit(solution)/shard_map/ppermute | solution.py:23
  52.4 0.9 %collective-permute-done.17.z2_ref = bf16[16,1024]{1,0:T(8,128)(2,1)S(1)} collective-permute-done((bf16[16,1024]{1,0:T(8,128)(2,1)S(1)}, bf16[16,1024]{1,0:T(8,128)(2,1)S(1)}, u32[]{:S(2)}, u32[]{:S(2)}) %collective-permute-start.17) | collective-permute-done | bytes 32800 | tf_op jit(solution)/shard_map/ppermute | solution.py:23
  53.4 4.6 %collective-permute-start.18 = (bf16[16,1024]{1,0:T(8,128)(2,1)S(1)}, bf16[16,1024]{1,0:T(8,128)(2,1)S(1)}, u32[]{:S(2)}, u32[]{:S(2)}) collective-permute-start(bf16[16,1024]{1,0:T(8,128)(2,1)S(1)} %broadcast_select_fusion.1), channel_id=1, source_target_pairs={{0,224},{4,228},{8,232},{12,236},{16,240},{20,244},{24,248},{28,25... | collective-permute-start | bytes 98312 | tf_op jit(solution)/shard_map/ppermute | solution.py:23
  58.4 2.0 %collective-permute-done.18.z7_ref = bf16[16,1024]{1,0:T(8,128)(2,1)S(1)} collective-permute-done((bf16[16,1024]{1,0:T(8,128)(2,1)S(1)}, bf16[16,1024]{1,0:T(8,128)(2,1)S(1)}, u32[]{:S(2)}, u32[]{:S(2)}) %collective-permute-start.18) | collective-permute-done | bytes 32800 | tf_op jit(solution)/shard_map/ppermute | solution.py:23
  60.3 0.8 %finish.1 = (bf16[128,1024]{1,0:T(8,128)(2,1)}, bf16[128,1024]{1,0:T(8,128)(2,1)}) custom-call(f32[128,1024]{1,0:T(8,128)S(1)} %get-tuple-element.155.part_k_ref, f32[128,1024]{1,0:T(8,128)S(1)} %get-tuple-element.156.part_v_ref, bf16[16,1024]{1,0:T(8,128)(2,1)S(1)} %collective-permute-done.18.z7_ref), custom_call_target="tpu_custom_call" | custom-call | tf_op jit(solution)/shard_map/finish/pallas_call | solution.py:493
  (46 shorter events, 7.1 us)
Async XLA Ops:
  2.1 9.8 %collective-permute-start = (bf16[16,1024]{1,0:T(8,128)(2,1)S(1)}, bf16[16,1024]{1,0:T(8,128)(2,1)S(1)}, u32[]{:S(2)}, u32[]{:S(2)}) collective-permute-start(bf16[16,1024]{1,0:T(8,128)(2,1)S(1)} %get-tuple-element.84), channel_id=1, source_target_pairs={{0,224},{4,228},{8,232},{12,236},{16,240},{20,244},{24,248},{28,25... | collective-permute-start | bytes 98312 | tf_op jit(solution)/shard_map/ppermute | solution.py:23
  8.0 8.9 %collective-permute-start.3 = (bf16[32,1024]{1,0:T(8,128)(2,1)S(1)}, bf16[32,1024]{1,0:T(8,128)(2,1)S(1)}, u32[]{:S(2)}, u32[]{:S(2)}) collective-permute-start(bf16[32,1024]{1,0:T(8,128)(2,1)S(1)} %get-tuple-element.88), channel_id=1, source_target_pairs={{0,16},{4,20},{8,24},{12,28},{16,0},{20,4},{24,8},{28,12},{32,48},... | collective-permute-start | bytes 196616 | tf_op jit(solution)/shard_map/ppermute | solution.py:23
  11.2 5.7 %collective-permute-start.2 = (bf16[64,1024]{1,0:T(8,128)(2,1)S(1)}, bf16[64,1024]{1,0:T(8,128)(2,1)S(1)}, u32[]{:S(2)}, u32[]{:S(2)}) collective-permute-start(bf16[64,1024]{1,0:T(8,128)(2,1)S(1)} %get-tuple-element.87), channel_id=1, source_target_pairs={{0,8},{4,12},{8,0},{12,4},{16,24},{20,28},{24,16},{28,20},{32,40},... | collective-permute-start | bytes 393224 | tf_op jit(solution)/shard_map/ppermute | solution.py:23
  11.9 9.4 %collective-permute-start.5 = (bf16[128,1024]{1,0:T(8,128)(2,1)S(1)}, bf16[128,1024]{1,0:T(8,128)(2,1)S(1)}, u32[]{:S(2)}, u32[]{:S(2)}) collective-permute-start(bf16[128,1024]{1,0:T(8,128)(2,1)S(1)} %get-tuple-element.90), channel_id=1, source_target_pairs={{0,4},{4,0},{8,12},{12,8},{16,20},{20,16},{24,28},{28,24},{32,36},... | collective-permute-start | bytes 786440 | tf_op jit(solution)/shard_map/ppermute | solution.py:23
  12.0 4.8 %collective-permute-start.1 = (bf16[16,1024]{1,0:T(8,128)(2,1)S(1)}, bf16[16,1024]{1,0:T(8,128)(2,1)S(1)}, u32[]{:S(2)}, u32[]{:S(2)}) collective-permute-start(bf16[16,1024]{1,0:T(8,128)(2,1)S(1)} %broadcast_select_fusion), channel_id=1, source_target_pairs={{0,64},{4,68},{8,72},{12,76},{16,80},{20,84},{24,88},{28,92},{32,9... | collective-permute-start | bytes 98312 | tf_op jit(solution)/shard_map/ppermute | solution.py:23
  17.0 4.4 %collective-permute-start.4 = (bf16[32,1024]{1,0:T(8,128)(2,1)S(1)}, bf16[32,1024]{1,0:T(8,128)(2,1)S(1)}, u32[]{:S(2)}, u32[]{:S(2)}) collective-permute-start(bf16[32,1024]{1,0:T(8,128)(2,1)S(1)} %pad_maximum_fusion.5), channel_id=1, source_target_pairs={{0,32},{4,36},{8,40},{12,44},{16,48},{20,52},{24,56},{28,60},{32,0... | collective-permute-start | bytes 196616 | tf_op jit(solution)/shard_map/ppermute | solution.py:23
  17.2 4.2 %collective-permute-start.6 = (bf16[64,1024]{1,0:T(8,128)(2,1)S(1)}, bf16[64,1024]{1,0:T(8,128)(2,1)S(1)}, u32[]{:S(2)}, u32[]{:S(2)}) collective-permute-start(bf16[64,1024]{1,0:T(8,128)(2,1)S(1)} %collective-permute-done.2.rest_1_), channel_id=1, source_target_pairs={{0,4},{4,0},{8,12},{12,8},{16,20},{20,16},{24,28},{28,24},{32,36},... | collective-permute-start | bytes 393224 | tf_op jit(solution)/shard_map/ppermute | solution.py:23
  21.4 7.7 %collective-permute-start.7 = (bf16[80,1024]{1,0:T(8,128)(2,1)S(1)}, bf16[80,1024]{1,0:T(8,128)(2,1)S(1)}, u32[]{:S(2)}, u32[]{:S(2)}) collective-permute-start(bf16[80,1024]{1,0:T(8,128)(2,1)S(1)} %pad_maximum_fusion.2), channel_id=1, source_target_pairs={{0,24},{4,28},{8,16},{12,20},{16,8},{20,12},{24,0},{28,4},{32,56},... | collective-permute-start | bytes 491528 | tf_op jit(solution)/shard_map/ppermute | solution.py:23
  22.5 6.6 %collective-permute-start.9 = (bf16[48,1024]{1,0:T(8,128)(2,1)S(1)}, bf16[48,1024]{1,0:T(8,128)(2,1)S(1)}, u32[]{:S(2)}, u32[]{:S(2)}) collective-permute-start(bf16[48,1024]{1,0:T(8,128)(2,1)S(1)} %pad_maximum_fusion.4.own), channel_id=1, source_target_pairs={{0,16},{4,20},{8,24},{12,28},{16,0},{20,4},{24,8},{28,12},{32,48},... | collective-permute-start | bytes 294920 | tf_op jit(solution)/shard_map/ppermute | solution.py:23
  24.9 4.6 %collective-permute-start.8 = (bf16[48,1024]{1,0:T(8,128)(2,1)S(1)}, bf16[48,1024]{1,0:T(8,128)(2,1)S(1)}, u32[]{:S(2)}, u32[]{:S(2)}) collective-permute-start(bf16[48,1024]{1,0:T(8,128)(2,1)S(1)} %pad_maximum_fusion.4.own), channel_id=1, source_target_pairs={{0,8},{4,12},{8,0},{12,4},{16,24},{20,28},{24,16},{28,20},{32,40},... | collective-permute-start | bytes 294920 | tf_op jit(solution)/shard_map/ppermute | solution.py:23
  29.1 2.0 %collective-permute-start.11 = (bf16[160,1024]{1,0:T(8,128)(2,1)S(1)}, bf16[160,1024]{1,0:T(8,128)(2,1)S(1)}, u32[]{:S(2)}, u32[]{:S(2)}) collective-permute-start(bf16[160,1024]{1,0:T(8,128)(2,1)S(1)} %pad_maximum_fusion), channel_id=1, source_target_pairs={{0,4},{4,0},{8,12},{12,8},{16,20},{20,16},{24,28},{28,24},{32,36},... | collective-permute-start | bytes 983048 | tf_op jit(solution)/shard_map/ppermute | solution.py:23
  29.5 1.6 %collective-permute-start.10 = (bf16[96,1024]{1,0:T(8,128)(2,1)S(1)}, bf16[96,1024]{1,0:T(8,128)(2,1)S(1)}, u32[]{:S(2)}, u32[]{:S(2)}) collective-permute-start(bf16[96,1024]{1,0:T(8,128)(2,1)S(1)} %pad_maximum_fusion.1), channel_id=1, source_target_pairs={{0,4},{4,0},{8,12},{12,8},{16,20},{20,16},{24,28},{28,24},{32,36},... | collective-permute-start | bytes 589832 | tf_op jit(solution)/shard_map/ppermute | solution.py:23
  32.0 2.0 %collective-permute-start.12 = (bf16[256,1024]{1,0:T(8,128)(2,1)S(1)}, bf16[256,1024]{1,0:T(8,128)(2,1)S(1)}, u32[]{:S(2)}, u32[]{:S(2)}) collective-permute-start(bf16[256,1024]{1,0:T(8,128)(2,1)S(1)} %get-tuple-element.106), channel_id=1, source_target_pairs={{0,4},{4,0},{8,12},{12,8},{16,20},{20,16},{24,28},{28,24},{32,36},... | collective-permute-start | bytes 1572872 | tf_op jit(solution)/shard_map/ppermute | solution.py:23
  34.1 9.7 %collective-permute-start.14 = (bf16[80,1024]{1,0:T(8,128)(2,1)S(1)}, bf16[80,1024]{1,0:T(8,128)(2,1)S(1)}, u32[]{:S(2)}, u32[]{:S(2)}) collective-permute-start(bf16[80,1024]{1,0:T(8,128)(2,1)S(1)} %get-tuple-element.118), channel_id=1, source_target_pairs={{0,24},{4,28},{8,16},{12,20},{16,8},{20,12},{24,0},{28,4},{32,56},... | collective-permute-start | bytes 491528 | tf_op jit(solution)/shard_map/ppermute | solution.py:23
  35.9 5.6 %collective-permute-start.13 = (bf16[48,1024]{1,0:T(8,128)(2,1)S(1)}, bf16[48,1024]{1,0:T(8,128)(2,1)S(1)}, u32[]{:S(2)}, u32[]{:S(2)}) collective-permute-start(bf16[48,1024]{1,0:T(8,128)(2,1)S(1)} %get-tuple-element.117), channel_id=1, source_target_pairs={{0,8},{4,12},{8,0},{12,4},{16,24},{20,28},{24,16},{28,20},{32,40},... | collective-permute-start | bytes 294920 | tf_op jit(solution)/shard_map/ppermute | solution.py:23
  36.0 7.5 %collective-permute-start.15 = (bf16[48,1024]{1,0:T(8,128)(2,1)S(1)}, bf16[48,1024]{1,0:T(8,128)(2,1)S(1)}, u32[]{:S(2)}, u32[]{:S(2)}) collective-permute-start(bf16[48,1024]{1,0:T(8,128)(2,1)S(1)} %get-tuple-element.119), channel_id=1, source_target_pairs={{0,16},{4,20},{8,24},{12,28},{16,0},{20,4},{24,8},{28,12},{32,48},... | collective-permute-start | bytes 294920 | tf_op jit(solution)/shard_map/ppermute | solution.py:23
  43.7 7.5 %collective-permute-start.19 = (bf16[192,1024]{1,0:T(8,128)(2,1)S(1)}, bf16[192,1024]{1,0:T(8,128)(2,1)S(1)}, u32[]{:S(2)}, u32[]{:S(2)}) collective-permute-start(bf16[192,1024]{1,0:T(8,128)(2,1)S(1)} %get-tuple-element.150), channel_id=1, source_target_pairs={{0,4},{4,0},{8,12},{12,8},{16,20},{20,16},{24,28},{28,24},{32,36},... | collective-permute-start | bytes 1179656 | tf_op jit(solution)/shard_map/ppermute | solution.py:23
  43.8 4.6 %collective-permute-start.16 = (bf16[32,1024]{1,0:T(8,128)(2,1)S(1)}, bf16[32,1024]{1,0:T(8,128)(2,1)S(1)}, u32[]{:S(2)}, u32[]{:S(2)}) collective-permute-start(bf16[32,1024]{1,0:T(8,128)(2,1)S(1)} %get-tuple-element.130), channel_id=1, source_target_pairs={{0,32},{4,36},{8,40},{12,44},{16,48},{20,52},{24,56},{28,60},{32,0... | collective-permute-start | bytes 196616 | tf_op jit(solution)/shard_map/ppermute | solution.py:23
  48.4 4.9 %collective-permute-start.17 = (bf16[16,1024]{1,0:T(8,128)(2,1)S(1)}, bf16[16,1024]{1,0:T(8,128)(2,1)S(1)}, u32[]{:S(2)}, u32[]{:S(2)}) collective-permute-start(bf16[16,1024]{1,0:T(8,128)(2,1)S(1)} %add_convert_fusion), channel_id=1, source_target_pairs={{0,64},{4,68},{8,72},{12,76},{16,80},{20,84},{24,88},{28,92},{32,9... | collective-permute-start | bytes 98312 | tf_op jit(solution)/shard_map/ppermute | solution.py:23
  49.9 8.0 %collective-permute-start.21 = (bf16[32,1024]{1,0:T(8,128)(2,1)S(1)}, bf16[32,1024]{1,0:T(8,128)(2,1)S(1)}, u32[]{:S(2)}, u32[]{:S(2)}) collective-permute-start(bf16[32,1024]{1,0:T(8,128)(2,1)S(1)} %get-tuple-element.152), channel_id=1, source_target_pairs={{0,16},{4,20},{8,24},{12,28},{16,0},{20,4},{24,8},{28,12},{32,48},... | collective-permute-start | bytes 196616 | tf_op jit(solution)/shard_map/ppermute | solution.py:23
  51.2 6.7 %collective-permute-start.20 = (bf16[64,1024]{1,0:T(8,128)(2,1)S(1)}, bf16[64,1024]{1,0:T(8,128)(2,1)S(1)}, u32[]{:S(2)}, u32[]{:S(2)}) collective-permute-start(bf16[64,1024]{1,0:T(8,128)(2,1)S(1)} %chip_sum.3), channel_id=1, source_target_pairs={{0,8},{4,12},{8,0},{12,4},{16,24},{20,28},{24,16},{28,20},{32,40},... | collective-permute-start | bytes 393224 | tf_op jit(solution)/shard_map/ppermute | solution.py:23
  53.4 6.9 %collective-permute-start.18 = (bf16[16,1024]{1,0:T(8,128)(2,1)S(1)}, bf16[16,1024]{1,0:T(8,128)(2,1)S(1)}, u32[]{:S(2)}, u32[]{:S(2)}) collective-permute-start(bf16[16,1024]{1,0:T(8,128)(2,1)S(1)} %broadcast_select_fusion.1), channel_id=1, source_target_pairs={{0,224},{4,228},{8,232},{12,236},{16,240},{20,244},{24,248},{28,25... | collective-permute-start | bytes 98312 | tf_op jit(solution)/shard_map/ppermute | solution.py:23

commit v5 on v4

--- a/solution.py
+++ b/solution.py
@@ -245,7 +245,7 @@
     key_ref, value_ref, weight_ref, dscore_ref, final_ref, grad_ref,
     key_tmp, value_tmp, score_tmp, dprob_tmp,
 ):
-    tiles = ((early, 0), (early, 48), (late, 0), (late, 80))
+    tiles = ((early, 0), (late, 0), (late, 48), (late, 128))
     place_far(tiles, key_ref, value_ref, key_tmp, value_tmp)
 
     def scores_of(columns):
@@ -528,9 +528,9 @@
         queries, keys, values, cotangent, c1, c2, core
     )
     far2 = jnp.concatenate([far2, c3a])
-    early = swap(jnp.concatenate([own, near]), 1)
+    early = swap(own, 1)
     far3, stats = together(far3, stats)
-    late = swap(jnp.concatenate([far2, far3]), 1)
+    late = swap(jnp.concatenate([near, far2, far3]), 1)
     mine_key, mine_value, mine_exponent, mine_dprob, joint = mine_scores(
         queries, cotangent, stats, own, near, far2, far3
     )

time: 61.3 us -> 61.7 us (level)
  waiting for transfers between devices: 22.6 us -> 24.1 us
  starting transfers between devices: 29.9 us -> 28.8 us
    ppermute x22, waiting for transfers between devices: 22.6 us -> 24.1 us  [swap(): return lax.ppermute(block, 'ctx', [(i, i ^ mask) for i in range(count)])]
    ppermute x22, starting transfers between devices: 29.9 us -> 28.8 us  [swap(): return lax.ppermute(block, 'ctx', [(i, i ^ mask) for i in range(count)])]
  transfers between devices with their start and end apart: 22 -> 22, of which waited for: 12 -> 12; matrix products, arithmetic and copies ran while one was open for 1% -> 0% of each run, Pallas kernels for 7% -> 7%
where the time goes in v5:
time: 61.7 us; the launch traced here: 61.6 us
  starting transfers between devices  28.8 us (47%)
  waiting for transfers between devices  24.1 us (39%)
  Pallas kernels  7.53 us (12%)
  between operations  0.8 us (1%)
    ppermute x22, starting transfers between devices, swap(): return lax.ppermute(block, 'ctx', [(i, i ^ mask) for i in range(count)])  28.8 us
    ppermute x22, waiting for transfers between devices, swap(): return lax.ppermute(block, 'ctx', [(i, i ^ mask) for i in range(count)])  24.1 us
    pallas_call x1, Pallas kernels, outputs(): pl.pallas_call(output_kernel, out_shape=(shape((ROWS, D), BF16), shape((R...  1.68 us
    pallas_call x1, Pallas kernels, coarsen(): pl.pallas_call(coarsen_kernel, out_shape=tuple((jax.ShapeDtypeStruct((cou...  1.47 us
  transfers between devices with their start and end apart: 22, of which 12 were waited for; matrix products, arithmetic and copies ran while one was open for 0% of the time, Pallas kernels for 7%

profile of v5, /device:TPU:36, one launch (start us, length us, event | category | flops | bytes accessed | tf_op | source)
XLA Modules:
  0.0 61.6 jit_solution(11968727207490770315)
XLA Ops:
  0.6 1.5 %coarsen.1 = (bf16[128,1024]{1,0:T(8,128)(2,1)S(1)}, bf16[64,1024]{1,0:T(8,128)(2,1)S(1)}, bf16[32,1024]{1,0:T(8,128)(2,1)S(1)}, bf16[16,1024]{1,0:T(8,128)(2,1)...) custom-call(bf16[128,1024]{1,0:T(8,128)(2,1)} %k_hbm.1, ...), custom_call_target="tpu_custom_call" | custom-call | tf_op jit(solution)/shard_map/coarsen/pallas_call | solution.py:76
  2.1 5.9 %collective-permute-start = (bf16[16,1024]{1,0:T(8,128)(2,1)S(1)}, bf16[16,1024]{1,0:T(8,128)(2,1)S(1)}, u32[]{:S(2)}, u32[]{:S(2)}) collective-permute-start(bf16[16,1024]{1,0:T(8,128)(2,1)S(1)} %get-tuple-element.84), channel_id=1, source_target_pairs={{0,224},{4,228},{8,232},{12,236},{16,240},{20,244},{24,248},{28,25... | collective-permute-start | bytes 98312 | tf_op jit(solution)/shard_map/ppermute | solution.py:23
  8.0 3.2 %collective-permute-start.3 = (bf16[32,1024]{1,0:T(8,128)(2,1)S(1)}, bf16[32,1024]{1,0:T(8,128)(2,1)S(1)}, u32[]{:S(2)}, u32[]{:S(2)}) collective-permute-start(bf16[32,1024]{1,0:T(8,128)(2,1)S(1)} %get-tuple-element.88), channel_id=1, source_target_pairs={{0,16},{4,20},{8,24},{12,28},{16,0},{20,4},{24,8},{28,12},{32,48},... | collective-permute-start | bytes 196616 | tf_op jit(solution)/shard_map/ppermute | solution.py:23
  12.6 4.3 %collective-permute-done.1 = bf16[16,1024]{1,0:T(8,128)(2,1)S(1)} collective-permute-done((bf16[16,1024]{1,0:T(8,128)(2,1)S(1)}, bf16[16,1024]{1,0:T(8,128)(2,1)S(1)}, u32[]{:S(2)}, u32[]{:S(2)}) %collective-permute-start.1) | collective-permute-done | bytes 32800 | tf_op jit(solution)/shard_map/ppermute | solution.py:23
  17.2 4.1 %collective-permute-done.4 = bf16[32,1024]{1,0:T(8,128)(2,1)S(1)} collective-permute-done((bf16[32,1024]{1,0:T(8,128)(2,1)S(1)}, bf16[32,1024]{1,0:T(8,128)(2,1)S(1)}, u32[]{:S(2)}, u32[]{:S(2)}) %collective-permute-start.4) | collective-permute-done | bytes 65568 | tf_op jit(solution)/shard_map/ppermute | solution.py:23
  21.4 1.1 %collective-permute-start.7 = (bf16[80,1024]{1,0:T(8,128)(2,1)S(1)}, bf16[80,1024]{1,0:T(8,128)(2,1)S(1)}, u32[]{:S(2)}, u32[]{:S(2)}) collective-permute-start(bf16[80,1024]{1,0:T(8,128)(2,1)S(1)} %pad_maximum_fusion.1), channel_id=1, source_target_pairs={{0,24},{4,28},{8,16},{12,20},{16,8},{20,12},{24,0},{28,4},{32,56},... | collective-permute-start | bytes 491528 | tf_op jit(solution)/shard_map/ppermute | solution.py:23
  22.5 2.4 %collective-permute-start.9 = (bf16[48,1024]{1,0:T(8,128)(2,1)S(1)}, bf16[48,1024]{1,0:T(8,128)(2,1)S(1)}, u32[]{:S(2)}, u32[]{:S(2)}) collective-permute-start(bf16[48,1024]{1,0:T(8,128)(2,1)S(1)} %pad_maximum_fusion.3.own), channel_id=1, source_target_pairs={{0,16},{4,20},{8,24},{12,28},{16,0},{20,4},{24,8},{28,12},{32,48},... | collective-permute-start | bytes 294920 | tf_op jit(solution)/shard_map/ppermute | solution.py:23
  26.2 2.8 %collective-permute-done.7.far3 = bf16[80,1024]{1,0:T(8,128)(2,1)S(1)} collective-permute-done((bf16[80,1024]{1,0:T(8,128)(2,1)S(1)}, bf16[80,1024]{1,0:T(8,128)(2,1)S(1)}, u32[]{:S(2)}, u32[]{:S(2)}) %collective-permute-start.7) | collective-permute-done | bytes 163872 | tf_op jit(solution)/shard_map/ppermute | solution.py:23
  30.7 0.8 %collective-permute-done.10.early = bf16[48,1024]{1,0:T(8,128)(2,1)S(1)} collective-permute-done((bf16[48,1024]{1,0:T(8,128)(2,1)S(1)}, bf16[48,1024]{1,0:T(8,128)(2,1)S(1)}, u32[]{:S(2)}, u32[]{:S(2)}) %collective-permute-start.10) | collective-permute-done | bytes 98336 | tf_op jit(solution)/shard_map/ppermute | solution.py:23
  31.5 0.9 %other_attend.1 = (bf16[128,1024]{1,0:T(8,128)(2,1)S(1)}, bf16[128,1024]{1,0:T(8,128)(2,1)S(1)}, bf16[128,1024]{1,0:T(8,128)(2,1)S(1)}, bf16[128,1024]{1,0:T(8,1...) custom-call(bf16[128,1024]{1,0:T(8,128)(2,1)S(1)} %get-tuple-element.82.q_ref, ...), custom_call_target="tpu_custom_call" | custom-call | flops 67108864 | bytes 2097152 | tf_op jit(solution)/shard_map/other_attend/pallas_call | solution.py:283
  33.0 1.4 %collective-permute-done.12.got_ref = bf16[256,1024]{1,0:T(8,128)(2,1)S(1)} collective-permute-done((bf16[256,1024]{1,0:T(8,128)(2,1)S(1)}, bf16[256,1024]{1,0:T(8,128)(2,1)S(1)}, u32[]{:S(2)}, u32[]{:S(2)}) %collective-permute-start.12) | collective-permute-done | bytes 524320 | tf_op jit(solution)/shard_map/ppermute | solution.py:23
  34.5 1.4 %collective-permute-start.14 = (bf16[80,1024]{1,0:T(8,128)(2,1)S(1)}, bf16[80,1024]{1,0:T(8,128)(2,1)S(1)}, u32[]{:S(2)}, u32[]{:S(2)}) collective-permute-start(bf16[80,1024]{1,0:T(8,128)(2,1)S(1)} %get-tuple-element.118), channel_id=1, source_target_pairs={{0,24},{4,28},{8,16},{12,20},{16,8},{20,12},{24,0},{28,4},{32,56},... | collective-permute-start | bytes 491528 | tf_op jit(solution)/shard_map/ppermute | solution.py:23
  36.1 3.2 %collective-permute-start.15 = (bf16[48,1024]{1,0:T(8,128)(2,1)S(1)}, bf16[48,1024]{1,0:T(8,128)(2,1)S(1)}, u32[]{:S(2)}, u32[]{:S(2)}) collective-permute-start(bf16[48,1024]{1,0:T(8,128)(2,1)S(1)} %get-tuple-element.119), channel_id=1, source_target_pairs={{0,16},{4,20},{8,24},{12,28},{16,0},{20,4},{24,8},{28,12},{32,48},... | collective-permute-start | bytes 294920 | tf_op jit(solution)/shard_map/ppermute | solution.py:23
  39.8 1.7 %collective-permute-done.13.near_ref = bf16[48,1024]{1,0:T(8,128)(2,1)S(1)} collective-permute-done((bf16[48,1024]{1,0:T(8,128)(2,1)S(1)}, bf16[48,1024]{1,0:T(8,128)(2,1)S(1)}, u32[]{:S(2)}, u32[]{:S(2)}) %collective-permute-start.13) | collective-permute-done | bytes 98336 | tf_op jit(solution)/shard_map/ppermute | solution.py:23
  41.5 2.5 %collective-permute-done.15.far2_ref = bf16[48,1024]{1,0:T(8,128)(2,1)S(1)} collective-permute-done((bf16[48,1024]{1,0:T(8,128)(2,1)S(1)}, bf16[48,1024]{1,0:T(8,128)(2,1)S(1)}, u32[]{:S(2)}, u32[]{:S(2)}) %collective-permute-start.15) | collective-permute-done | bytes 98336 | tf_op jit(solution)/shard_map/ppermute | solution.py:23
  44.9 1.7 %outputs.1 = (bf16[128,1024]{1,0:T(8,128)(2,1)}, bf16[128,1024]{1,0:T(8,128)(2,1)}) custom-call(bf16[256,1024]{1,0:T(8,128)(2,1)S(1)} %get-tuple-element.131.refs_0_, bf16[256,1024]{1,0:T(8,128)(2,1)S(1)} %get-tuple-element.132.refs_1_, bf16[256,1024]{1,0:T(8,128)(2,1)S(1)} %get-tuple-element.133.refs_2_, bf16[256,1024]{1,0:T(8,128)(2,1)S(1)} %get-tuple-element.134.refs_3_, ...), custom_call_target="tpu_custom_call" | custom-call | flops 268435456 | bytes 4194304 | tf_op jit(solution)/shard_map/outputs/pallas_call | solution.py:385
  46.6 2.2 %collective-permute-done.16 = bf16[32,1024]{1,0:T(8,128)(2,1)S(1)} collective-permute-done((bf16[32,1024]{1,0:T(8,128)(2,1)S(1)}, bf16[32,1024]{1,0:T(8,128)(2,1)S(1)}, u32[]{:S(2)}, u32[]{:S(2)}) %collective-permute-start.16) | collective-permute-done | bytes 65568 | tf_op jit(solution)/shard_map/ppermute | solution.py:23
  48.8 1.1 %collective-permute-start.17 = (bf16[16,1024]{1,0:T(8,128)(2,1)S(1)}, bf16[16,1024]{1,0:T(8,128)(2,1)S(1)}, u32[]{:S(2)}, u32[]{:S(2)}) collective-permute-start(bf16[16,1024]{1,0:T(8,128)(2,1)S(1)} %add_convert_fusion), channel_id=1, source_target_pairs={{0,64},{4,68},{8,72},{12,76},{16,80},{20,84},{24,88},{28,92},{32,9... | collective-permute-start | bytes 98312 | tf_op jit(solution)/shard_map/ppermute | solution.py:23
  49.9 1.3 %collective-permute-start.21 = (bf16[32,1024]{1,0:T(8,128)(2,1)S(1)}, bf16[32,1024]{1,0:T(8,128)(2,1)S(1)}, u32[]{:S(2)}, u32[]{:S(2)}) collective-permute-start(bf16[32,1024]{1,0:T(8,128)(2,1)S(1)} %get-tuple-element.152), channel_id=1, source_target_pairs={{0,16},{4,20},{8,24},{12,28},{16,0},{20,4},{24,8},{28,12},{32,48},... | collective-permute-start | bytes 196616 | tf_op jit(solution)/shard_map/ppermute | solution.py:23
  51.2 1.2 %collective-permute-start.20 = (bf16[64,1024]{1,0:T(8,128)(2,1)S(1)}, bf16[64,1024]{1,0:T(8,128)(2,1)S(1)}, u32[]{:S(2)}, u32[]{:S(2)}) collective-permute-start(bf16[64,1024]{1,0:T(8,128)(2,1)S(1)} %chip_sum.3), channel_id=1, source_target_pairs={{0,8},{4,12},{8,0},{12,4},{16,24},{20,28},{24,16},{28,20},{32,40},... | collective-permute-start | bytes 393224 | tf_op jit(solution)/shard_map/ppermute | solution.py:23
  52.4 1.3 %collective-permute-done.17.z2_ref = bf16[16,1024]{1,0:T(8,128)(2,1)S(1)} collective-permute-done((bf16[16,1024]{1,0:T(8,128)(2,1)S(1)}, bf16[16,1024]{1,0:T(8,128)(2,1)S(1)}, u32[]{:S(2)}, u32[]{:S(2)}) %collective-permute-start.17) | collective-permute-done | bytes 32800 | tf_op jit(solution)/shard_map/ppermute | solution.py:23
  53.8 4.2 %collective-permute-start.18 = (bf16[16,1024]{1,0:T(8,128)(2,1)S(1)}, bf16[16,1024]{1,0:T(8,128)(2,1)S(1)}, u32[]{:S(2)}, u32[]{:S(2)}) collective-permute-start(bf16[16,1024]{1,0:T(8,128)(2,1)S(1)} %broadcast_select_fusion.1), channel_id=1, source_target_pairs={{0,224},{4,228},{8,232},{12,236},{16,240},{20,244},{24,248},{28,25... | collective-permute-start | bytes 98312 | tf_op jit(solution)/shard_map/ppermute | solution.py:23
  58.4 2.4 %collective-permute-done.18.z7_ref = bf16[16,1024]{1,0:T(8,128)(2,1)S(1)} collective-permute-done((bf16[16,1024]{1,0:T(8,128)(2,1)S(1)}, bf16[16,1024]{1,0:T(8,128)(2,1)S(1)}, u32[]{:S(2)}, u32[]{:S(2)}) %collective-permute-start.18) | collective-permute-done | bytes 32800 | tf_op jit(solution)/shard_map/ppermute | solution.py:23
  60.7 0.8 %finish.1 = (bf16[128,1024]{1,0:T(8,128)(2,1)}, bf16[128,1024]{1,0:T(8,128)(2,1)}) custom-call(f32[128,1024]{1,0:T(8,128)S(1)} %get-tuple-element.155.part_k_ref, f32[128,1024]{1,0:T(8,128)S(1)} %get-tuple-element.156.part_v_ref, bf16[16,1024]{1,0:T(8,128)(2,1)S(1)} %collective-permute-done.18.z7_ref), custom_call_target="tpu_custom_call" | custom-call | tf_op jit(solution)/shard_map/finish/pallas_call | solution.py:493
  (45 shorter events, 7.4 us)
Async XLA Ops:
  2.1 9.8 %collective-permute-start = (bf16[16,1024]{1,0:T(8,128)(2,1)S(1)}, bf16[16,1024]{1,0:T(8,128)(2,1)S(1)}, u32[]{:S(2)}, u32[]{:S(2)}) collective-permute-start(bf16[16,1024]{1,0:T(8,128)(2,1)S(1)} %get-tuple-element.84), channel_id=1, source_target_pairs={{0,224},{4,228},{8,232},{12,236},{16,240},{20,244},{24,248},{28,25... | collective-permute-start | bytes 98312 | tf_op jit(solution)/shard_map/ppermute | solution.py:23
  8.0 8.9 %collective-permute-start.3 = (bf16[32,1024]{1,0:T(8,128)(2,1)S(1)}, bf16[32,1024]{1,0:T(8,128)(2,1)S(1)}, u32[]{:S(2)}, u32[]{:S(2)}) collective-permute-start(bf16[32,1024]{1,0:T(8,128)(2,1)S(1)} %get-tuple-element.88), channel_id=1, source_target_pairs={{0,16},{4,20},{8,24},{12,28},{16,0},{20,4},{24,8},{28,12},{32,48},... | collective-permute-start | bytes 196616 | tf_op jit(solution)/shard_map/ppermute | solution.py:23
  11.2 5.7 %collective-permute-start.2 = (bf16[64,1024]{1,0:T(8,128)(2,1)S(1)}, bf16[64,1024]{1,0:T(8,128)(2,1)S(1)}, u32[]{:S(2)}, u32[]{:S(2)}) collective-permute-start(bf16[64,1024]{1,0:T(8,128)(2,1)S(1)} %get-tuple-element.87), channel_id=1, source_target_pairs={{0,8},{4,12},{8,0},{12,4},{16,24},{20,28},{24,16},{28,20},{32,40},... | collective-permute-start | bytes 393224 | tf_op jit(solution)/shard_map/ppermute | solution.py:23
  11.9 9.4 %collective-permute-start.5 = (bf16[128,1024]{1,0:T(8,128)(2,1)S(1)}, bf16[128,1024]{1,0:T(8,128)(2,1)S(1)}, u32[]{:S(2)}, u32[]{:S(2)}) collective-permute-start(bf16[128,1024]{1,0:T(8,128)(2,1)S(1)} %get-tuple-element.90), channel_id=1, source_target_pairs={{0,4},{4,0},{8,12},{12,8},{16,20},{20,16},{24,28},{28,24},{32,36},... | collective-permute-start | bytes 786440 | tf_op jit(solution)/shard_map/ppermute | solution.py:23
  12.0 4.8 %collective-permute-start.1 = (bf16[16,1024]{1,0:T(8,128)(2,1)S(1)}, bf16[16,1024]{1,0:T(8,128)(2,1)S(1)}, u32[]{:S(2)}, u32[]{:S(2)}) collective-permute-start(bf16[16,1024]{1,0:T(8,128)(2,1)S(1)} %broadcast_select_fusion), channel_id=1, source_target_pairs={{0,64},{4,68},{8,72},{12,76},{16,80},{20,84},{24,88},{28,92},{32,9... | collective-permute-start | bytes 98312 | tf_op jit(solution)/shard_map/ppermute | solution.py:23
  17.0 4.4 %collective-permute-start.4 = (bf16[32,1024]{1,0:T(8,128)(2,1)S(1)}, bf16[32,1024]{1,0:T(8,128)(2,1)S(1)}, u32[]{:S(2)}, u32[]{:S(2)}) collective-permute-start(bf16[32,1024]{1,0:T(8,128)(2,1)S(1)} %pad_maximum_fusion.4), channel_id=1, source_target_pairs={{0,32},{4,36},{8,40},{12,44},{16,48},{20,52},{24,56},{28,60},{32,0... | collective-permute-start | bytes 196616 | tf_op jit(solution)/shard_map/ppermute | solution.py:23
  17.2 4.2 %collective-permute-start.6 = (bf16[64,1024]{1,0:T(8,128)(2,1)S(1)}, bf16[64,1024]{1,0:T(8,128)(2,1)S(1)}, u32[]{:S(2)}, u32[]{:S(2)}) collective-permute-start(bf16[64,1024]{1,0:T(8,128)(2,1)S(1)} %collective-permute-done.2.rest_1_), channel_id=1, source_target_pairs={{0,4},{4,0},{8,12},{12,8},{16,20},{20,16},{24,28},{28,24},{32,36},... | collective-permute-start | bytes 393224 | tf_op jit(solution)/shard_map/ppermute | solution.py:23
  21.4 7.7 %collective-permute-start.7 = (bf16[80,1024]{1,0:T(8,128)(2,1)S(1)}, bf16[80,1024]{1,0:T(8,128)(2,1)S(1)}, u32[]{:S(2)}, u32[]{:S(2)}) collective-permute-start(bf16[80,1024]{1,0:T(8,128)(2,1)S(1)} %pad_maximum_fusion.1), channel_id=1, source_target_pairs={{0,24},{4,28},{8,16},{12,20},{16,8},{20,12},{24,0},{28,4},{32,56},... | collective-permute-start | bytes 491528 | tf_op jit(solution)/shard_map/ppermute | solution.py:23
  22.5 6.6 %collective-permute-start.9 = (bf16[48,1024]{1,0:T(8,128)(2,1)S(1)}, bf16[48,1024]{1,0:T(8,128)(2,1)S(1)}, u32[]{:S(2)}, u32[]{:S(2)}) collective-permute-start(bf16[48,1024]{1,0:T(8,128)(2,1)S(1)} %pad_maximum_fusion.3.own), channel_id=1, source_target_pairs={{0,16},{4,20},{8,24},{12,28},{16,0},{20,4},{24,8},{28,12},{32,48},... | collective-permute-start | bytes 294920 | tf_op jit(solution)/shard_map/ppermute | solution.py:23
  24.9 4.6 %collective-permute-start.8 = (bf16[48,1024]{1,0:T(8,128)(2,1)S(1)}, bf16[48,1024]{1,0:T(8,128)(2,1)S(1)}, u32[]{:S(2)}, u32[]{:S(2)}) collective-permute-start(bf16[48,1024]{1,0:T(8,128)(2,1)S(1)} %pad_maximum_fusion.3.own), channel_id=1, source_target_pairs={{0,8},{4,12},{8,0},{12,4},{16,24},{20,28},{24,16},{28,20},{32,40},... | collective-permute-start | bytes 294920 | tf_op jit(solution)/shard_map/ppermute | solution.py:23
  29.5 2.0 %collective-permute-start.11 = (bf16[208,1024]{1,0:T(8,128)(2,1)S(1)}, bf16[208,1024]{1,0:T(8,128)(2,1)S(1)}, u32[]{:S(2)}, u32[]{:S(2)}) collective-permute-start(bf16[208,1024]{1,0:T(8,128)(2,1)S(1)} %pad_maximum_fusion), channel_id=1, source_target_pairs={{0,4},{4,0},{8,12},{12,8},{16,20},{20,16},{24,28},{28,24},{32,36},... | collective-permute-start | bytes 1277960 | tf_op jit(solution)/shard_map/ppermute | solution.py:23
  29.6 1.9 %collective-permute-start.10 = (bf16[48,1024]{1,0:T(8,128)(2,1)S(1)}, bf16[48,1024]{1,0:T(8,128)(2,1)S(1)}, u32[]{:S(2)}, u32[]{:S(2)}) collective-permute-start(bf16[48,1024]{1,0:T(8,128)(2,1)S(1)} %pad_maximum_fusion.3.own), channel_id=1, source_target_pairs={{0,4},{4,0},{8,12},{12,8},{16,20},{20,16},{24,28},{28,24},{32,36},... | collective-permute-start | bytes 294920 | tf_op jit(solution)/shard_map/ppermute | solution.py:23
  32.4 2.0 %collective-permute-start.12 = (bf16[256,1024]{1,0:T(8,128)(2,1)S(1)}, bf16[256,1024]{1,0:T(8,128)(2,1)S(1)}, u32[]{:S(2)}, u32[]{:S(2)}) collective-permute-start(bf16[256,1024]{1,0:T(8,128)(2,1)S(1)} %get-tuple-element.106), channel_id=1, source_target_pairs={{0,4},{4,0},{8,12},{12,8},{16,20},{20,16},{24,28},{28,24},{32,36},... | collective-permute-start | bytes 1572872 | tf_op jit(solution)/shard_map/ppermute | solution.py:23
  34.5 9.6 %collective-permute-start.14 = (bf16[80,1024]{1,0:T(8,128)(2,1)S(1)}, bf16[80,1024]{1,0:T(8,128)(2,1)S(1)}, u32[]{:S(2)}, u32[]{:S(2)}) collective-permute-start(bf16[80,1024]{1,0:T(8,128)(2,1)S(1)} %get-tuple-element.118), channel_id=1, source_target_pairs={{0,24},{4,28},{8,16},{12,20},{16,8},{20,12},{24,0},{28,4},{32,56},... | collective-permute-start | bytes 491528 | tf_op jit(solution)/shard_map/ppermute | solution.py:23
  35.9 5.6 %collective-permute-start.13 = (bf16[48,1024]{1,0:T(8,128)(2,1)S(1)}, bf16[48,1024]{1,0:T(8,128)(2,1)S(1)}, u32[]{:S(2)}, u32[]{:S(2)}) collective-permute-start(bf16[48,1024]{1,0:T(8,128)(2,1)S(1)} %get-tuple-element.117), channel_id=1, source_target_pairs={{0,8},{4,12},{8,0},{12,4},{16,24},{20,28},{24,16},{28,20},{32,40},... | collective-permute-start | bytes 294920 | tf_op jit(solution)/shard_map/ppermute | solution.py:23
  36.1 7.9 %collective-permute-start.15 = (bf16[48,1024]{1,0:T(8,128)(2,1)S(1)}, bf16[48,1024]{1,0:T(8,128)(2,1)S(1)}, u32[]{:S(2)}, u32[]{:S(2)}) collective-permute-start(bf16[48,1024]{1,0:T(8,128)(2,1)S(1)} %get-tuple-element.119), channel_id=1, source_target_pairs={{0,16},{4,20},{8,24},{12,28},{16,0},{20,4},{24,8},{28,12},{32,48},... | collective-permute-start | bytes 294920 | tf_op jit(solution)/shard_map/ppermute | solution.py:23
  44.1 7.1 %collective-permute-start.19 = (bf16[192,1024]{1,0:T(8,128)(2,1)S(1)}, bf16[192,1024]{1,0:T(8,128)(2,1)S(1)}, u32[]{:S(2)}, u32[]{:S(2)}) collective-permute-start(bf16[192,1024]{1,0:T(8,128)(2,1)S(1)} %get-tuple-element.150), channel_id=1, source_target_pairs={{0,4},{4,0},{8,12},{12,8},{16,20},{20,16},{24,28},{28,24},{32,36},... | collective-permute-start | bytes 1179656 | tf_op jit(solution)/shard_map/ppermute | solution.py:23
  44.2 4.6 %collective-permute-start.16 = (bf16[32,1024]{1,0:T(8,128)(2,1)S(1)}, bf16[32,1024]{1,0:T(8,128)(2,1)S(1)}, u32[]{:S(2)}, u32[]{:S(2)}) collective-permute-start(bf16[32,1024]{1,0:T(8,128)(2,1)S(1)} %get-tuple-element.130), channel_id=1, source_target_pairs={{0,32},{4,36},{8,40},{12,44},{16,48},{20,52},{24,56},{28,60},{32,0... | collective-permute-start | bytes 196616 | tf_op jit(solution)/shard_map/ppermute | solution.py:23
  48.8 4.9 %collective-permute-start.17 = (bf16[16,1024]{1,0:T(8,128)(2,1)S(1)}, bf16[16,1024]{1,0:T(8,128)(2,1)S(1)}, u32[]{:S(2)}, u32[]{:S(2)}) collective-permute-start(bf16[16,1024]{1,0:T(8,128)(2,1)S(1)} %add_convert_fusion), channel_id=1, source_target_pairs={{0,64},{4,68},{8,72},{12,76},{16,80},{20,84},{24,88},{28,92},{32,9... | collective-permute-start | bytes 98312 | tf_op jit(solution)/shard_map/ppermute | solution.py:23
  49.9 8.0 %collective-permute-start.21 = (bf16[32,1024]{1,0:T(8,128)(2,1)S(1)}, bf16[32,1024]{1,0:T(8,128)(2,1)S(1)}, u32[]{:S(2)}, u32[]{:S(2)}) collective-permute-start(bf16[32,1024]{1,0:T(8,128)(2,1)S(1)} %get-tuple-element.152), channel_id=1, source_target_pairs={{0,16},{4,20},{8,24},{12,28},{16,0},{20,4},{24,8},{28,12},{32,48},... | collective-permute-start | bytes 196616 | tf_op jit(solution)/shard_map/ppermute | solution.py:23
  51.2 6.7 %collective-permute-start.20 = (bf16[64,1024]{1,0:T(8,128)(2,1)S(1)}, bf16[64,1024]{1,0:T(8,128)(2,1)S(1)}, u32[]{:S(2)}, u32[]{:S(2)}) collective-permute-start(bf16[64,1024]{1,0:T(8,128)(2,1)S(1)} %chip_sum.3), channel_id=1, source_target_pairs={{0,8},{4,12},{8,0},{12,4},{16,24},{20,28},{24,16},{28,20},{32,40},... | collective-permute-start | bytes 393224 | tf_op jit(solution)/shard_map/ppermute | solution.py:23
  53.8 6.9 %collective-permute-start.18 = (bf16[16,1024]{1,0:T(8,128)(2,1)S(1)}, bf16[16,1024]{1,0:T(8,128)(2,1)S(1)}, u32[]{:S(2)}, u32[]{:S(2)}) collective-permute-start(bf16[16,1024]{1,0:T(8,128)(2,1)S(1)} %broadcast_select_fusion.1), channel_id=1, source_target_pairs={{0,224},{4,228},{8,232},{12,236},{16,240},{20,244},{24,248},{28,25... | collective-permute-start | bytes 98312 | tf_op jit(solution)/shard_map/ppermute | solution.py:23
